TPU v7x, 32 devices: a whole 2x2x4 slice. The times are simulated.
32 devices in a mesh: wave: 8 (over z, y), lev: 4 (over x, core).
Axes of the slice: x: 2, y: 2, z: 4, core: 2. Of those that a mesh axis runs over, the one named last changes fastest.
Arguments:
- control: bfloat16 [32, 1281, 512], P(('wave', 'lev')), may hold values from -6 to 6
- covariance: float32 [1280, 128, 128], P(('wave', 'lev')), may hold values from -0.5 to 0.5
- legendre: bfloat16 [32, 1281, 2560], P(('wave', 'lev')), may hold values from -0.25 to 0.25
- pair_order: int32 [32], P(('wave', 'lev')), may hold values from 0 to 639, as said below
- band_rows: int32 [8], replicated, may hold values from 1 to 400, 2560 in all
Outputs:
- fourier: bfloat16 [64, 3200, 512], P(None, 'wave', 'lev')
Inputs may be any that keep to these rules, and one draw needn't show every extreme that they name: `pair_order`: the pair holds zonal wavenumbers m and 1279 - m; values may repeat. `band_rows`: band sizes sum to 2560; bands follow one another from latitude 0.
All inputs are finite; a program needn't handle non-finite values.
Results may differ from a plain program's by a relative error of at most 0.0049.
Values may be sent and summed in bfloat16 or wider, within the bound.
No kernel may reach another device: no remote copies, remote signals or barrier semaphores. Data moves between devices by JAX's collectives and lax.ppermute only.
A program may use at most 128 MiB of HBM per device.

v0:
```python
import jax
import jax.numpy as jnp
from jax import lax
from jax.sharding import PartitionSpec as P


def by_degree(coeffs, lowest, degrees):
    pair_count = coeffs.shape[0]
    columns = coeffs.shape[2]
    padding = jnp.zeros((pair_count, degrees, columns), coeffs.dtype)
    padded = jnp.concatenate([padding, coeffs], axis=1)
    leading = jnp.stack(
        [lax.dynamic_slice_in_dim(padded[0], degrees - lowest[0], degrees, 0)], axis=0
    )
    degree_index = jnp.arange(degrees, dtype=jnp.int32)
    active = degree_index[None, :] >= (degrees - 1 - lowest)[:, None]
    tail_part = coeffs[:, 1:, :]
    second = jnp.where(active[:, :, None], tail_part, jnp.zeros_like(tail_part))
    return jnp.stack([leading, second], axis=1)


def by_slot(spectra, lowest, degrees):
    pair_count = spectra.shape[0]
    columns = spectra.shape[3]
    slot_count = degrees + 1
    padded = jnp.concatenate(
        [spectra[:, 0], jnp.zeros((pair_count, slot_count, columns), spectra.dtype)], axis=1
    )
    head_part = jnp.stack([lax.dynamic_slice_in_dim(padded[0], lowest[0], slot_count, 0)], axis=0)
    tail_part = jnp.concatenate(
        [jnp.zeros((pair_count, 1, columns), spectra.dtype), spectra[:, 1]], axis=1
    )
    slot_index = jnp.arange(slot_count, dtype=jnp.int32)
    leading = (slot_index[None, :] < (degrees - lowest)[:, None])[:, :, None]
    upper_seg = jnp.where(leading, head_part, jnp.zeros_like(head_part))
    lower_seg = jnp.where(leading, jnp.zeros_like(tail_part), tail_part)
    return jnp.stack([upper_seg, lower_seg], axis=1)


def per_device(control, covariance, legendre, pair_order, band_rows):
    pair_count, slot_count, columns = control.shape
    degrees = slot_count - 1
    levels = columns // 4
    latitudes = legendre.shape[2]
    wave_count = lax.axis_size("wave")
    level_count = lax.axis_size("lev")
    band_depth = 5 * latitudes // (4 * wave_count)
    level_cols = columns // level_count
    spectra = by_degree(control, pair_order, degrees)
    received = lax.all_to_all(spectra, ("wave", "lev"), split_axis=2, concat_axis=0, tiled=True)
    shape_in = received.shape
    split_cols = received.reshape(shape_in[0], shape_in[1], shape_in[2], 4, levels)
    product = jnp.einsum(
        "nij,pgncj->pgnci",
        covariance,
        split_cols.astype(jnp.float32),
        precision=lax.Precision.HIGHEST,
    )
    product = product.astype(jnp.bfloat16).reshape(shape_in)
    filtered = lax.all_to_all(product, ("wave", "lev"), split_axis=0, concat_axis=2, tiled=True)
    halves = by_slot(filtered, pair_order, degrees)
    gridded = jnp.einsum(
        "psl,pgsk->pglk", legendre, halves, preferred_element_type=jnp.float32
    ).astype(jnp.bfloat16)
    starts = jnp.cumsum(band_rows) - band_rows
    padded_grid = jnp.concatenate(
        [gridded, jnp.zeros((pair_count, 2, band_depth, columns), gridded.dtype)], axis=2
    )
    offsets = jnp.arange(band_depth, dtype=jnp.int32)

    def put_band(wave_pos, collected):
        piece = lax.dynamic_slice_in_dim(padded_grid, starts[wave_pos], band_depth, 2)
        keep = offsets < band_rows[wave_pos]
        piece = jnp.where(keep[None, None, :, None], piece, jnp.zeros_like(piece))
        return lax.dynamic_update_slice_in_dim(
            collected, piece, (wave_pos * band_depth).astype(jnp.int32), 2
        )

    picked = lax.fori_loop(
        0,
        wave_count,
        put_band,
        jnp.zeros((pair_count, 2, wave_count * band_depth, columns), gridded.dtype),
    )
    picked = picked.reshape(pair_count * 2, wave_count * band_depth, columns)
    outgoing = picked.reshape(pair_count * 2, wave_count, band_depth, level_count, level_cols)
    outgoing = outgoing.transpose(1, 3, 0, 2, 4).reshape(
        wave_count * level_count * pair_count * 2, band_depth, level_cols
    )
    fourier = lax.all_to_all(outgoing, ("wave", "lev"), split_axis=0, concat_axis=0, tiled=True)
    return fourier


def solution(mesh):
    return jax.shard_map(
        per_device,
        mesh=mesh,
        in_specs=(
            P(("wave", "lev"), None, None),
            P(("wave", "lev"), None, None),
            P(("wave", "lev"), None, None),
            P(("wave", "lev")),
            P(),
        ),
        out_specs=P(None, "wave", "lev"),
        check_vma=False,
    )
```

profile of v0, /device:TPU:0, one launch (start us, length us, event | category | flops | bytes accessed | tf_op | source)
XLA Modules:
  0.0 410.6 jit_solution(1927819315632547390)
XLA Ops:
  0.8 2.9 fusion.21
  4.0 10.3 %copy.20 = bf16[1,2,1280,512]{3,1,0,2:T(2,128)(2,1)S(1)} copy(bf16[1,2,1280,512]{3,2,1,0:T(8,128)(2,1)S(1)} %pad_maximum_fusion) | data formatting | bytes 5242880 | tf_op jit(solution)/shard_map/stack | solution.py:19
  14.3 67.8 %all_to_all.38 = bf16[1,2,1280,512]{3,1,0,2:T(2,128)(2,1)S(1)} all-to-all(bf16[1,2,1280,512]{3,1,0,2:T(2,128)(2,1)S(1)} %copy.20), channel_id=1, replica_groups=mesh['wave'=8,'lev'=4] {'wave','lev'}, dimensions={2} | all-to-all | bytes 5242880 | tf_op jit(solution)/shard_map/all_to_all | solution.py:50
  84.2 4.9 %reshape.90 = bf16[32,2,40,4,128]{4,3,2,1,0:T(4,128)(2,1)} reshape(bf16[32,1,2,40,512]{4,3,2,0,1:T(8,128)(2,1)} %bitcast.74) | data formatting | bytes 5242880 | tf_op jit(solution)/shard_map/reshape | solution.py:52
  89.1 5.4 %convert_bitcast_fusion = bf16[32,2,40,4,128]{4,0,3,1,2:T(8,128)(2,1)S(1)} fusion(f32[40,128,128]{2,1,0:T(8,128)S(1)} %copy-done, bf16[32,2,40,4,128]{4,3,2,1,0:T(4,128)(2,1)} %reshape.90), kind=kOutput, calls=%fused_computation.17 | convolution fusion | flops 2014576640 | bytes 7864320 | tf_op jit(solution)/shard_map/nij,pgncj->pgnci/dot_general | solution.py:53
  95.8 3.0 reshape.91
  98.8 3.3 all-to-all-start.1
  102.3 59.9 %all-to-all-done.1 = bf16[32,2,40,512]{3,2,1,0:T(8,128)(2,1)S(1)} async-done(((bf16[32,2,40,512]{3,2,1,0:T(8,128)(2,1)}), bf16[32,2,40,512]{3,2,1,0:T(8,128)(2,1)S(1)}, u32[]{:S(2)}, u32[]{:S(2)}) %all-to-all-start.1) | async-done | bytes 2621472 | tf_op jit(solution)/shard_map/all_to_all | solution.py:60
  165.2 10.3 %fusion.7 = bf16[1,2,2560,512]{2,3,1,0:T(8,128)(2,1)} fusion(bf16[1,1281,2560]{2,1,0:T(8,128)(2,1)S(1)} %bitcast.76, bf16[1,1,1281,512]{3,2,1,0:T(8,128)(2,1)S(1)} %get-tuple-element.162, bf16[1,1,1281,512]{3,2,1,0:T(8,128)(2,1)S(1)} %get-tuple-element.161), kind=kOutput, calls=%fused_computation.6 | convolution fusion | flops 6720062464 | bytes 14425088 | tf_op jit(solution)/shard_map/psl,pgsk->pglk/dot_general | solution.py:62
  175.5 8.0 %copy.28 = bf16[1,2,2560,512]{3,2,1,0:T(8,128)(2,1)} copy(bf16[1,2,2560,512]{2,3,1,0:T(8,128)(2,1)} %fusion.7) | data formatting | bytes 10485760
  183.5 5.5 %concatenate.15.clone = bf16[1,2,2960,512]{3,2,1,0:T(8,128)(2,1)} pad(bf16[1,2,2560,512]{3,2,1,0:T(8,128)(2,1)} %copy.28, bf16[]{:T(256)} %constant.63.clone.1), padding=0_0x0_0x0_400x0_0 | pad | bytes 11304962 | tf_op jit(solution)/shard_map/concatenate | solution.py:66
  189.0 3.2 broadcast_in_dim.48
  192.2 49.2 %while.14 = (s32[]{:T(128)}, bf16[1,2,3200,512]{3,2,1,0:T(8,128)(2,1)}, s32[8]{0:T(128)S(1)}, s32[8]{0:T(128)S(1)}, bf16[1,2,2960,512]{3,2,1,0:T(8,128)(2,1)}, /...) while((s32[]{:T(128)}, bf16[1,2,3200,512]{3,2,1,0:T(8,128)(2,1)}, ...), condition=%wide.region_2.3_spmd.clone, body=%wide.region_1.2_spmd.clone.sunk | while | flops 410009 | bytes 1639425 | solution.py:79
  196.0 2.3 select_dynamic-update-slice_fusion.2
  202.1 2.3 select_dynamic-update-slice_fusion.2
  214.5 2.3 select_dynamic-update-slice_fusion.2
  220.6 2.3 select_dynamic-update-slice_fusion.2
  226.8 2.3 select_dynamic-update-slice_fusion.2
  232.9 2.3 select_dynamic-update-slice_fusion.2
  239.1 2.3 select_dynamic-update-slice_fusion.2
  241.4 12.2 %reshape_reshape.3 = bf16[2,8,400,4,128]{4,3,2,1,0:T(4,128)(2,1)} reshape(bf16[1,2,3200,512]{3,2,1,0:T(8,128)(2,1)} %get-tuple-element.114) | data formatting | bytes 13107200 | tf_op jit(solution)/shard_map/reshape;reshape | solution.py:86
  253.6 4.0 copy.26
  257.7 149.3 %all_to_all.39 = bf16[64,400,128]{2,1,0:T(8,128)(2,1)S(1)} all-to-all(bf16[64,400,128]{2,1,0:T(8,128)(2,1)S(1)} %bitcast.70), channel_id=1, replica_groups=mesh['wave'=8,'lev'=4] {'wave','lev'}, dimensions={0} | all-to-all | bytes 13107200 | tf_op jit(solution)/shard_map/all_to_all | solution.py:90
  406.9 3.1 copy.44
  (46 shorter events, 24.9 us)
Async XLA Ops:
  0.0 89.1 %copy-start = (f32[40,128,128]{2,1,0:T(8,128)S(1)}, f32[40,128,128]{2,1,0:T(8,128)}, u32[]{:S(2)}) copy-start(f32[40,128,128]{2,1,0:T(8,128)} %param.8) | copy-start | bytes 7864324
  98.8 3.3 copy-start.2
  98.8 63.4 %all-to-all-start.1 = ((bf16[32,2,40,512]{3,2,1,0:T(8,128)(2,1)}), bf16[32,2,40,512]{3,2,1,0:T(8,128)(2,1)S(1)}, u32[]{:S(2)}, u32[]{:S(2)}) async-start(bf16[32,2,40,512]{3,2,1,0:T(8,128)(2,1)} %reshape.91), calls=%async_computation.1 | async-start | bytes 5242880 | tf_op jit(solution)/shard_map/all_to_all | solution.py:60
  162.2 2.2 slice-start
  162.4 2.8 slice-start.1
  406.9 3.7 copy-start.1
where the time goes:
time: 412 us; the launch traced here: 411 us
  blocking collectives  217 us (53%)
  local copies, waits for them, and re-layouts  70.2 us (17%)
  waiting for transfers between devices  59.9 us (15%)
  other arithmetic  28.2 us (7%)
  matrix products  15.7 us (4%)
  loops' own time  15.3 us (4%)
    all_to_all x1, blocking collectives, per_device(): lax.all_to_all(outgoing, ('wave', 'lev'), split_axis=0, concat_axis=0, ti...  149 us
    all_to_all x1, blocking collectives, per_device(): lax.all_to_all(spectra, ('wave', 'lev'), split_axis=2, concat_axis=0, til...  67.8 us
    all_to_all x1, waiting for transfers between devices, per_device(): lax.all_to_all(product, ('wave', 'lev'), split_axis=0, concat_axis=2, til...  59.9 us
    dynamic_update_slice x8, other arithmetic, put_band(): lax.dynamic_update_slice_in_dim(collected, piece, (wave_pos * band_depth)...  18.8 us
    another operation x2, local copies, waits for them, and re-layouts, per_device(): picked.reshape(pair_count * 2, wave_count, band_depth, level_count, level...  16.2 us
    another operation x1, loops' own time, per_device(): lax.fori_loop(0, wave_count, put_band, jnp.zeros((pair_count, 2, wave_cou...  15.3 us
    unnamed x12, local copies, waits for them, and re-layouts  13.3 us
    dot_general x1, matrix products, per_device(): jnp.einsum('psl,pgsk->pglk', legendre, halves, preferred_element_type=jnp...  10.3 us
  transfers between devices with their start and end apart: 1, of which 1 were waited for; matrix products, arithmetic and copies ran while one was open for 0% of the time, Pallas kernels for 0%

commit v1 on v0

v1 whole, which is shorter than its diff:
```python
import functools

import jax
import jax.numpy as jnp
import numpy as np
from jax import lax
from jax.experimental import pallas as pl
from jax.experimental.pallas import tpu as pltpu
from jax.sharding import PartitionSpec as P

BF = jnp.bfloat16
F32 = jnp.float32
VMEM_LIMIT = 56 * 1024 * 1024
SUB = 16


def ceil_to(value, step):
    return (value + step - 1) // step * step


class Plan:
    def __init__(self, devices, degrees):
        self.devices = devices
        self.group = devices // 2
        self.degrees = degrees
        self.block = degrees // devices
        self.chunks = []
        row, fold = 0, 0
        for count in self.fold_counts(self.block):
            self.chunks.append((row, fold, count))
            row += ceil_to(2 * count, SUB)
            fold += count
        self.rows = row

    @staticmethod
    def fold_counts(block):
        return (block,)

    def row_tables(self):
        fold = np.zeros(self.rows, np.int32)
        folded = np.zeros(self.rows, bool)
        used = np.zeros(self.rows, bool)
        for row, first, count in self.chunks:
            index = np.arange(count)
            fold[row:row + count] = first + index
            folded[row:row + count] = True
            fold[row + count:row + 2 * count] = first + index
            used[row:row + 2 * count] = True
        return fold, folded, used


def pack_kernel(plan, levels, info_ref, slot_ref, control_ref, out_ref):
    slots = control_ref.shape[0]
    messages = out_ref.shape[0]
    even = slots - 1
    rows = messages * plan.rows
    slot = slot_ref[...]
    pick = (slot == lax.broadcasted_iota(jnp.int32, (rows, even), 1)).astype(F32).astype(BF)
    got = jnp.dot(pick, control_ref[:even, :], preferred_element_type=F32)
    last = control_ref[even:slots, :].astype(F32)
    got = jnp.where(slot == even, last, got).astype(BF)
    extra_slot = plan.degrees - info_ref[0]
    lane = lax.broadcasted_iota(jnp.int32, (SUB, even), 1)
    first = lax.broadcasted_iota(jnp.int32, (SUB, even), 0) == 0
    choose = jnp.where(first & (lane == extra_slot), 1.0, 0.0).astype(BF)
    extra = jnp.dot(choose, control_ref[:even, :], preferred_element_type=F32)
    extra = jnp.where(extra_slot == even, last, extra)
    place = lax.broadcasted_iota(jnp.int32, (SUB, levels), 0)
    tail = jnp.zeros((SUB, levels), F32)
    for c in range(4):
        tail = jnp.where(place == c, extra[0:1, c * levels:(c + 1) * levels], tail)
    tail = tail.astype(BF)
    for k in range(messages):
        for c in range(4):
            out_ref[k, c * plan.rows:(c + 1) * plan.rows, :] = got[
                k * plan.rows:(k + 1) * plan.rows, c * levels:(c + 1) * levels
            ]
        out_ref[k, 4 * plan.rows:, :] = tail


def pack(plan, control, lowest, slots_of_rows):
    slots, columns = control.shape
    levels = columns // 4
    height = 4 * plan.rows + SUB
    per_step = max(1, min(plan.group, 320 // plan.rows))
    return pl.pallas_call(
        functools.partial(pack_kernel, plan, levels),
        grid=(plan.group // per_step,),
        out_shape=jax.ShapeDtypeStruct((plan.group, height, levels), BF),
        in_specs=[
            pl.BlockSpec(memory_space=pltpu.SMEM),
            pl.BlockSpec((per_step * plan.rows, 1), lambda k: (k, 0)),
            pl.BlockSpec((slots, columns), lambda k: (0, 0)),
        ],
        out_specs=pl.BlockSpec((per_step, height, levels), lambda k: (k, 0, 0)),
        compiler_params=pltpu.CompilerParams(vmem_limit_bytes=VMEM_LIMIT),
        cost_estimate=pl.CostEstimate(
            flops=2 * plan.group * plan.rows * slots * columns,
            bytes_accessed=slots * columns * 2 + plan.group * height * levels * 2,
            transcendentals=0,
        ),
        name="pack_rows",
    )(lowest, slots_of_rows, control)


def swap_matrix():
    i = lax.broadcasted_iota(jnp.int32, (SUB * SUB, SUB * SUB), 0)
    j = lax.broadcasted_iota(jnp.int32, (SUB * SUB, SUB * SUB), 1)
    return jnp.where((i // SUB == j % SUB) & (i % SUB == j // SUB), 1.0, 0.0).astype(BF)


def filter_kernel(plan, chunk, with_extra, levels, info_ref, lowest_ref, low_ref, rows_ref, own_ref, other_ref, out_ref, x_ref, y_ref):
    row0, fold0, count = chunk
    height = ceil_to(2 * count, SUB)
    is_high = info_ref[0] == 1
    first_fold = info_ref[1]
    block = plan.block
    swap = swap_matrix()

    def low_matrix(fold):
        return jnp.where(is_high, other_ref[fold], own_ref[fold])

    def high_matrix(fold):
        return jnp.where(is_high, own_ref[block - 1 - fold], other_ref[block - 1 - fold])

    def times(rows, matrix):
        return lax.dot_general(rows, matrix, (((1,), (1,)), ((), ())), preferred_element_type=F32)

    for g in range(plan.group // SUB):
        sources = range(g * SUB, (g + 1) * SUB)
        for r in range(0, height, SUB):
            parts = []
            for c in range(4):
                at = c * plan.rows + row0 + r
                parts.append(
                    rows_ref[g * SUB:(g + 1) * SUB, at:at + SUB, :].reshape(SUB * SUB, levels)
                )
            block_rows = jnp.concatenate(parts, axis=1)
            x_ref[r * SUB:(r + SUB) * SUB, :] = jnp.dot(
                swap, block_rows, preferred_element_type=F32
            ).astype(BF)
        low = low_ref[g * SUB:(g + 1) * SUB, :]
        low = jnp.concatenate([low] * 4, axis=0)
        for i in range(count):
            def stack(row):
                return jnp.concatenate(
                    [x_ref[row * SUB:(row + 1) * SUB, c * levels:(c + 1) * levels] for c in range(4)], axis=0
                )

            folded, high = stack(i), stack(count + i)
            from_low = times(folded, low_matrix(fold0 + i))
            from_high = times(jnp.concatenate([folded, high], axis=0), high_matrix(fold0 + i))
            mixed = jnp.where(low <= first_fold + fold0 + i, from_low, from_high[:4 * SUB])
            for row, value in ((i, mixed), (count + i, from_high[4 * SUB:])):
                value = value.astype(BF)
                for c in range(4):
                    y_ref[row * SUB:(row + 1) * SUB, c * levels:(c + 1) * levels] = value[c * SUB:(c + 1) * SUB]
        if height > 2 * count:
            y_ref[2 * count * SUB:height * SUB, :] = jnp.zeros(((height - 2 * count) * SUB, 4 * levels), BF)
        for r in range(0, height, SUB):
            back = jnp.dot(swap, y_ref[r * SUB:(r + SUB) * SUB, :], preferred_element_type=F32).astype(BF)
            for c in range(4):
                at = c * height + r
                out_ref[g * SUB:(g + 1) * SUB, at:at + SUB, :] = back[:, c * levels:(c + 1) * levels].reshape(
                    SUB, SUB, levels
                )
        if with_extra:
            for s in sources:
                fold = jnp.clip(lowest_ref[info_ref[2] + s] - first_fold, 0, block - 1)
                value = times(rows_ref[s, 4 * plan.rows:4 * plan.rows + SUB, :], high_matrix(fold))
                out_ref[s, 4 * height:4 * height + SUB, :] = value.astype(BF)


def filter_rows(plan, chunk, with_extra, info, lowest_all, low_rows, received, own, other):
    levels = received.shape[2]
    height = ceil_to(2 * chunk[2], SUB)
    out_height = 4 * height + (SUB if with_extra else 0)
    smem = pl.BlockSpec(memory_space=pltpu.SMEM)
    vmem = pl.BlockSpec(memory_space=pltpu.VMEM)
    return pl.pallas_call(
        functools.partial(filter_kernel, plan, chunk, with_extra, levels),
        out_shape=jax.ShapeDtypeStruct((plan.group, out_height, levels), BF),
        in_specs=[smem, smem, vmem, vmem, vmem, vmem],
        out_specs=vmem,
        scratch_shapes=[
            pltpu.VMEM((height * SUB, 4 * levels), BF),
            pltpu.VMEM((height * SUB, 4 * levels), BF),
        ],
        compiler_params=pltpu.CompilerParams(vmem_limit_bytes=VMEM_LIMIT),
        cost_estimate=pl.CostEstimate(
            flops=2 * plan.group * 12 * chunk[2] * levels * levels * 4,
            bytes_accessed=plan.group * out_height * levels * 4 + 4 * chunk[2] * levels * levels,
            transcendentals=0,
        ),
        name="filter_rows",
    )(info, lowest_all, low_rows, received, own, other)


def grid_kernel(plan, levels, latitudes, depth, level_cols, info_ref, starts_ref, bands_ref, *refs):
    count = len(plan.chunks)
    parts = refs[:count]
    table_ref, out_ref, rows_ref, grid_ref = refs[count:]
    half, step = pl.program_id(0), pl.program_id(1)
    tile = table_ref.shape[1]

    @pl.when((half == 0) & (step == 0))
    def _():
        for k in range(plan.group):
            for c in range(4):
                for (row, _, folds), part in zip(plan.chunks, parts):
                    height = ceil_to(2 * folds, SUB)
                    at = k * plan.rows + row
                    rows_ref[at:at + height, c * levels:(c + 1) * levels] = part[k, c * height:(c + 1) * height, :]

    @pl.when((half == 1) & (step == 0))
    def _():
        height = ceil_to(2 * plan.chunks[-1][2], SUB)
        extra = parts[-1][info_ref[0], 4 * height:4 * height + SUB, :]
        base = info_ref[1] // SUB * SUB
        at = pl.ds(pl.multiple_of(base, SUB), SUB)
        here = lax.broadcasted_iota(jnp.int32, (SUB, levels), 0) == info_ref[1] - base
        for c in range(4):
            cols = slice(c * levels, (c + 1) * levels)
            held = rows_ref[at, cols].astype(F32)
            rows_ref[at, cols] = jnp.where(here, extra[c:c + 1, :].astype(F32), held).astype(BF)

    @pl.when((half == 0) & (step == 0))
    def _():
        grid_ref[latitudes:, :] = jnp.zeros((grid_ref.shape[0] - latitudes, 4 * levels), BF)

    grid_ref[pl.ds(pl.multiple_of(step * tile, tile), tile), :] = jnp.dot(
        table_ref[0], rows_ref[...], preferred_element_type=F32
    ).astype(BF)

    @pl.when(step == pl.num_programs(1) - 1)
    def _():
        waves = bands_ref.shape[0]
        groups = 4 * levels // level_cols
        piece = 80 if depth % 80 == 0 else depth
        window = ceil_to(piece + SUB - 1, SUB)
        i = lax.broadcasted_iota(jnp.int32, (piece, window), 0)
        j = lax.broadcasted_iota(jnp.int32, (piece, window), 1)
        for w in range(waves):
            start = starts_ref[w]
            base = start // SUB * SUB
            moved = j - i == start - base
            for r in range(0, depth, piece):
                pick = jnp.where(moved & (i < bands_ref[w] - r), 1.0, 0.0).astype(BF)
                held = grid_ref[pl.ds(pl.multiple_of(base + r, SUB), window), :]
                got = jnp.dot(pick, held, preferred_element_type=F32).astype(BF)
                for g in range(groups):
                    out_ref[w * groups + g, 0, r:r + piece, :] = got[:, g * level_cols:(g + 1) * level_cols]


def to_bands(plan, info, starts, bands, parts, table, depth, level_cols):
    halves, latitudes, width = table.shape
    levels = parts[0].shape[2]
    columns = 4 * levels
    waves = bands.shape[0]
    tile = 512
    smem = pl.BlockSpec(memory_space=pltpu.SMEM)
    messages = waves * columns // level_cols
    return pl.pallas_call(
        functools.partial(grid_kernel, plan, levels, latitudes, depth, level_cols),
        grid=(halves, latitudes // tile),
        out_shape=jax.ShapeDtypeStruct((messages, halves, depth, level_cols), BF),
        in_specs=[smem, smem, smem]
        + [pl.BlockSpec(part.shape, lambda h, t: (0, 0, 0)) for part in parts]
        + [pl.BlockSpec((1, tile, width), lambda h, t: (h, t, 0))],
        out_specs=pl.BlockSpec((messages, 1, depth, level_cols), lambda h, t: (0, h, 0, 0)),
        scratch_shapes=[
            pltpu.VMEM((width, columns), BF),
            pltpu.VMEM((ceil_to(latitudes + depth, SUB) + SUB, columns), BF),
        ],
        compiler_params=pltpu.CompilerParams(vmem_limit_bytes=VMEM_LIMIT),
        cost_estimate=pl.CostEstimate(
            flops=2 * halves * latitudes * width * columns,
            bytes_accessed=2 * halves * latitudes * width + 2 * messages * halves * depth * level_cols,
            transcendentals=0,
        ),
        name="grid_bands",
    )(info, starts, bands, *parts, table)


def per_device(control, covariance, legendre, pair_order, band_rows):
    axes = ("wave", "lev")
    waves, lev_count = lax.axis_size("wave"), lax.axis_size("lev")
    _, slots, columns = control.shape
    degrees, levels = slots - 1, columns // 4
    latitudes = legendre.shape[2]
    depth = 5 * latitudes // (4 * waves)
    level_cols = columns // lev_count
    plan = Plan(waves * lev_count, degrees)
    group, block = plan.group, plan.block
    me = lax.axis_index("wave") * lev_count + lax.axis_index("lev")
    is_high = (me >= group).astype(jnp.int32)
    rank = me - group * is_high
    mine = jnp.where(is_high == 1, group - 1 - rank, rank)
    lowest = pair_order[0]
    halves = [list(range(group)), list(range(group, 2 * group))]

    own = covariance.astype(BF)
    other = lax.ppermute(own, axes, [(d, 2 * group - 1 - d) for d in range(2 * group)])
    lowest_all = lax.all_gather(pair_order, axes, tiled=True)

    fold, folded, used = plan.row_tables()
    message = jnp.arange(group, dtype=jnp.int32)
    message = jnp.where(is_high == 1, group - 1 - message, message)
    degree = (message[:, None] * block + fold[None, :]).reshape(-1)
    folded = jnp.asarray(np.tile(folded, group))
    used = jnp.asarray(np.tile(used, group))
    upper = jnp.where(folded, degree - lowest, degrees - 1 - degree - lowest)
    upper = jnp.where(used & (upper >= 0), upper, -1)
    lower = jnp.where(used & folded, degrees - degree, -1)
    sent = jnp.where(used & folded & (degree < lowest), lower, upper)
    lower = jnp.where(degree <= lowest, lower, -1)

    packed = pack(plan, control[0], pair_order, sent[:, None])
    received = lax.all_to_all(packed, axes, split_axis=0, concat_axis=0, tiled=True, axis_index_groups=halves)

    slot_index = jnp.arange(slots, dtype=jnp.int32)[:, None]
    pick = jnp.stack([upper, lower])[:, None, :] == slot_index[None]
    table = jnp.einsum("sl,hsr->hlr", legendre[0], pick.astype(BF), preferred_element_type=F32).astype(BF)

    info = jnp.stack([is_high, mine * block, is_high * group])
    low_group = lax.dynamic_slice_in_dim(lowest_all, is_high * group, group, 0)
    low_rows = jnp.broadcast_to(low_group[:, None], (group, levels))
    parts = []
    for at, chunk in enumerate(plan.chunks):
        result = filter_rows(
            plan, chunk, at == len(plan.chunks) - 1, info, lowest_all, low_rows, received, own, other
        )
        parts.append(
            lax.all_to_all(result, axes, split_axis=0, concat_axis=0, tiled=True, axis_index_groups=halves)
        )

    extra_block = lowest // block
    extra_message = jnp.where(is_high == 1, group - 1 - extra_block, extra_block)
    extra_fold = lowest - extra_block * block
    extra_row = jnp.int32(0)
    for row, first, count in plan.chunks:
        extra_row = jnp.where(extra_fold >= first, row + extra_fold - first, extra_row)
    where = jnp.stack([extra_message, extra_message * plan.rows + extra_row])
    starts = jnp.cumsum(band_rows) - band_rows
    outgoing = to_bands(plan, where, starts, band_rows, parts, table, depth, level_cols)
    outgoing = outgoing.reshape(-1, depth, level_cols)
    return lax.all_to_all(outgoing, axes, split_axis=0, concat_axis=0, tiled=True)


def solution(mesh):
    return jax.shard_map(
        per_device,
        mesh=mesh,
        in_specs=(
            P(("wave", "lev"), None, None),
            P(("wave", "lev"), None, None),
            P(("wave", "lev"), None, None),
            P(("wave", "lev")),
            P(),
        ),
        out_specs=P(None, "wave", "lev"),
        check_vma=False,
    )
```

time: 412 us -> 318 us (0.77)
  local copies, waits for them, and re-layouts: 70.2 us -> 6.53 us
  waiting for transfers between devices: 59.9 us -> 0.01 us
  Pallas kernels: 0 us -> 29.1 us
  other arithmetic: 28.2 us -> 5.55 us
  blocking collectives: 217 us -> 235 us
  loops' own time: 15.3 us -> 0 us
  starting transfers between devices: 3.3 us -> 15.9 us
  matrix products: 15.7 us -> 24.9 us
    unnamed x0 -> x1, blocking collectives: none -> 83.3 us
    all_to_all x2 -> x1, blocking collectives: 217 us -> 151 us  [per_device(): lax.all_to_all(outgoing, axes, split_axis=0, concat_axis=0, tiled=True)]
    all_to_all x1 -> x2, waiting for transfers between devices: 59.9 us -> 0.01 us  [the longest x1 0.01 us: per_device(): lax.all_to_all(packed, axes, split_axis=0, concat_axis=0, tiled=True, axi...]
    pallas_call x0 -> x3, Pallas kernels: none -> 29.1 us  [the longest x1 17.4 us: to_bands(): pl.pallas_call(functools.partial(grid_kernel, plan, levels, latitudes, de...]
    another operation x3 -> x2, local copies, waits for them, and re-layouts: 26.5 us -> 0.01 us  [per_device(): pick = jnp.stack([upper, lower])[:, None, :] == slot_index[None]]
    dynamic_update_slice x8 -> x0, other arithmetic: 18.8 us -> none  [put_band(): lax.dynamic_update_slice_in_dim(collected, piece, (wave_pos * band_depth)...]
    another operation x1 -> x0, loops' own time: 15.3 us -> none  [per_device(): lax.fori_loop(0, wave_count, put_band, jnp.zeros((pair_count, 2, wave_cou...]
    dynamic_slice x16 -> x1, local copies, waits for them, and re-layouts: 10.1 us -> 0.07 us  [per_device(): low_group = lax.dynamic_slice_in_dim(lowest_all, is_high * group, group, 0)]
  transfers between devices with their start and end apart: 1 -> 3, of which waited for: 1 -> 0; matrix products, arithmetic and copies ran while one was open for 0% -> 9% of each run, Pallas kernels for 0% -> 0%
where the time goes in v1:
time: 318 us
  blocking collectives  235 us (74%)
  Pallas kernels  29.1 us (9%)
  matrix products  24.9 us (8%)
  starting transfers between devices  15.9 us (5%)
  local copies, waits for them, and re-layouts  6.53 us (2%)
  other arithmetic  5.55 us (2%)
    all_to_all x1, blocking collectives, per_device(): lax.all_to_all(outgoing, axes, split_axis=0, concat_axis=0, tiled=True)  151 us
    unnamed x1, blocking collectives  83.3 us
    dot_general x1, matrix products, per_device(): jnp.einsum('sl,hsr->hlr', legendre[0], pick.astype(BF), preferred_element...  24.9 us
    pallas_call x1, Pallas kernels, to_bands(): pl.pallas_call(functools.partial(grid_kernel, plan, levels, latitudes, de...  17.4 us
  transfers between devices with their start and end apart: 3, of which 0 were waited for; matrix products, arithmetic and copies ran while one was open for 9% of the time, Pallas kernels for 0%

profile of v1, /device:TPU:0, one launch (start us, length us, event | category | flops | bytes accessed | tf_op | source)
XLA Modules:
  0.0 317.6 jit_solution(17078561698077680550)
XLA Ops:
  0.7 0.8 add_compare_fusion
  1.5 0.1 le.8
  1.5 0.1 reshape.59
  1.6 0.8 fusion.4
  2.6 1.1 broadcast_in_dim.20.slot_ref
  3.6 5.6 %pack_rows.1 = bf16[16,336,128]{2,1,0:T(8,128)(2,1)} custom-call(s32[1]{0:T(128)} %copy.15.info_ref, s32[1280,1]{1,0:T(8,128)} %broadcast_in_dim.20.slot_ref, bf16[1281,512]{1,0:T(8,128)(2,1)} %bitcast.24), custom_call_target="tpu_custom_call" | custom-call | flops 1679032320 | bytes 2688000 | tf_op jit(solution)/shard_map/pack_rows/pallas_call | solution.py:86
  9.3 6.3 %all-to-all-start = ((bf16[16,336,128]{2,1,0:T(8,128)(2,1)}), bf16[16,336,128]{2,1,0:T(8,128)(2,1)S(1)}, u32[]{:S(2)}, u32[]{:S(2)}) async-start(bf16[16,336,128]{2,1,0:T(8,128)(2,1)} %pack_rows.1), calls=%async_computation | async-start | bytes 2752512 | tf_op jit(solution)/shard_map/all_to_all | solution.py:319
  15.6 1.9 convert_element_type.13.own_ref
  17.5 5.6 %collective-permute-start = (bf16[40,128,128]{2,1,0:T(8,128)(2,1)S(1)}, bf16[40,128,128]{2,1,0:T(8,128)(2,1)}, u32[]{:S(2)}, u32[]{:S(2)}) collective-permute-start(bf16[40,128,128]{2,1,0:T(8,128)(2,1)S(1)} %convert_element_type.13.own_ref), channel_id=1, source_target_pairs={{0,31},{1,30},{2,29},{3,28},{4,27},{5,26},{6,25},{7,24},{8,23},{9,... | collective-permute-start | bytes 3932168 | tf_op jit(solution)/shard_map/ppermute | solution.py:303
  23.1 0.1 dynamic-update-slice
  23.2 83.3 %all-reduce.lowest_ref = s32[32]{0:T(128)S(1)} all-reduce(s32[32]{0:T(128)S(1)} %dynamic-update-slice), channel_id=1, replica_groups=mesh['wave'=8,'lev'=4] {'wave','lev'}, use_global_device_ids=true, to_apply=%add | all-reduce | flops 32 | bytes 256
  106.6 0.2 reduce-window.9
  106.8 0.6 pad_add_fusion.1.info_ref
  107.5 0.6 pad_add_fusion.2.info_ref
  108.1 0.6 bitcast_subtract_fusion.starts_ref
  108.7 0.8 broadcast_in_dim.17.low_ref
  109.5 0.3 copy-done
  109.8 6.1 %filter_rows.1 = bf16[16,336,128]{2,1,0:T(8,128)(2,1)} custom-call(s32[3]{0:T(128)} %pad_add_fusion.2.info_ref, s32[32]{0:T(128)} %copy-done.3, s32[16,128]{1,0:T(8,128)} %broadcast_in_dim.17.low_ref, bf16[16,336,128]{2,1,0:T(8,128)(2,1)} %copy-done, bf16[40,128,128]{2,1,0:T(8,128)(2,1)} %copy-done.1, bf16[40,128,128]{2,1,0:T(8,128)(2,1)} %collective-permute-done.other_ref), custom_call_target="tpu_custom_call" | custom-call | flops 1006632960 | bytes 5373952 | tf_op jit(solution)/shard_map/filter_rows/pallas_call | solution.py:180
  115.9 4.0 %all-to-all-start.1 = ((bf16[16,336,128]{2,1,0:T(8,128)(2,1)}), bf16[16,336,128]{2,1,0:T(8,128)(2,1)S(1)}, u32[]{:S(2)}, u32[]{:S(2)}) async-start(bf16[16,336,128]{2,1,0:T(8,128)(2,1)} %filter_rows.1), calls=%async_computation.1 | async-start | bytes 2752512 | tf_op jit(solution)/shard_map/all_to_all | solution.py:334
  119.9 24.9 %fusion.refs_1_ = bf16[2,2560,1280]{2,1,0:T(8,128)(2,1)} fusion(bf16[1,1281,2560]{2,1,0:T(8,128)(2,1)} %param.10, s32[2,1280]{1,0:T(2,128)S(1)} %pad_add_fusion), kind=kOutput, calls=%fused_computation.2 | convolution fusion | flops 16800155648 | bytes 19676160 | tf_op jit(solution)/shard_map/sl,hsr->hlr/dot_general | solution.py:323
  144.8 1.1 copy-done.2
  145.9 17.4 %grid_bands.1 = bf16[32,2,400,128]{3,2,1,0:T(8,128)(2,1)} custom-call(s32[2]{0:T(128)} %pad_add_fusion.1.info_ref, s32[8]{0:T(128)} %bitcast_subtract_fusion.starts_ref, s32[8]{0:T(128)} %bands_ref.1, bf16[16,336,128]{2,1,0:T(8,128)(2,1)} %copy-done.2, bf16[2,2560,1280]{2,1,0:T(8,128)(2,1)} %fusion.refs_1_), custom_call_target="tpu_custom_call" | custom-call | flops 6710886400 | bytes 19660800 | tf_op jit(solution)/shard_map/grid_bands/pallas_call | solution.py:263
  163.3 151.5 %all_to_all.15 = bf16[64,400,128]{2,1,0:T(8,128)(2,1)S(1)} all-to-all(bf16[64,400,128]{2,1,0:T(8,128)(2,1)} %bitcast.23), channel_id=1, replica_groups=mesh['wave'=8,'lev'=4] {'wave','lev'}, dimensions={0} | all-to-all | bytes 13107200 | tf_op jit(solution)/shard_map/all_to_all | solution.py:347
  314.8 2.8 copy.16
  (20 shorter events, 0.3 us)
Async XLA Ops:
  3.6 102.9 %copy-start.4 = (s32[8]{0:T(128)S(1)}, s32[8]{0:T(128)}, u32[]{:S(2)}) copy-start(s32[8]{0:T(128)} %bands_ref.1) | copy-start | bytes 100
  9.3 99.4 %all-to-all-start = ((bf16[16,336,128]{2,1,0:T(8,128)(2,1)}), bf16[16,336,128]{2,1,0:T(8,128)(2,1)S(1)}, u32[]{:S(2)}, u32[]{:S(2)}) async-start(bf16[16,336,128]{2,1,0:T(8,128)(2,1)} %pack_rows.1), calls=%async_computation | async-start | bytes 2752512 | tf_op jit(solution)/shard_map/all_to_all | solution.py:319
  17.5 92.0 %copy-start.1 = (bf16[40,128,128]{2,1,0:T(8,128)(2,1)}, bf16[40,128,128]{2,1,0:T(8,128)(2,1)S(1)}, u32[]{:S(2)}) copy-start(bf16[40,128,128]{2,1,0:T(8,128)(2,1)S(1)} %convert_element_type.13.own_ref) | copy-start | bytes 3932164
  17.5 91.2 %collective-permute-start = (bf16[40,128,128]{2,1,0:T(8,128)(2,1)S(1)}, bf16[40,128,128]{2,1,0:T(8,128)(2,1)}, u32[]{:S(2)}, u32[]{:S(2)}) collective-permute-start(bf16[40,128,128]{2,1,0:T(8,128)(2,1)S(1)} %convert_element_type.13.own_ref), channel_id=1, source_target_pairs={{0,31},{1,30},{2,29},{3,28},{4,27},{5,26},{6,25},{7,24},{8,23},{9,... | collective-permute-start | bytes 3932168 | tf_op jit(solution)/shard_map/ppermute | solution.py:303
  106.6 2.9 copy-start.3
  108.7 1.1 copy-start
  115.9 28.9 %all-to-all-start.1 = ((bf16[16,336,128]{2,1,0:T(8,128)(2,1)}), bf16[16,336,128]{2,1,0:T(8,128)(2,1)S(1)}, u32[]{:S(2)}, u32[]{:S(2)}) async-start(bf16[16,336,128]{2,1,0:T(8,128)(2,1)} %filter_rows.1), calls=%async_computation.1 | async-start | bytes 2752512 | tf_op jit(solution)/shard_map/all_to_all | solution.py:334
  144.8 1.1 copy-start.2

commit v2 on v1

v2 whole, which is shorter than its diff:
```python
import functools

import jax
import jax.numpy as jnp
import numpy as np
from jax import lax
from jax.experimental import pallas as pl
from jax.experimental.pallas import tpu as pltpu
from jax.sharding import PartitionSpec as P

BF = jnp.bfloat16
F32 = jnp.float32
VMEM_LIMIT = 56 * 1024 * 1024
SUB = 16
DIGIT = 16


def ceil_to(value, step):
    return (value + step - 1) // step * step


class Plan:
    def __init__(self, devices, degrees):
        self.devices = devices
        self.group = devices // 2
        self.degrees = degrees
        self.block = degrees // devices
        self.chunks = []
        row, fold = 0, 0
        for count in self.fold_counts(self.block):
            self.chunks.append((row, fold, count))
            row += ceil_to(2 * count, SUB)
            fold += count
        self.rows = row
        whole = [(at, n) for at, (_, _, n) in enumerate(self.chunks) if n % SUB == 0]
        mixed = [(at, n) for at, (_, _, n) in enumerate(self.chunks) if n % SUB]
        lower = [(at, 0, n) for at, n in whole] + [(at, 0, ceil_to(2 * n, SUB)) for at, n in mixed]
        self.segments = lower + [(at, n, n) for at, n in whole]
        self.widths = [
            self.group * sum(n for _, _, n in self.segments),
            self.group * sum(n for _, _, n in lower),
        ]

    @staticmethod
    def fold_counts(block):
        return (block - 8, 8) if block % SUB == 8 and block > 8 else (block,)

    def chunk_rows(self, at):
        _, first, count = self.chunks[at]
        height = ceil_to(2 * count, SUB)
        fold = np.zeros(height, np.int32)
        fold[:2 * count] = first + np.tile(np.arange(count), 2)
        row = np.arange(height)
        return fold, row < count, row < 2 * count

    def message_rows(self):
        tables = [self.chunk_rows(at) for at in range(len(self.chunks))]
        one = [np.concatenate(column) for column in zip(*tables)]
        return [np.repeat(np.arange(self.group, dtype=np.int32), self.rows)] + [
            np.tile(column, self.group) for column in one
        ]

    def transform_rows(self):
        parts = []
        for at, first, count in self.segments:
            columns = [column[first:first + count] for column in self.chunk_rows(at)]
            parts.append(
                [np.repeat(np.arange(self.group, dtype=np.int32), count)]
                + [np.tile(column, self.group) for column in columns]
            )
        return [np.concatenate(column) for column in zip(*parts)]

    def extra_row(self, message, fold):
        base, result = 0, jnp.int32(0)
        for at, first, count in self.segments:
            if first == 0:
                start = self.chunks[at][1]
                here = (fold >= start) & (fold < start + self.chunks[at][2])
                result = jnp.where(here, base + message * count + fold - start, result)
            base += self.group * count
        return result


def pack_kernel(plan, levels, info_ref, slot_ref, control_ref, out_ref):
    slots = control_ref.shape[0]
    messages = out_ref.shape[0]
    even = slots - 1
    rows = messages * plan.rows
    slot = slot_ref[...]
    pick = (slot == lax.broadcasted_iota(jnp.int32, (rows, even), 1)).astype(F32).astype(BF)
    got = jnp.dot(pick, control_ref[:even, :], preferred_element_type=F32)
    last = control_ref[even:slots, :].astype(F32)
    got = jnp.where(slot == even, last, got).astype(BF)
    extra_slot = plan.degrees - info_ref[0]
    lane = lax.broadcasted_iota(jnp.int32, (SUB, even), 1)
    first = lax.broadcasted_iota(jnp.int32, (SUB, even), 0) == 0
    choose = jnp.where(first & (lane == extra_slot), 1.0, 0.0).astype(BF)
    extra = jnp.dot(choose, control_ref[:even, :], preferred_element_type=F32)
    extra = jnp.where(extra_slot == even, last, extra)
    place = lax.broadcasted_iota(jnp.int32, (SUB, levels), 0)
    tail = jnp.zeros((SUB, levels), F32)
    for c in range(4):
        tail = jnp.where(place == c, extra[0:1, c * levels:(c + 1) * levels], tail)
    high_digit = (info_ref[0] // DIGIT).astype(F32)
    low_digit = (info_ref[0] % DIGIT).astype(F32)
    tail = jnp.where(place == 4, high_digit, jnp.where(place == 5, low_digit, tail)).astype(BF)
    for k in range(messages):
        for c in range(4):
            out_ref[k, c * plan.rows:(c + 1) * plan.rows, :] = got[
                k * plan.rows:(k + 1) * plan.rows, c * levels:(c + 1) * levels
            ]
        out_ref[k, 4 * plan.rows:, :] = tail


def pack(plan, control, lowest, slots_of_rows):
    slots, columns = control.shape
    levels = columns // 4
    height = 4 * plan.rows + SUB
    per_step = max(1, min(plan.group, 320 // plan.rows))
    return pl.pallas_call(
        functools.partial(pack_kernel, plan, levels),
        grid=(plan.group // per_step,),
        out_shape=jax.ShapeDtypeStruct((plan.group, height, levels), BF),
        in_specs=[
            pl.BlockSpec(memory_space=pltpu.SMEM),
            pl.BlockSpec((per_step * plan.rows, 1), lambda k: (k, 0)),
            pl.BlockSpec((slots, columns), lambda k: (0, 0)),
        ],
        out_specs=pl.BlockSpec((per_step, height, levels), lambda k: (k, 0, 0)),
        compiler_params=pltpu.CompilerParams(vmem_limit_bytes=VMEM_LIMIT),
        cost_estimate=pl.CostEstimate(
            flops=2 * plan.group * plan.rows * slots * columns,
            bytes_accessed=slots * columns * 2 + plan.group * height * levels * 2,
            transcendentals=0,
        ),
        name="pack_rows",
    )(lowest, slots_of_rows, control)


def swap_matrix():
    i = lax.broadcasted_iota(jnp.int32, (SUB * SUB, SUB * SUB), 0)
    j = lax.broadcasted_iota(jnp.int32, (SUB * SUB, SUB * SUB), 1)
    return jnp.where((i // SUB == j % SUB) & (i % SUB == j // SUB), 1.0, 0.0).astype(BF)


def filter_kernel(plan, at, levels, info_ref, rows_ref, own_ref, other_ref, *refs):
    row0, fold0, count = plan.chunks[at]
    last = at == len(plan.chunks) - 1
    before_ref = None if at == 0 else refs[0]
    out_ref, *carry, x_ref, y_ref = refs[0 if at == 0 else 1:]
    height = ceil_to(2 * count, SUB)
    is_high = info_ref[0] == 1
    first_fold = (info_ref[1] + fold0).astype(F32)
    swap = swap_matrix()

    def low_matrix(i):
        return jnp.where(is_high, other_ref[i], own_ref[i])

    def high_matrix(i):
        return jnp.where(is_high, own_ref[count - 1 - i], other_ref[count - 1 - i])

    def times(rows, matrix):
        return lax.dot_general(rows, matrix, (((1,), (1,)), ((), ())), preferred_element_type=F32)

    def turn(rows):
        return jnp.dot(swap, rows, preferred_element_type=F32)

    for g in range(plan.group // SUB):
        sources = slice(g * SUB, (g + 1) * SUB)
        for r in range(0, height, SUB):
            parts = []
            for c in range(4):
                start = c * plan.rows + row0 + r
                parts.append(rows_ref[sources, start:start + SUB, :].reshape(SUB * SUB, levels))
            x_ref[r * SUB:(r + SUB) * SUB, :] = turn(jnp.concatenate(parts, axis=1)).astype(BF)
        tail = turn(rows_ref[sources, 4 * plan.rows:4 * plan.rows + SUB, :].reshape(SUB * SUB, levels))
        extra = tail[:4 * SUB].astype(BF)
        low = tail[4 * SUB:5 * SUB] * DIGIT + tail[5 * SUB:6 * SUB]
        low = jnp.concatenate([low] * 4, axis=0)
        if at == 0:
            kept = jnp.zeros((4 * SUB, levels), F32)
        else:
            kept = before_ref[4 * SUB * g:4 * SUB * (g + 1), :]
        for i in range(count):
            def stack(row):
                return jnp.concatenate(
                    [x_ref[row * SUB:(row + 1) * SUB, c * levels:(c + 1) * levels] for c in range(4)], axis=0
                )

            folded, high = stack(i), stack(count + i)
            from_low = times(folded, low_matrix(i))
            from_high = times(jnp.concatenate([folded, high, extra], axis=0), high_matrix(i))
            mixed = jnp.where(low <= first_fold + i, from_low, from_high[:4 * SUB])
            kept = jnp.where(low == first_fold + i, from_high[8 * SUB:], kept)
            for row, value in ((i, mixed), (count + i, from_high[4 * SUB:8 * SUB])):
                value = value.astype(BF)
                for c in range(4):
                    y_ref[row * SUB:(row + 1) * SUB, c * levels:(c + 1) * levels] = value[c * SUB:(c + 1) * SUB]
        if height > 2 * count:
            y_ref[2 * count * SUB:height * SUB, :] = jnp.zeros(((height - 2 * count) * SUB, 4 * levels), BF)
        for r in range(0, height, SUB):
            back = turn(y_ref[r * SUB:(r + SUB) * SUB, :]).astype(BF)
            for c in range(4):
                out_ref[sources, c * height + r:c * height + r + SUB, :] = back[
                    :, c * levels:(c + 1) * levels
                ].reshape(SUB, SUB, levels)
        if last:
            filled = jnp.concatenate([kept, jnp.zeros((12 * SUB, levels), F32)], axis=0).astype(BF)
            out_ref[sources, 4 * height:4 * height + SUB, :] = turn(filled).astype(BF).reshape(SUB, SUB, levels)
        else:
            carry[0][4 * SUB * g:4 * SUB * (g + 1), :] = kept


def filter_rows(plan, at, info, received, own, other, before):
    levels = received.shape[2]
    count = plan.chunks[at][2]
    last = at == len(plan.chunks) - 1
    height = ceil_to(2 * count, SUB)
    out_height = 4 * height + (SUB if last else 0)
    smem = pl.BlockSpec(memory_space=pltpu.SMEM)
    vmem = pl.BlockSpec(memory_space=pltpu.VMEM)
    out_shape = [jax.ShapeDtypeStruct((plan.group, out_height, levels), BF)]
    if not last:
        out_shape.append(jax.ShapeDtypeStruct((4 * plan.group, levels), F32))
    operands = [info, received, own, other] + ([] if at == 0 else [before])
    return pl.pallas_call(
        functools.partial(filter_kernel, plan, at, levels),
        out_shape=out_shape,
        in_specs=[smem] + [vmem] * (len(operands) - 1),
        out_specs=[vmem] * len(out_shape),
        scratch_shapes=[
            pltpu.VMEM((height * SUB, 4 * levels), BF),
            pltpu.VMEM((height * SUB, 4 * levels), BF),
        ],
        compiler_params=pltpu.CompilerParams(vmem_limit_bytes=VMEM_LIMIT),
        cost_estimate=pl.CostEstimate(
            flops=2 * plan.group * 16 * count * levels * levels * 4,
            bytes_accessed=plan.group * out_height * levels * 4 + 4 * count * levels * levels,
            transcendentals=0,
        ),
        name="filter_rows",
    )(*operands)


def grid_kernel(plan, half, levels, latitudes, depth, level_cols, info_ref, starts_ref, bands_ref, *refs):
    count = len(plan.chunks)
    parts = refs[:count]
    table_ref, out_ref, rows_ref, grid_ref = refs[count:]
    step = pl.program_id(0)
    tile, width = table_ref.shape

    @pl.when(step == 0)
    def _():
        grid_ref[latitudes:, :] = jnp.zeros((grid_ref.shape[0] - latitudes, 4 * levels), BF)
        base = 0
        for at, first, rows in plan.segments:
            if base < width:
                height = ceil_to(2 * plan.chunks[at][2], SUB)
                for k in range(plan.group):
                    for c in range(4):
                        rows_ref[base + k * rows:base + (k + 1) * rows, c * levels:(c + 1) * levels] = parts[at][
                            k, c * height + first:c * height + first + rows, :
                        ]
            base += plan.group * rows
        if half == 1:
            height = ceil_to(2 * plan.chunks[-1][2], SUB)
            extra = parts[-1][info_ref[0], 4 * height:4 * height + SUB, :]
            base = info_ref[1] // SUB * SUB
            place = pl.ds(pl.multiple_of(base, SUB), SUB)
            here = lax.broadcasted_iota(jnp.int32, (SUB, levels), 0) == info_ref[1] - base
            for c in range(4):
                cols = slice(c * levels, (c + 1) * levels)
                held = rows_ref[place, cols].astype(F32)
                rows_ref[place, cols] = jnp.where(here, extra[c:c + 1, :].astype(F32), held).astype(BF)

    grid_ref[pl.ds(pl.multiple_of(step * tile, tile), tile), :] = jnp.dot(
        table_ref[...], rows_ref[...], preferred_element_type=F32
    ).astype(BF)

    @pl.when(step == pl.num_programs(0) - 1)
    def _():
        waves = bands_ref.shape[0]
        groups = 4 * levels // level_cols
        piece = 80 if depth % 80 == 0 else depth
        window = ceil_to(piece + SUB - 1, SUB)
        i = lax.broadcasted_iota(jnp.int32, (piece, window), 0)
        j = lax.broadcasted_iota(jnp.int32, (piece, window), 1)
        for w in range(waves):
            start = starts_ref[w]
            base = start // SUB * SUB
            moved = j - i == start - base
            for r in range(0, depth, piece):
                pick = jnp.where(moved & (i < bands_ref[w] - r), 1.0, 0.0).astype(BF)
                held = grid_ref[pl.ds(pl.multiple_of(base + r, SUB), window), :]
                got = jnp.dot(pick, held, preferred_element_type=F32).astype(BF)
                for g in range(groups):
                    out_ref[w * groups + g, r:r + piece, :] = got[:, g * level_cols:(g + 1) * level_cols]


def to_bands(plan, half, info, starts, bands, parts, table, depth, level_cols):
    latitudes, width = table.shape
    levels = parts[0].shape[2]
    columns = 4 * levels
    tile = 512
    smem = pl.BlockSpec(memory_space=pltpu.SMEM)
    messages = bands.shape[0] * columns // level_cols
    return pl.pallas_call(
        functools.partial(grid_kernel, plan, half, levels, latitudes, depth, level_cols),
        grid=(latitudes // tile,),
        out_shape=jax.ShapeDtypeStruct((messages, depth, level_cols), BF),
        in_specs=[smem, smem, smem]
        + [pl.BlockSpec(part.shape, lambda t: (0, 0, 0)) for part in parts]
        + [pl.BlockSpec((tile, width), lambda t: (t, 0))],
        out_specs=pl.BlockSpec((messages, depth, level_cols), lambda t: (0, 0, 0)),
        scratch_shapes=[
            pltpu.VMEM((width, columns), BF),
            pltpu.VMEM((ceil_to(latitudes + depth, SUB) + SUB, columns), BF),
        ],
        compiler_params=pltpu.CompilerParams(vmem_limit_bytes=VMEM_LIMIT),
        cost_estimate=pl.CostEstimate(
            flops=2 * latitudes * width * columns,
            bytes_accessed=2 * latitudes * width + 2 * messages * depth * level_cols,
            transcendentals=0,
        ),
        name="grid_bands",
    )(info, starts, bands, *parts, table)


def per_device(control, covariance, legendre, pair_order, band_rows):
    axes = ("wave", "lev")
    waves, lev_count = lax.axis_size("wave"), lax.axis_size("lev")
    _, slots, columns = control.shape
    degrees, levels = slots - 1, columns // 4
    latitudes = legendre.shape[2]
    depth = 5 * latitudes // (4 * waves)
    level_cols = columns // lev_count
    plan = Plan(waves * lev_count, degrees)
    group, block = plan.group, plan.block
    me = lax.axis_index("wave") * lev_count + lax.axis_index("lev")
    is_high = (me >= group).astype(jnp.int32)
    rank = me - group * is_high
    mine = jnp.where(is_high == 1, group - 1 - rank, rank)
    lowest = pair_order[0]
    halves = [list(range(group)), list(range(group, 2 * group))]

    def exchange(rows):
        return lax.all_to_all(rows, axes, split_axis=0, concat_axis=0, tiled=True, axis_index_groups=halves)

    mirror = [(d, 2 * group - 1 - d) for d in range(2 * group)]
    own, other = [], []
    for _, first, count in plan.chunks:
        start = jnp.where(is_high == 1, block - first - count, first)
        own.append(lax.dynamic_slice_in_dim(covariance, start, count, 0).astype(BF))
        other.append(lax.ppermute(own[-1], axes, mirror))

    def slots_of(message, fold, folded, used):
        message = jnp.where(is_high == 1, group - 1 - message, message)
        degree = message * block + fold
        upper = jnp.where(folded, degree - lowest, degrees - 1 - degree - lowest)
        upper = jnp.where(used & (upper >= 0), upper, -1)
        lower = jnp.where(used & folded & (degree <= lowest), degrees - degree, -1)
        return upper, lower

    upper, lower = slots_of(*plan.message_rows())
    sent = jnp.where(upper >= 0, upper, lower)
    received = exchange(pack(plan, control[0], pair_order, sent[:, None]))

    slot_index = jnp.arange(slots, dtype=jnp.int32)[:, None]
    tables = [
        jnp.einsum(
            "sl,sr->lr", legendre[0], (index[None, :] == slot_index).astype(BF), preferred_element_type=F32
        ).astype(BF)
        for index in (
            index[:width] for index, width in zip(slots_of(*plan.transform_rows()), plan.widths)
        )
    ]

    info = jnp.stack([is_high, mine * block])
    parts, before = [], None
    for at in range(len(plan.chunks)):
        result, *rest = filter_rows(plan, at, info, received, own[at], other[at], before)
        before = rest[0] if rest else None
        parts.append(exchange(result))

    extra_block = lowest // block
    extra_message = jnp.where(is_high == 1, group - 1 - extra_block, extra_block)
    extra_row = plan.extra_row(extra_message, lowest - extra_block * block)
    where = jnp.stack([extra_message, extra_row])
    starts = jnp.cumsum(band_rows) - band_rows
    fourier = [None, None]
    for half in (1, 0):
        outgoing = to_bands(plan, half, where, starts, band_rows, parts, tables[half], depth, level_cols)
        fourier[half] = lax.all_to_all(outgoing, axes, split_axis=0, concat_axis=0, tiled=True)
    return jnp.stack(fourier, axis=1).reshape(-1, depth, level_cols)


def solution(mesh):
    return jax.shard_map(
        per_device,
        mesh=mesh,
        in_specs=(
            P(("wave", "lev"), None, None),
            P(("wave", "lev"), None, None),
            P(("wave", "lev"), None, None),
            P(("wave", "lev")),
            P(),
        ),
        out_specs=P(None, "wave", "lev"),
        check_vma=False,
    )
```

time: 318 us -> 296 us (0.931)
  blocking collectives: 235 us -> 79.5 us
  waiting for transfers between devices: 0.01 us -> 100 us
  starting transfers between devices: 15.9 us -> 43.2 us
    unnamed x1 -> x0, blocking collectives: 83.3 us -> none
    all_to_all x1, blocking collectives: 151 us -> 79.5 us  [per_device(): lax.all_to_all(outgoing, axes, split_axis=0, concat_axis=0, tiled=True)]
    all_to_all x2 -> x4, waiting for transfers between devices: 0.01 us -> 61.5 us  [the longest x1 52.7 us: per_device(): lax.all_to_all(outgoing, axes, split_axis=0, concat_axis=0, tiled=True)]
    ppermute x1 -> x2, waiting for transfers between devices: 0.01 us -> 38.6 us  [per_device(): other.append(lax.ppermute(own[-1], axes, mirror))]
    all_to_all x2 -> x4, starting transfers between devices: 10.3 us -> 37.7 us  [the longest x3 33.6 us: exchange(): lax.all_to_all(rows, axes, split_axis=0, concat_axis=0, tiled=True, axis_...]
    unnamed x13 -> x18, local copies, waits for them, and re-layouts: 4.29 us -> 0.73 us
    another operation x2 -> x1, local copies, waits for them, and re-layouts: 0.01 us -> 3.28 us  [per_device(): return jnp.stack(fourier, axis=1).reshape(-1, depth, level_cols)]
    pallas_call x2 -> x4, Pallas kernels: 23.5 us -> 26.6 us  [the longest x2 18.4 us: to_bands(): pl.pallas_call(functools.partial(grid_kernel, plan, half, levels, latitud...]
  transfers between devices with their start and end apart: 3 -> 6, of which waited for: 0 -> 5; matrix products, arithmetic and copies ran while one was open for 9% -> 10% of each run, Pallas kernels for 0% -> 5%
where the time goes in v2:
time: 296 us; the launch traced here: 295 us
  waiting for transfers between devices  100 us (34%)
  blocking collectives  79.5 us (27%)
  starting transfers between devices  43.2 us (15%)
  Pallas kernels  32.2 us (11%)
  matrix products  27.6 us (9%)
  local copies, waits for them, and re-layouts  6.27 us (2%)
  other arithmetic  5.25 us (2%)
    all_to_all x1, blocking collectives, per_device(): lax.all_to_all(outgoing, axes, split_axis=0, concat_axis=0, tiled=True)  79.5 us
    all_to_all x1, waiting for transfers between devices, per_device(): lax.all_to_all(outgoing, axes, split_axis=0, concat_axis=0, tiled=True)  52.7 us
    ppermute x2, waiting for transfers between devices, per_device(): other.append(lax.ppermute(own[-1], axes, mirror))  38.6 us
    all_to_all x3, starting transfers between devices, exchange(): lax.all_to_all(rows, axes, split_axis=0, concat_axis=0, tiled=True, axis_...  33.6 us
    dot_general x2, matrix products, per_device(): jnp.einsum('sl,sr->lr', legendre[0], (index[None, :] == slot_index).astyp...  27.6 us
    pallas_call x2, Pallas kernels, to_bands(): pl.pallas_call(functools.partial(grid_kernel, plan, half, levels, latitud...  18.4 us
    all_to_all x3, waiting for transfers between devices, exchange(): lax.all_to_all(rows, axes, split_axis=0, concat_axis=0, tiled=True, axis_...  8.78 us
    pallas_call x2, Pallas kernels, filter_rows(): pl.pallas_call(functools.partial(filter_kernel, plan, at, levels), out_sh...  8.18 us
  transfers between devices with their start and end apart: 6, of which 5 were waited for; matrix products, arithmetic and copies ran while one was open for 10% of the time, Pallas kernels for 5%

profile of v2, /device:TPU:0, one launch (start us, length us, event | category | flops | bytes accessed | tf_op | source)
XLA Modules:
  0.0 295.0 jit_solution(14909715375788748208)
XLA Ops:
  0.8 0.7 compare_select_fusion.1
  1.6 1.1 broadcast_in_dim.15.slot_ref
  2.6 5.6 %pack_rows.1 = bf16[16,336,128]{2,1,0:T(8,128)(2,1)} custom-call(s32[1]{0:T(128)} %copy.26.info_ref, s32[1280,1]{1,0:T(8,128)} %broadcast_in_dim.15.slot_ref, bf16[1281,512]{1,0:T(8,128)(2,1)} %bitcast.34), custom_call_target="tpu_custom_call" | custom-call | flops 1679032320 | bytes 2688000 | tf_op jit(solution)/shard_map/pack_rows/pallas_call | solution.py:120
  8.3 6.5 %all-to-all-start = ((bf16[16,336,128]{2,1,0:T(8,128)(2,1)}), bf16[16,336,128]{2,1,0:T(8,128)(2,1)}, u32[]{:S(2)}, u32[]{:S(2)}) async-start(bf16[16,336,128]{2,1,0:T(8,128)(2,1)} %pack_rows.1), calls=%async_computation | async-start | bytes 2752512 | tf_op jit(solution)/shard_map/all_to_all | solution.py:347
  14.8 1.2 dynamic-slice_convert_fusion.own_ref
  15.9 5.5 %collective-permute-start = (bf16[32,128,128]{2,1,0:T(8,128)(2,1)}, bf16[32,128,128]{2,1,0:T(8,128)(2,1)}, u32[]{:S(2)}, u32[]{:S(2)}) collective-permute-start(bf16[32,128,128]{2,1,0:T(8,128)(2,1)} %dynamic-slice_convert_fusion.own_ref), channel_id=1, source_target_pairs={{0,31},{1,30},{2,29},{3,28},{4,27},{5,26},{6,25},{7,24},{8,23},{9,... | collective-permute-start | bytes 3145736 | tf_op jit(solution)/shard_map/ppermute | solution.py:354
  21.5 0.7 pad_add_fusion.1.info_ref
  22.2 38.2 %collective-permute-done.other_ref = bf16[32,128,128]{2,1,0:T(8,128)(2,1)} collective-permute-done((bf16[32,128,128]{2,1,0:T(8,128)(2,1)}, bf16[32,128,128]{2,1,0:T(8,128)(2,1)}, u32[]{:S(2)}, u32[]{:S(2)}) %collective-permute-start) | collective-permute-done | bytes 1048608 | tf_op jit(solution)/shard_map/ppermute | solution.py:354
  60.4 5.1 %filter_rows.2 = (bf16[16,256,128]{2,1,0:T(8,128)(2,1)}, f32[64,128]{1,0:T(8,128)}) custom-call(s32[2]{0:T(128)} %pad_add_fusion.1.info_ref, bf16[16,336,128]{2,1,0:T(8,128)(2,1)} %all-to-all-done.rows_ref, bf16[32,128,128]{2,1,0:T(8,128)(2,1)} %dynamic-slice_convert_fusion.own_ref, bf16[32,128,128]{2,1,0:T(8,128)(2,1)} %collective-permute-done.other_ref), custom_call_target="tpu_custom_call" | custom-call | flops 1073741824 | bytes 4194304 | tf_op jit(solution)/shard_map/filter_rows/pallas_call | solution.py:226
  65.9 0.7 copy-done.3
  66.6 3.1 %filter_rows.3 = bf16[16,80,128]{2,1,0:T(8,128)(2,1)} custom-call(s32[2]{0:T(128)} %pad_add_fusion.1.info_ref, bf16[16,336,128]{2,1,0:T(8,128)(2,1)} %all-to-all-done.rows_ref, bf16[8,128,128]{2,1,0:T(8,128)(2,1)} %copy-done.2, bf16[8,128,128]{2,1,0:T(8,128)(2,1)} %copy-done.3, f32[64,128]{1,0:T(8,128)} %get-tuple-element.8.refs_0_), custom_call_target="tpu_custom_call" | custom-call | flops 268435456 | bytes 1179648 | tf_op jit(solution)/shard_map/filter_rows/pallas_call | solution.py:226
  69.7 22.8 %all-to-all-start.2 = ((bf16[16,80,128]{2,1,0:T(8,128)(2,1)}), bf16[16,80,128]{2,1,0:T(8,128)(2,1)S(1)}, u32[]{:S(2)}, u32[]{:S(2)}) async-start(bf16[16,80,128]{2,1,0:T(8,128)(2,1)} %filter_rows.3), calls=%async_computation.2 | async-start | bytes 655360 | tf_op jit(solution)/shard_map/all_to_all | solution.py:347
  92.7 8.2 %all-to-all-done.2.refs_1_ = bf16[16,80,128]{2,1,0:T(8,128)(2,1)S(1)} async-done(((bf16[16,80,128]{2,1,0:T(8,128)(2,1)}), bf16[16,80,128]{2,1,0:T(8,128)(2,1)S(1)}, u32[]{:S(2)}, u32[]{:S(2)}) %all-to-all-start.2) | async-done | bytes 327712 | tf_op jit(solution)/shard_map/all_to_all | solution.py:347
  100.9 4.3 %all-to-all-start.1 = ((bf16[16,256,128]{2,1,0:T(8,128)(2,1)}), bf16[16,256,128]{2,1,0:T(8,128)(2,1)}, u32[]{:S(2)}, u32[]{:S(2)}) async-start(bf16[16,256,128]{2,1,0:T(8,128)(2,1)} %get-tuple-element.7), calls=%async_computation.1 | async-start | bytes 2097152 | tf_op jit(solution)/shard_map/all_to_all | solution.py:347
  105.8 0.6 pad_add_fusion.info_ref
  106.4 14.5 %fusion.refs_2_ = bf16[2560,1280]{1,0:T(8,128)(2,1)} fusion(bf16[1,1281,2560]{2,1,0:T(8,128)(2,1)} %param.19, s32[1280]{0:T(1024)S(1)} %get-tuple-element.9), kind=kOutput, calls=%fused_computation.1 | convolution fusion | flops 8400077824 | bytes 13117440 | tf_op jit(solution)/shard_map/sl,sr->lr/dot_general | solution.py:370
  121.5 9.9 %grid_bands.2 = bf16[32,400,128]{2,1,0:T(8,128)(2,1)} custom-call(s32[2]{0:T(128)} %pad_add_fusion.info_ref, s32[8]{0:T(128)} %bitcast_subtract_fusion.starts_ref, s32[8]{0:T(128)} %bands_ref.3, bf16[16,256,128]{2,1,0:T(8,128)(2,1)} %all-to-all-done.1.refs_0_, bf16[16,80,128]{2,1,0:T(8,128)(2,1)} %copy-done.1, bf16[2560,1280]{1,0:T(8,128)(2,1)} %fusion.refs_2_), custom_call_target="tpu_custom_call" | custom-call | flops 3355443200 | bytes 9830400 | tf_op jit(solution)/shard_map/grid_bands/pallas_call | solution.py:307
  131.4 4.0 %all-to-all-start.3 = ((bf16[32,400,128]{2,1,0:T(8,128)(2,1)}), bf16[32,400,128]{2,1,0:T(8,128)(2,1)}, u32[]{:S(2)}, u32[]{:S(2)}) async-start(bf16[32,400,128]{2,1,0:T(8,128)(2,1)} %grid_bands.2), calls=%async_computation.3 | async-start | bytes 6553600 | tf_op jit(solution)/shard_map/all_to_all | solution.py:393
  135.4 13.1 %fusion.7.refs_2_ = bf16[2560,768]{1,0:T(8,128)(2,1)} fusion(bf16[1,1281,2560]{2,1,0:T(8,128)(2,1)} %param.19, s32[768]{0:T(1024)S(1)} %subtract_select_fusion), kind=kOutput, calls=%fused_computation.8 | convolution fusion | flops 5040047104 | bytes 10493952 | tf_op jit(solution)/shard_map/sl,sr->lr/dot_general | solution.py:370
  148.5 8.5 %grid_bands.3 = bf16[32,400,128]{2,1,0:T(8,128)(2,1)} custom-call(s32[2]{0:T(128)} %pad_add_fusion.info_ref, s32[8]{0:T(128)} %bitcast_subtract_fusion.starts_ref, s32[8]{0:T(128)} %bands_ref.3, bf16[16,256,128]{2,1,0:T(8,128)(2,1)} %all-to-all-done.1.refs_0_, bf16[16,80,128]{2,1,0:T(8,128)(2,1)} %copy-done.1, bf16[2560,768]{1,0:T(8,128)(2,1)} %fusion.7.refs_2_), custom_call_target="tpu_custom_call" | custom-call | flops 2013265920 | bytes 7208960 | tf_op jit(solution)/shard_map/grid_bands/pallas_call | solution.py:307
  157.0 52.7 %all-to-all-done.3 = bf16[32,400,128]{2,1,0:T(8,128)(2,1)} async-done(((bf16[32,400,128]{2,1,0:T(8,128)(2,1)}), bf16[32,400,128]{2,1,0:T(8,128)(2,1)}, u32[]{:S(2)}, u32[]{:S(2)}) %all-to-all-start.3) | async-done | bytes 3276832 | tf_op jit(solution)/shard_map/all_to_all | solution.py:393
  209.6 79.5 %all_to_all.25 = bf16[32,400,128]{2,1,0:T(8,128)(2,1)S(1)} all-to-all(bf16[32,400,128]{2,1,0:T(8,128)(2,1)} %grid_bands.3), channel_id=1, replica_groups=mesh['wave'=8,'lev'=4] {'wave','lev'}, dimensions={0} | all-to-all | bytes 6553600 | tf_op jit(solution)/shard_map/all_to_all | solution.py:393
  289.2 2.5 pad_maximum_fusion
  291.7 3.3 %copy.23 = bf16[32,2,400,128]{3,2,1,0:T(8,128)(2,1)} copy(bf16[32,2,400,128]{3,2,0,1:T(8,128)(2,1)S(1)} %pad_maximum_fusion) | data formatting | bytes 13107200 | tf_op jit(solution)/shard_map/stack | solution.py:394
  (26 shorter events, 1.8 us)
Async XLA Ops:
  0.0 14.8 %copy-start = (f32[40,128,128]{2,1,0:T(8,128)S(1)}, f32[40,128,128]{2,1,0:T(8,128)}, u32[]{:S(2)}) copy-start(f32[40,128,128]{2,1,0:T(8,128)} %param.18) | copy-start | bytes 7864324
  8.2 84.3 %copy-start.8 = (s32[8]{0:T(128)S(1)}, s32[8]{0:T(128)}, u32[]{:S(2)}) copy-start(s32[8]{0:T(128)} %bands_ref.3) | copy-start | bytes 100
  8.3 84.4 %copy-start.4 = (s32[1280]{0:T(1024)S(1)}, s32[1280]{0:T(1024)}, u32[]{:S(2)}) copy-start(s32[1280]{0:T(1024)} %constant.72.clone) | copy-start | bytes 15364
  8.3 84.4 %copy-start.5 = (s32[1280]{0:T(1024)S(1)}, s32[1280]{0:T(1024)}, u32[]{:S(2)}) copy-start(s32[1280]{0:T(1024)} %constant.73.clone) | copy-start | bytes 15364
  8.3 84.4 %copy-start.6 = (s32[1280]{0:T(1024)S(1)}, s32[1280]{0:T(1024)}, u32[]{:S(2)}) copy-start(s32[1280]{0:T(1024)} %constant.74.clone) | copy-start | bytes 15364
  8.3 84.4 %copy-start.7 = (pred[1280]{0:T(1024)(128)(4,1)S(1)}, pred[1280]{0:T(1024)(128)(4,1)}, u32[]{:S(2)}) copy-start(pred[1280]{0:T(1024)(128)(4,1)} %constant.75.clone) | copy-start | bytes 3844
  8.3 52.1 %all-to-all-start = ((bf16[16,336,128]{2,1,0:T(8,128)(2,1)}), bf16[16,336,128]{2,1,0:T(8,128)(2,1)}, u32[]{:S(2)}, u32[]{:S(2)}) async-start(bf16[16,336,128]{2,1,0:T(8,128)(2,1)} %pack_rows.1), calls=%async_computation | async-start | bytes 2752512 | tf_op jit(solution)/shard_map/all_to_all | solution.py:347
  15.9 44.5 %collective-permute-start = (bf16[32,128,128]{2,1,0:T(8,128)(2,1)}, bf16[32,128,128]{2,1,0:T(8,128)(2,1)}, u32[]{:S(2)}, u32[]{:S(2)}) collective-permute-start(bf16[32,128,128]{2,1,0:T(8,128)(2,1)} %dynamic-slice_convert_fusion.own_ref), channel_id=1, source_target_pairs={{0,31},{1,30},{2,29},{3,28},{4,27},{5,26},{6,25},{7,24},{8,23},{9,... | collective-permute-start | bytes 3145736 | tf_op jit(solution)/shard_map/ppermute | solution.py:354
  21.4 44.5 %copy-start.2 = (bf16[8,128,128]{2,1,0:T(8,128)(2,1)}, bf16[8,128,128]{2,1,0:T(8,128)(2,1)S(1)}, u32[]{:S(2)}) copy-start(bf16[8,128,128]{2,1,0:T(8,128)(2,1)S(1)} %dynamic-slice_convert_fusion.1.own_ref) | copy-start | bytes 786436
  21.4 44.5 %collective-permute-start.1 = (bf16[8,128,128]{2,1,0:T(8,128)(2,1)S(1)}, bf16[8,128,128]{2,1,0:T(8,128)(2,1)S(1)}, u32[]{:S(2)}, u32[]{:S(2)}) collective-permute-start(bf16[8,128,128]{2,1,0:T(8,128)(2,1)S(1)} %dynamic-slice_convert_fusion.1.own_ref), channel_id=1, source_target_pairs={{0,31},{1,30},{2,29},{3,28},{4,27},{5,26},{6,25},{7,24},{8,23},{9,... | collective-permute-start | bytes 786440 | tf_op jit(solution)/shard_map/ppermute | solution.py:354
  65.9 0.7 copy-start.3
  69.7 31.3 %all-to-all-start.2 = ((bf16[16,80,128]{2,1,0:T(8,128)(2,1)}), bf16[16,80,128]{2,1,0:T(8,128)(2,1)S(1)}, u32[]{:S(2)}, u32[]{:S(2)}) async-start(bf16[16,80,128]{2,1,0:T(8,128)(2,1)} %filter_rows.3), calls=%async_computation.2 | async-start | bytes 655360 | tf_op jit(solution)/shard_map/all_to_all | solution.py:347
  100.9 20.0 %copy-start.1 = (bf16[16,80,128]{2,1,0:T(8,128)(2,1)}, bf16[16,80,128]{2,1,0:T(8,128)(2,1)S(1)}, u32[]{:S(2)}) copy-start(bf16[16,80,128]{2,1,0:T(8,128)(2,1)S(1)} %all-to-all-done.2.refs_1_) | copy-start | bytes 983044
  100.9 20.5 %all-to-all-start.1 = ((bf16[16,256,128]{2,1,0:T(8,128)(2,1)}), bf16[16,256,128]{2,1,0:T(8,128)(2,1)}, u32[]{:S(2)}, u32[]{:S(2)}) async-start(bf16[16,256,128]{2,1,0:T(8,128)(2,1)} %get-tuple-element.7), calls=%async_computation.1 | async-start | bytes 2097152 | tf_op jit(solution)/shard_map/all_to_all | solution.py:347
  131.4 78.3 %all-to-all-start.3 = ((bf16[32,400,128]{2,1,0:T(8,128)(2,1)}), bf16[32,400,128]{2,1,0:T(8,128)(2,1)}, u32[]{:S(2)}, u32[]{:S(2)}) async-start(bf16[32,400,128]{2,1,0:T(8,128)(2,1)} %grid_bands.2), calls=%async_computation.3 | async-start | bytes 6553600 | tf_op jit(solution)/shard_map/all_to_all | solution.py:393

commit v3 on v2

--- a/solution.py
+++ b/solution.py
@@ -242,88 +242,92 @@
     )(*operands)
 
 
-def grid_kernel(plan, half, levels, latitudes, depth, level_cols, info_ref, starts_ref, bands_ref, *refs):
+def grid_kernel(plan, levels, latitudes, depth, level_cols, info_ref, starts_ref, bands_ref, *refs):
     count = len(plan.chunks)
     parts = refs[:count]
-    table_ref, out_ref, rows_ref, grid_ref = refs[count:]
-    step = pl.program_id(0)
-    tile, width = table_ref.shape
-
-    @pl.when(step == 0)
+    tables, (out_ref, rows_ref, grid_ref) = refs[count:count + 2], refs[count + 2:]
+    half, step = pl.program_id(0), pl.program_id(1)
+    tile = tables[0].shape[0]
+
+    @pl.when((half == 0) & (step == 0))
     def _():
-        grid_ref[latitudes:, :] = jnp.zeros((grid_ref.shape[0] - latitudes, 4 * levels), BF)
         base = 0
         for at, first, rows in plan.segments:
-            if base < width:
-                height = ceil_to(2 * plan.chunks[at][2], SUB)
-                for k in range(plan.group):
-                    for c in range(4):
-                        rows_ref[base + k * rows:base + (k + 1) * rows, c * levels:(c + 1) * levels] = parts[at][
-                            k, c * height + first:c * height + first + rows, :
-                        ]
+            height = ceil_to(2 * plan.chunks[at][2], SUB)
+            for k in range(plan.group):
+                for c in range(4):
+                    rows_ref[base + k * rows:base + (k + 1) * rows, c * levels:(c + 1) * levels] = parts[at][
+                        k, c * height + first:c * height + first + rows, :
+                    ]
             base += plan.group * rows
-        if half == 1:
-            height = ceil_to(2 * plan.chunks[-1][2], SUB)
-            extra = parts[-1][info_ref[0], 4 * height:4 * height + SUB, :]
-            base = info_ref[1] // SUB * SUB
-            place = pl.ds(pl.multiple_of(base, SUB), SUB)
-            here = lax.broadcasted_iota(jnp.int32, (SUB, levels), 0) == info_ref[1] - base
-            for c in range(4):
-                cols = slice(c * levels, (c + 1) * levels)
-                held = rows_ref[place, cols].astype(F32)
-                rows_ref[place, cols] = jnp.where(here, extra[c:c + 1, :].astype(F32), held).astype(BF)
-
-    grid_ref[pl.ds(pl.multiple_of(step * tile, tile), tile), :] = jnp.dot(
-        table_ref[...], rows_ref[...], preferred_element_type=F32
-    ).astype(BF)
-
-    @pl.when(step == pl.num_programs(0) - 1)
+
+    @pl.when((half == 1) & (step == 0))
+    def _():
+        height = ceil_to(2 * plan.chunks[-1][2], SUB)
+        extra = parts[-1][info_ref[0], 4 * height:4 * height + SUB, :]
+        base = info_ref[1] // SUB * SUB
+        place = pl.ds(pl.multiple_of(base, SUB), SUB)
+        here = lax.broadcasted_iota(jnp.int32, (SUB, levels), 0) == info_ref[1] - base
+        for c in range(4):
+            cols = slice(c * levels, (c + 1) * levels)
+            held = rows_ref[place, cols].astype(F32)
+            rows_ref[place, cols] = jnp.where(here, extra[c:c + 1, :].astype(F32), held).astype(BF)
+
+    for at in range(2):
+        @pl.when(half == at)
+        def _():
+            grid_ref[pl.ds(pl.multiple_of(step * tile, tile), tile), :] = jnp.dot(
+                tables[at][...], rows_ref[:plan.widths[at], :], preferred_element_type=F32
+            )
+
+    @pl.when(step == pl.num_programs(1) - 1)
     def _():
         waves = bands_ref.shape[0]
         groups = 4 * levels // level_cols
         piece = 80 if depth % 80 == 0 else depth
-        window = ceil_to(piece + SUB - 1, SUB)
-        i = lax.broadcasted_iota(jnp.int32, (piece, window), 0)
-        j = lax.broadcasted_iota(jnp.int32, (piece, window), 1)
+        i = lax.broadcasted_iota(jnp.int32, (piece, 4 * levels), 0)
         for w in range(waves):
             start = starts_ref[w]
-            base = start // SUB * SUB
-            moved = j - i == start - base
+            base = start // 8 * 8
             for r in range(0, depth, piece):
-                pick = jnp.where(moved & (i < bands_ref[w] - r), 1.0, 0.0).astype(BF)
-                held = grid_ref[pl.ds(pl.multiple_of(base + r, SUB), window), :]
-                got = jnp.dot(pick, held, preferred_element_type=F32).astype(BF)
+                held = grid_ref[pl.ds(pl.multiple_of(base + r, 8), piece + 8), :]
+                held = pltpu.roll(held, (piece + 8 - (start - base)) % (piece + 8), axis=0)[:piece]
+                got = jnp.where(i < bands_ref[w] - r, held, 0.0).astype(BF)
                 for g in range(groups):
-                    out_ref[w * groups + g, r:r + piece, :] = got[:, g * level_cols:(g + 1) * level_cols]
-
-
-def to_bands(plan, half, info, starts, bands, parts, table, depth, level_cols):
-    latitudes, width = table.shape
+                    out_ref[w * groups + g, 0, r:r + piece, :] = got[:, g * level_cols:(g + 1) * level_cols]
+
+
+def to_bands(plan, info, starts, bands, parts, tables, depth, level_cols):
+    latitudes = tables[0].shape[0]
     levels = parts[0].shape[2]
     columns = 4 * levels
     tile = 512
+    steps = latitudes // tile
     smem = pl.BlockSpec(memory_space=pltpu.SMEM)
     messages = bands.shape[0] * columns // level_cols
     return pl.pallas_call(
-        functools.partial(grid_kernel, plan, half, levels, latitudes, depth, level_cols),
-        grid=(latitudes // tile,),
-        out_shape=jax.ShapeDtypeStruct((messages, depth, level_cols), BF),
+        functools.partial(grid_kernel, plan, levels, latitudes, depth, level_cols),
+        grid=(2, steps),
+        out_shape=jax.ShapeDtypeStruct((messages, 2, depth, level_cols), BF),
         in_specs=[smem, smem, smem]
-        + [pl.BlockSpec(part.shape, lambda t: (0, 0, 0)) for part in parts]
-        + [pl.BlockSpec((tile, width), lambda t: (t, 0))],
-        out_specs=pl.BlockSpec((messages, depth, level_cols), lambda t: (0, 0, 0)),
+        + [pl.BlockSpec(part.shape, lambda h, t: (0, 0, 0)) for part in parts]
+        + [
+            pl.BlockSpec((tile, plan.widths[0]), lambda h, t: (jnp.where(h == 0, t, steps - 1), 0)),
+            pl.BlockSpec((tile, plan.widths[1]), lambda h, t: (jnp.where(h == 0, 0, t), 0)),
+        ],
+        out_specs=pl.BlockSpec((messages, 1, depth, level_cols), lambda h, t: (0, h, 0, 0)),
         scratch_shapes=[
-            pltpu.VMEM((width, columns), BF),
-            pltpu.VMEM((ceil_to(latitudes + depth, SUB) + SUB, columns), BF),
+            pltpu.VMEM((plan.widths[0], columns), BF),
+            pltpu.VMEM((ceil_to(latitudes + depth, 8) + 8, columns), F32),
         ],
         compiler_params=pltpu.CompilerParams(vmem_limit_bytes=VMEM_LIMIT),
         cost_estimate=pl.CostEstimate(
-            flops=2 * latitudes * width * columns,
-            bytes_accessed=2 * latitudes * width + 2 * messages * depth * level_cols,
+            flops=2 * latitudes * sum(plan.widths) * columns,
+            bytes_accessed=2 * latitudes * sum(plan.widths) + 4 * messages * depth * level_cols,
             transcendentals=0,
         ),
         name="grid_bands",
-    )(info, starts, bands, *parts, table)
+    )(info, starts, bands, *parts, *tables)
 
 
 def per_device(control, covariance, legendre, pair_order, band_rows):
@@ -350,7 +354,12 @@
     own, other = [], []
     for _, first, count in plan.chunks:
         start = jnp.where(is_high == 1, block - first - count, first)
-        own.append(lax.dynamic_slice_in_dim(covariance, start, count, 0).astype(BF))
+        block_rows = lax.dynamic_slice_in_dim(covariance, start, count, 0).astype(BF)
+        if other:
+            block_rows, other[-1] = lax.optimization_barrier((block_rows, other[-1]))
+        else:
+            block_rows, control = lax.optimization_barrier((block_rows, control))
+        own.append(block_rows)
         other.append(lax.ppermute(own[-1], axes, mirror))
 
     def slots_of(message, fold, folded, used):
@@ -376,6 +385,7 @@
     ]
 
     info = jnp.stack([is_high, mine * block])
+    received, tables = lax.optimization_barrier((received, tables))
     parts, before = [], None
     for at in range(len(plan.chunks)):
         result, *rest = filter_rows(plan, at, info, received, own[at], other[at], before)
@@ -387,11 +397,9 @@
     extra_row = plan.extra_row(extra_message, lowest - extra_block * block)
     where = jnp.stack([extra_message, extra_row])
     starts = jnp.cumsum(band_rows) - band_rows
-    fourier = [None, None]
-    for half in (1, 0):
-        outgoing = to_bands(plan, half, where, starts, band_rows, parts, tables[half], depth, level_cols)
-        fourier[half] = lax.all_to_all(outgoing, axes, split_axis=0, concat_axis=0, tiled=True)
-    return jnp.stack(fourier, axis=1).reshape(-1, depth, level_cols)
+    outgoing = to_bands(plan, where, starts, band_rows, parts, tables, depth, level_cols)
+    outgoing = outgoing.reshape(-1, depth, level_cols)
+    return lax.all_to_all(outgoing, axes, split_axis=0, concat_axis=0, tiled=True)
 
 
 def solution(mesh):

time: 296 us -> 309 us (1.044)
  blocking collectives: 79.5 us -> 179 us
  waiting for transfers between devices: 100 us -> 41.5 us
  starting transfers between devices: 43.2 us -> 18.5 us
    all_to_all x1, blocking collectives: 79.5 us -> 148 us  [per_device(): lax.all_to_all(outgoing, axes, split_axis=0, concat_axis=0, tiled=True)]
    all_to_all x1 -> x0, waiting for transfers between devices: 52.7 us -> none  [per_device(): lax.all_to_all(outgoing, axes, split_axis=0, concat_axis=0, tiled=True)]
    all_to_all x0 -> x1, blocking collectives: none -> 30.5 us  [exchange(): lax.all_to_all(rows, axes, split_axis=0, concat_axis=0, tiled=True, axis_...]
    all_to_all x3 -> x2, starting transfers between devices: 33.6 us -> 10.9 us  [exchange(): lax.all_to_all(rows, axes, split_axis=0, concat_axis=0, tiled=True, axis_...]
    ppermute x2, waiting for transfers between devices: 38.6 us -> 26.9 us  [per_device(): other.append(lax.ppermute(own[-1], axes, mirror))]
    all_to_all x3 -> x2, waiting for transfers between devices: 8.78 us -> 14.5 us  [exchange(): lax.all_to_all(rows, axes, split_axis=0, concat_axis=0, tiled=True, axis_...]
    all_to_all x1 -> x0, starting transfers between devices: 4.02 us -> none  [per_device(): lax.all_to_all(outgoing, axes, split_axis=0, concat_axis=0, tiled=True)]
    another operation x1 -> x0, local copies, waits for them, and re-layouts: 3.28 us -> none  [per_device(): return jnp.stack(fourier, axis=1).reshape(-1, depth, level_cols)]
  transfers between devices with their start and end apart: 6 -> 4, of which waited for: 5 -> 2; matrix products, arithmetic and copies ran while one was open for 10% -> 10% of each run, Pallas kernels for 5% -> 2%
where the time goes in v3:
time: 309 us; the launch traced here: 308 us
  blocking collectives  179 us (58%)
  waiting for transfers between devices  41.5 us (13%)
  Pallas kernels  31.9 us (10%)
  matrix products  27.7 us (9%)
  starting transfers between devices  18.5 us (6%)
  local copies, waits for them, and re-layouts  5.74 us (2%)
    all_to_all x1, blocking collectives, per_device(): lax.all_to_all(outgoing, axes, split_axis=0, concat_axis=0, tiled=True)  148 us
    all_to_all x1, blocking collectives, exchange(): lax.all_to_all(rows, axes, split_axis=0, concat_axis=0, tiled=True, axis_...  30.5 us
    dot_general x2, matrix products, per_device(): jnp.einsum('sl,sr->lr', legendre[0], (index[None, :] == slot_index).astyp...  27.7 us
    ppermute x2, waiting for transfers between devices, per_device(): other.append(lax.ppermute(own[-1], axes, mirror))  26.9 us
    pallas_call x1, Pallas kernels, to_bands(): pl.pallas_call(functools.partial(grid_kernel, plan, levels, latitudes, de...  18.1 us
    all_to_all x2, waiting for transfers between devices, exchange(): lax.all_to_all(rows, axes, split_axis=0, concat_axis=0, tiled=True, axis_...  14.5 us
    all_to_all x2, starting transfers between devices, exchange(): lax.all_to_all(rows, axes, split_axis=0, concat_axis=0, tiled=True, axis_...  10.9 us
    pallas_call x2, Pallas kernels, filter_rows(): pl.pallas_call(functools.partial(filter_kernel, plan, at, levels), out_sh...  8.18 us
  transfers between devices with their start and end apart: 4, of which 2 were waited for; matrix products, arithmetic and copies ran while one was open for 10% of the time, Pallas kernels for 2%

profile of v3, /device:TPU:0, one launch (start us, length us, event | category | flops | bytes accessed | tf_op | source)
XLA Modules:
  0.0 308.1 jit_solution(4973645124193609254)
XLA Ops:
  0.8 0.8 multiply_add_fusion
  1.6 1.1 broadcast_in_dim.15.slot_ref
  2.7 1.1 dynamic-slice_convert_fusion.own_ref
  3.8 5.6 %pack_rows.1 = bf16[16,336,128]{2,1,0:T(8,128)(2,1)} custom-call(s32[1]{0:T(128)} %copy.26.info_ref, s32[1280,1]{1,0:T(8,128)} %broadcast_in_dim.15.slot_ref, bf16[1281,512]{1,0:T(8,128)(2,1)} %bitcast.30), custom_call_target="tpu_custom_call" | custom-call | flops 1679032320 | bytes 2688000 | tf_op jit(solution)/shard_map/pack_rows/pallas_call | solution.py:120
  9.4 6.3 %all-to-all-start = ((bf16[16,336,128]{2,1,0:T(8,128)(2,1)}), bf16[16,336,128]{2,1,0:T(8,128)(2,1)}, u32[]{:S(2)}, u32[]{:S(2)}) async-start(bf16[16,336,128]{2,1,0:T(8,128)(2,1)} %pack_rows.1), calls=%async_computation | async-start | bytes 2752512 | tf_op jit(solution)/shard_map/all_to_all | solution.py:351
  15.8 5.5 %collective-permute-start = (bf16[32,128,128]{2,1,0:T(8,128)(2,1)}, bf16[32,128,128]{2,1,0:T(8,128)(2,1)}, u32[]{:S(2)}, u32[]{:S(2)}) collective-permute-start(bf16[32,128,128]{2,1,0:T(8,128)(2,1)} %dynamic-slice_convert_fusion.own_ref), channel_id=1, source_target_pairs={{0,31},{1,30},{2,29},{3,28},{4,27},{5,26},{6,25},{7,24},{8,23},{9,... | collective-permute-start | bytes 3145736 | tf_op jit(solution)/shard_map/ppermute | solution.py:363
  21.3 13.2 %fusion.7.refs_3_ = bf16[2560,768]{1,0:T(8,128)(2,1)} fusion(bf16[1,1281,2560]{2,1,0:T(8,128)(2,1)} %param.19, s32[768]{0:T(1024)S(1)} %subtract_select_fusion), kind=kOutput, calls=%fused_computation.7 | convolution fusion | flops 5040047104 | bytes 10493952 | tf_op jit(solution)/shard_map/sl,sr->lr/dot_general | solution.py:379
  34.5 26.9 %collective-permute-done.other_ref = bf16[32,128,128]{2,1,0:T(8,128)(2,1)} collective-permute-done((bf16[32,128,128]{2,1,0:T(8,128)(2,1)}, bf16[32,128,128]{2,1,0:T(8,128)(2,1)}, u32[]{:S(2)}, u32[]{:S(2)}) %collective-permute-start) | collective-permute-done | bytes 1048608 | tf_op jit(solution)/shard_map/ppermute | solution.py:363
  61.5 2.2 collective-permute-start.1
  63.7 14.5 %fusion.refs_2_ = bf16[2560,1280]{1,0:T(8,128)(2,1)} fusion(bf16[1,1281,2560]{2,1,0:T(8,128)(2,1)} %param.19, s32[1280]{0:T(1024)S(1)} %get-tuple-element.24), kind=kOutput, calls=%fused_computation.1 | convolution fusion | flops 8400077824 | bytes 13117440 | tf_op jit(solution)/shard_map/sl,sr->lr/dot_general | solution.py:379
  78.2 0.7 pad_add_fusion.1.info_ref
  78.8 0.0 all-to-all-done.rows_ref
  78.8 5.1 %filter_rows.2 = (bf16[16,256,128]{2,1,0:T(8,128)(2,1)}, f32[64,128]{1,0:T(8,128)}) custom-call(s32[2]{0:T(128)} %pad_add_fusion.1.info_ref, bf16[16,336,128]{2,1,0:T(8,128)(2,1)} %all-to-all-done.rows_ref, bf16[32,128,128]{2,1,0:T(8,128)(2,1)} %dynamic-slice_convert_fusion.own_ref, bf16[32,128,128]{2,1,0:T(8,128)(2,1)} %collective-permute-done.other_ref), custom_call_target="tpu_custom_call" | custom-call | flops 1073741824 | bytes 4194304 | tf_op jit(solution)/shard_map/filter_rows/pallas_call | solution.py:226
  83.9 0.7 copy-done.2
  84.6 3.1 %filter_rows.3 = bf16[16,80,128]{2,1,0:T(8,128)(2,1)} custom-call(s32[2]{0:T(128)} %pad_add_fusion.1.info_ref, bf16[16,336,128]{2,1,0:T(8,128)(2,1)} %all-to-all-done.rows_ref, bf16[8,128,128]{2,1,0:T(8,128)(2,1)} %copy-done.1, bf16[8,128,128]{2,1,0:T(8,128)(2,1)} %copy-done.2, f32[64,128]{1,0:T(8,128)} %get-tuple-element.20.refs_0_), custom_call_target="tpu_custom_call" | custom-call | flops 268435456 | bytes 1179648 | tf_op jit(solution)/shard_map/filter_rows/pallas_call | solution.py:226
  87.7 30.5 %all_to_all.20.refs_1_ = bf16[16,80,128]{2,1,0:T(8,128)(2,1)} all-to-all(bf16[16,80,128]{2,1,0:T(8,128)(2,1)} %filter_rows.3), channel_id=1, replica_groups={{0,1,2,3,4,5,6,7,8,9,10,11,12,13,14,15},{16,17,18,19,20,21,22,23,24,25,..., dimensions={0} | all-to-all | bytes 655360 | tf_op jit(solution)/shard_map/all_to_all | solution.py:351
  118.2 4.5 %all-to-all-start.1 = ((bf16[16,256,128]{2,1,0:T(8,128)(2,1)}), bf16[16,256,128]{2,1,0:T(8,128)(2,1)}, u32[]{:S(2)}, u32[]{:S(2)}) async-start(bf16[16,256,128]{2,1,0:T(8,128)(2,1)} %get-tuple-element.18), calls=%async_computation.1 | async-start | bytes 2097152 | tf_op jit(solution)/shard_map/all_to_all | solution.py:351
  122.8 0.2 reduce-window.9
  123.0 0.6 pad_add_fusion.info_ref
  123.6 0.6 bitcast_subtract_fusion.starts_ref
  124.2 14.5 %all-to-all-done.1.refs_0_ = bf16[16,256,128]{2,1,0:T(8,128)(2,1)} async-done(((bf16[16,256,128]{2,1,0:T(8,128)(2,1)}), bf16[16,256,128]{2,1,0:T(8,128)(2,1)}, u32[]{:S(2)}, u32[]{:S(2)}) %all-to-all-start.1) | async-done | bytes 1048608 | tf_op jit(solution)/shard_map/all_to_all | solution.py:351
  138.7 18.1 %grid_bands.1 = bf16[32,2,400,128]{3,2,1,0:T(8,128)(2,1)} custom-call(s32[2]{0:T(128)} %pad_add_fusion.info_ref, s32[8]{0:T(128)} %bitcast_subtract_fusion.starts_ref, s32[8]{0:T(128)} %bands_ref.1, bf16[16,256,128]{2,1,0:T(8,128)(2,1)} %all-to-all-done.1.refs_0_, bf16[16,80,128]{2,1,0:T(8,128)(2,1)} %all_to_all.20.refs_1_, bf16[2560,1280]{1,0:T(8,128)(2,1)} %fusion.refs_2_, ...), custom_call_target="tpu_custom_call" | custom-call | flops 5368709120 | bytes 17039360 | tf_op jit(solution)/shard_map/grid_bands/pallas_call | solution.py:308
  156.8 148.5 %all_to_all.21 = bf16[64,400,128]{2,1,0:T(8,128)(2,1)S(1)} all-to-all(bf16[64,400,128]{2,1,0:T(8,128)(2,1)} %bitcast.29), channel_id=1, replica_groups=mesh['wave'=8,'lev'=4] {'wave','lev'}, dimensions={0} | all-to-all | bytes 13107200 | tf_op jit(solution)/shard_map/all_to_all | solution.py:402
  305.3 2.8 copy.27
  (12 shorter events, 0.1 us)
Async XLA Ops:
  0.0 2.7 copy-start
  0.0 21.2 %copy-start.3 = (pred[1280]{0:T(1024)(128)(4,1)S(1)}, pred[1280]{0:T(1024)(128)(4,1)}, u32[]{:S(2)}) copy-start(pred[1280]{0:T(1024)(128)(4,1)} %constant.75.clone) | copy-start | bytes 3844
  9.4 69.4 %all-to-all-start = ((bf16[16,336,128]{2,1,0:T(8,128)(2,1)}), bf16[16,336,128]{2,1,0:T(8,128)(2,1)}, u32[]{:S(2)}, u32[]{:S(2)}) async-start(bf16[16,336,128]{2,1,0:T(8,128)(2,1)} %pack_rows.1), calls=%async_computation | async-start | bytes 2752512 | tf_op jit(solution)/shard_map/all_to_all | solution.py:351
  15.8 45.7 %collective-permute-start = (bf16[32,128,128]{2,1,0:T(8,128)(2,1)}, bf16[32,128,128]{2,1,0:T(8,128)(2,1)}, u32[]{:S(2)}, u32[]{:S(2)}) collective-permute-start(bf16[32,128,128]{2,1,0:T(8,128)(2,1)} %dynamic-slice_convert_fusion.own_ref), channel_id=1, source_target_pairs={{0,31},{1,30},{2,29},{3,28},{4,27},{5,26},{6,25},{7,24},{8,23},{9,... | collective-permute-start | bytes 3145736 | tf_op jit(solution)/shard_map/ppermute | solution.py:363
  34.5 43.6 %copy-start.1 = (bf16[8,128,128]{2,1,0:T(8,128)(2,1)}, bf16[8,128,128]{2,1,0:T(8,128)(2,1)S(1)}, u32[]{:S(2)}) copy-start(bf16[8,128,128]{2,1,0:T(8,128)(2,1)S(1)} %dynamic-slice_convert_fusion.1.own_ref) | copy-start | bytes 786436
  61.5 22.5 %collective-permute-start.1 = (bf16[8,128,128]{2,1,0:T(8,128)(2,1)S(1)}, bf16[8,128,128]{2,1,0:T(8,128)(2,1)S(1)}, u32[]{:S(2)}, u32[]{:S(2)}) collective-permute-start(bf16[8,128,128]{2,1,0:T(8,128)(2,1)S(1)} %dynamic-slice_convert_fusion.1.own_ref), channel_id=1, source_target_pairs={{0,31},{1,30},{2,29},{3,28},{4,27},{5,26},{6,25},{7,24},{8,23},{9,... | collective-permute-start | bytes 786440 | tf_op jit(solution)/shard_map/ppermute | solution.py:363
  78.2 44.6 %copy-start.4 = (s32[8]{0:T(128)S(1)}, s32[8]{0:T(128)}, u32[]{:S(2)}) copy-start(s32[8]{0:T(128)} %bands_ref.1) | copy-start | bytes 100
  83.9 0.7 copy-start.2
  118.2 20.5 %all-to-all-start.1 = ((bf16[16,256,128]{2,1,0:T(8,128)(2,1)}), bf16[16,256,128]{2,1,0:T(8,128)(2,1)}, u32[]{:S(2)}, u32[]{:S(2)}) async-start(bf16[16,256,128]{2,1,0:T(8,128)(2,1)} %get-tuple-element.18), calls=%async_computation.1 | async-start | bytes 2097152 | tf_op jit(solution)/shard_map/all_to_all | solution.py:351

commit v4 on v3

--- a/solution.py
+++ b/solution.py
@@ -10,7 +10,6 @@
 
 BF = jnp.bfloat16
 F32 = jnp.float32
-VMEM_LIMIT = 56 * 1024 * 1024
 SUB = 16
 DIGIT = 16
 
@@ -127,14 +126,50 @@
             pl.BlockSpec((slots, columns), lambda k: (0, 0)),
         ],
         out_specs=pl.BlockSpec((per_step, height, levels), lambda k: (k, 0, 0)),
-        compiler_params=pltpu.CompilerParams(vmem_limit_bytes=VMEM_LIMIT),
-        cost_estimate=pl.CostEstimate(
-            flops=2 * plan.group * plan.rows * slots * columns,
-            bytes_accessed=slots * columns * 2 + plan.group * height * levels * 2,
-            transcendentals=0,
-        ),
+        compiler_params=pltpu.CompilerParams(vmem_limit_bytes=16 * 1024 * 1024),
+        cost_estimate=pl.CostEstimate(flops=1, bytes_accessed=1, transcendentals=0),
         name="pack_rows",
     )(lowest, slots_of_rows, control)
+
+
+def table_kernel(plan, upper_ref, lower_ref, legendre_ref, *refs):
+    outs, picks = refs[:2], refs[2:]
+    slots = legendre_ref.shape[0]
+    even = slots - 1
+
+    @pl.when(pl.program_id(0) == 0)
+    def _():
+        for index_ref, pick_ref in zip((upper_ref, lower_ref), picks):
+            slot = lax.broadcasted_iota(jnp.int32, pick_ref.shape, 0)
+            pick_ref[...] = jnp.where(slot == index_ref[...], 1.0, 0.0).astype(BF)
+
+    def times(rows, picked):
+        return lax.dot_general(rows, picked, (((0,), (0,)), ((), ())), preferred_element_type=F32)
+
+    for out_ref, pick_ref in zip(outs, picks):
+        got = times(legendre_ref[:even, :], pick_ref[:even, :])
+        last = jnp.concatenate(
+            [legendre_ref[even:slots, :].astype(F32), jnp.zeros((SUB - 1, legendre_ref.shape[1]), F32)], axis=0
+        ).astype(BF)
+        out_ref[...] = (got + times(last, pick_ref[even:even + SUB, :])).astype(BF)
+
+
+def make_tables(plan, legendre, slots_of_rows):
+    slots, latitudes = legendre.shape
+    tile = 256
+    index = [rows[None, :width] for rows, width in zip(slots_of_rows, plan.widths)]
+    return pl.pallas_call(
+        functools.partial(table_kernel, plan),
+        grid=(latitudes // tile,),
+        out_shape=[jax.ShapeDtypeStruct((latitudes, width), BF) for width in plan.widths],
+        in_specs=[pl.BlockSpec((1, width), lambda t: (0, 0)) for width in plan.widths]
+        + [pl.BlockSpec((slots, tile), lambda t: (0, t))],
+        out_specs=[pl.BlockSpec((tile, width), lambda t: (t, 0)) for width in plan.widths],
+        scratch_shapes=[pltpu.VMEM((slots - 1 + SUB, width), BF) for width in plan.widths],
+        compiler_params=pltpu.CompilerParams(vmem_limit_bytes=32 * 1024 * 1024),
+        cost_estimate=pl.CostEstimate(flops=1, bytes_accessed=1, transcendentals=0),
+        name="make_tables",
+    )(*index, legendre)
 
 
 def swap_matrix():
@@ -143,21 +178,19 @@
     return jnp.where((i // SUB == j % SUB) & (i % SUB == j // SUB), 1.0, 0.0).astype(BF)
 
 
-def filter_kernel(plan, at, levels, info_ref, rows_ref, own_ref, other_ref, *refs):
-    row0, fold0, count = plan.chunks[at]
-    last = at == len(plan.chunks) - 1
-    before_ref = None if at == 0 else refs[0]
-    out_ref, *carry, x_ref, y_ref = refs[0 if at == 0 else 1:]
-    height = ceil_to(2 * count, SUB)
+def filter_kernel(plan, levels, pieces, info_ref, rows_ref, *refs):
+    own_refs, other_refs, (out_ref, x_ref, y_ref) = refs[:pieces], refs[pieces:2 * pieces], refs[2 * pieces:]
+    each = plan.block // pieces
     is_high = info_ref[0] == 1
-    first_fold = (info_ref[1] + fold0).astype(F32)
+    first_fold = info_ref[1].astype(F32)
     swap = swap_matrix()
 
-    def low_matrix(i):
-        return jnp.where(is_high, other_ref[i], own_ref[i])
-
-    def high_matrix(i):
-        return jnp.where(is_high, own_ref[count - 1 - i], other_ref[count - 1 - i])
+    def low_matrix(fold):
+        return jnp.where(is_high, other_refs[fold // each][fold % each], own_refs[fold // each][fold % each])
+
+    def high_matrix(fold):
+        at, place = fold // each, each - 1 - fold % each
+        return jnp.where(is_high, own_refs[at][place], other_refs[at][place])
 
     def times(rows, matrix):
         return lax.dot_general(rows, matrix, (((1,), (1,)), ((), ())), preferred_element_type=F32)
@@ -167,85 +200,74 @@
 
     for g in range(plan.group // SUB):
         sources = slice(g * SUB, (g + 1) * SUB)
-        for r in range(0, height, SUB):
+        for r in range(0, plan.rows, SUB):
             parts = []
             for c in range(4):
-                start = c * plan.rows + row0 + r
+                start = c * plan.rows + r
                 parts.append(rows_ref[sources, start:start + SUB, :].reshape(SUB * SUB, levels))
             x_ref[r * SUB:(r + SUB) * SUB, :] = turn(jnp.concatenate(parts, axis=1)).astype(BF)
         tail = turn(rows_ref[sources, 4 * plan.rows:4 * plan.rows + SUB, :].reshape(SUB * SUB, levels))
         extra = tail[:4 * SUB].astype(BF)
         low = tail[4 * SUB:5 * SUB] * DIGIT + tail[5 * SUB:6 * SUB]
         low = jnp.concatenate([low] * 4, axis=0)
-        if at == 0:
-            kept = jnp.zeros((4 * SUB, levels), F32)
-        else:
-            kept = before_ref[4 * SUB * g:4 * SUB * (g + 1), :]
-        for i in range(count):
-            def stack(row):
-                return jnp.concatenate(
-                    [x_ref[row * SUB:(row + 1) * SUB, c * levels:(c + 1) * levels] for c in range(4)], axis=0
-                )
-
-            folded, high = stack(i), stack(count + i)
-            from_low = times(folded, low_matrix(i))
-            from_high = times(jnp.concatenate([folded, high, extra], axis=0), high_matrix(i))
-            mixed = jnp.where(low <= first_fold + i, from_low, from_high[:4 * SUB])
-            kept = jnp.where(low == first_fold + i, from_high[8 * SUB:], kept)
-            for row, value in ((i, mixed), (count + i, from_high[4 * SUB:8 * SUB])):
-                value = value.astype(BF)
-                for c in range(4):
-                    y_ref[row * SUB:(row + 1) * SUB, c * levels:(c + 1) * levels] = value[c * SUB:(c + 1) * SUB]
-        if height > 2 * count:
-            y_ref[2 * count * SUB:height * SUB, :] = jnp.zeros(((height - 2 * count) * SUB, 4 * levels), BF)
-        for r in range(0, height, SUB):
+        kept = jnp.zeros((4 * SUB, levels), F32)
+        for row0, fold0, count in plan.chunks:
+            for i in range(count):
+                def stack(row):
+                    return jnp.concatenate(
+                        [x_ref[row * SUB:(row + 1) * SUB, c * levels:(c + 1) * levels] for c in range(4)], axis=0
+                    )
+
+                folded, high = stack(row0 + i), stack(row0 + count + i)
+                from_low = times(folded, low_matrix(fold0 + i))
+                from_high = times(jnp.concatenate([folded, high, extra], axis=0), high_matrix(fold0 + i))
+                fold = first_fold + (fold0 + i)
+                mixed = jnp.where(low <= fold, from_low, from_high[:4 * SUB])
+                kept = jnp.where(low == fold, from_high[8 * SUB:], kept)
+                for row, value in ((row0 + i, mixed), (row0 + count + i, from_high[4 * SUB:8 * SUB])):
+                    value = value.astype(BF)
+                    for c in range(4):
+                        y_ref[row * SUB:(row + 1) * SUB, c * levels:(c + 1) * levels] = value[c * SUB:(c + 1) * SUB]
+            unused = ceil_to(2 * count, SUB) - 2 * count
+            if unused:
+                start = (row0 + 2 * count) * SUB
+                y_ref[start:start + unused * SUB, :] = jnp.zeros((unused * SUB, 4 * levels), BF)
+        for r in range(0, plan.rows, SUB):
             back = turn(y_ref[r * SUB:(r + SUB) * SUB, :]).astype(BF)
             for c in range(4):
-                out_ref[sources, c * height + r:c * height + r + SUB, :] = back[
-                    :, c * levels:(c + 1) * levels
-                ].reshape(SUB, SUB, levels)
-        if last:
-            filled = jnp.concatenate([kept, jnp.zeros((12 * SUB, levels), F32)], axis=0).astype(BF)
-            out_ref[sources, 4 * height:4 * height + SUB, :] = turn(filled).astype(BF).reshape(SUB, SUB, levels)
-        else:
-            carry[0][4 * SUB * g:4 * SUB * (g + 1), :] = kept
-
-
-def filter_rows(plan, at, info, received, own, other, before):
+                start = c * plan.rows + r
+                out_ref[sources, start:start + SUB, :] = back[:, c * levels:(c + 1) * levels].reshape(
+                    SUB, SUB, levels
+                )
+        filled = jnp.concatenate([kept, jnp.zeros((12 * SUB, levels), F32)], axis=0).astype(BF)
+        out_ref[sources, 4 * plan.rows:4 * plan.rows + SUB, :] = turn(filled).astype(BF).reshape(SUB, SUB, levels)
+
+
+def filter_rows(plan, info, received, own, other):
     levels = received.shape[2]
-    count = plan.chunks[at][2]
-    last = at == len(plan.chunks) - 1
-    height = ceil_to(2 * count, SUB)
-    out_height = 4 * height + (SUB if last else 0)
-    smem = pl.BlockSpec(memory_space=pltpu.SMEM)
+    operands = [info, received, *own, *other]
     vmem = pl.BlockSpec(memory_space=pltpu.VMEM)
-    out_shape = [jax.ShapeDtypeStruct((plan.group, out_height, levels), BF)]
-    if not last:
-        out_shape.append(jax.ShapeDtypeStruct((4 * plan.group, levels), F32))
-    operands = [info, received, own, other] + ([] if at == 0 else [before])
     return pl.pallas_call(
-        functools.partial(filter_kernel, plan, at, levels),
-        out_shape=out_shape,
-        in_specs=[smem] + [vmem] * (len(operands) - 1),
-        out_specs=[vmem] * len(out_shape),
+        functools.partial(filter_kernel, plan, levels, len(own)),
+        out_shape=jax.ShapeDtypeStruct(received.shape, BF),
+        in_specs=[pl.BlockSpec(memory_space=pltpu.SMEM)] + [vmem] * (len(operands) - 1),
+        out_specs=vmem,
         scratch_shapes=[
-            pltpu.VMEM((height * SUB, 4 * levels), BF),
-            pltpu.VMEM((height * SUB, 4 * levels), BF),
+            pltpu.VMEM((plan.rows * SUB, 4 * levels), BF),
+            pltpu.VMEM((plan.rows * SUB, 4 * levels), BF),
         ],
-        compiler_params=pltpu.CompilerParams(vmem_limit_bytes=VMEM_LIMIT),
+        compiler_params=pltpu.CompilerParams(vmem_limit_bytes=20 * 1024 * 1024),
         cost_estimate=pl.CostEstimate(
-            flops=2 * plan.group * 16 * count * levels * levels * 4,
-            bytes_accessed=plan.group * out_height * levels * 4 + 4 * count * levels * levels,
+            flops=2 * plan.group * 16 * plan.block * levels * levels * 4,
+            bytes_accessed=2 * 2 * received.size + 4 * plan.block * levels * levels,
             transcendentals=0,
         ),
         name="filter_rows",
     )(*operands)
 
 
-def grid_kernel(plan, levels, latitudes, depth, level_cols, info_ref, starts_ref, bands_ref, *refs):
-    count = len(plan.chunks)
-    parts = refs[:count]
-    tables, (out_ref, rows_ref, grid_ref) = refs[count:count + 2], refs[count + 2:]
+def grid_kernel(plan, levels, latitudes, depth, level_cols, info_ref, starts_ref, bands_ref, part_ref, *refs):
+    tables, (out_ref, rows_ref, grid_ref) = refs[:2], refs[2:]
     half, step = pl.program_id(0), pl.program_id(1)
     tile = tables[0].shape[0]
 
@@ -253,18 +275,17 @@
     def _():
         base = 0
         for at, first, rows in plan.segments:
-            height = ceil_to(2 * plan.chunks[at][2], SUB)
             for k in range(plan.group):
                 for c in range(4):
-                    rows_ref[base + k * rows:base + (k + 1) * rows, c * levels:(c + 1) * levels] = parts[at][
-                        k, c * height + first:c * height + first + rows, :
+                    start = c * plan.rows + plan.chunks[at][0] + first
+                    rows_ref[base + k * rows:base + (k + 1) * rows, c * levels:(c + 1) * levels] = part_ref[
+                        k, start:start + rows, :
                     ]
             base += plan.group * rows
 
     @pl.when((half == 1) & (step == 0))
     def _():
-        height = ceil_to(2 * plan.chunks[-1][2], SUB)
-        extra = parts[-1][info_ref[0], 4 * height:4 * height + SUB, :]
+        extra = part_ref[info_ref[0], 4 * plan.rows:4 * plan.rows + SUB, :]
         base = info_ref[1] // SUB * SUB
         place = pl.ds(pl.multiple_of(base, SUB), SUB)
         here = lax.broadcasted_iota(jnp.int32, (SUB, levels), 0) == info_ref[1] - base
@@ -284,22 +305,33 @@
     def _():
         waves = bands_ref.shape[0]
         groups = 4 * levels // level_cols
-        piece = 80 if depth % 80 == 0 else depth
-        i = lax.broadcasted_iota(jnp.int32, (piece, 4 * levels), 0)
+        place = lax.broadcasted_iota(jnp.int32, (8, 4 * levels), 0)
         for w in range(waves):
             start = starts_ref[w]
             base = start // 8 * 8
-            for r in range(0, depth, piece):
-                held = grid_ref[pl.ds(pl.multiple_of(base + r, 8), piece + 8), :]
-                held = pltpu.roll(held, (piece + 8 - (start - base)) % (piece + 8), axis=0)[:piece]
-                got = jnp.where(i < bands_ref[w] - r, held, 0.0).astype(BF)
-                for g in range(groups):
-                    out_ref[w * groups + g, 0, r:r + piece, :] = got[:, g * level_cols:(g + 1) * level_cols]
-
-
-def to_bands(plan, info, starts, bands, parts, tables, depth, level_cols):
+            offset = start - base
+
+            def slab(at):
+                held = grid_ref[pl.ds(pl.multiple_of(base + at, 8), 8), :]
+                return pltpu.roll(held, (8 - offset) % 8, axis=0)
+
+            after = slab(0)
+            done = []
+            for r in range(0, depth, 8):
+                now, after = after, slab(r + 8)
+                got = jnp.where(place < 8 - offset, now, after)
+                done.append(jnp.where(place < bands_ref[w] - r, got, 0.0))
+                if len(done) == 2 or r + 8 == depth:
+                    rows = jnp.concatenate(done, axis=0).astype(BF)
+                    first = r + 8 - rows.shape[0]
+                    for g in range(groups):
+                        out_ref[w * groups + g, 0, first:r + 8, :] = rows[:, g * level_cols:(g + 1) * level_cols]
+                    done = []
+
+
+def to_bands(plan, info, starts, bands, part, tables, depth, level_cols):
     latitudes = tables[0].shape[0]
-    levels = parts[0].shape[2]
+    levels = part.shape[2]
     columns = 4 * levels
     tile = 512
     steps = latitudes // tile
@@ -309,9 +341,9 @@
         functools.partial(grid_kernel, plan, levels, latitudes, depth, level_cols),
         grid=(2, steps),
         out_shape=jax.ShapeDtypeStruct((messages, 2, depth, level_cols), BF),
-        in_specs=[smem, smem, smem]
-        + [pl.BlockSpec(part.shape, lambda h, t: (0, 0, 0)) for part in parts]
-        + [
+        in_specs=[
+            smem, smem, smem,
+            pl.BlockSpec(part.shape, lambda h, t: (0, 0, 0)),
             pl.BlockSpec((tile, plan.widths[0]), lambda h, t: (jnp.where(h == 0, t, steps - 1), 0)),
             pl.BlockSpec((tile, plan.widths[1]), lambda h, t: (jnp.where(h == 0, 0, t), 0)),
         ],
@@ -320,14 +352,14 @@
             pltpu.VMEM((plan.widths[0], columns), BF),
             pltpu.VMEM((ceil_to(latitudes + depth, 8) + 8, columns), F32),
         ],
-        compiler_params=pltpu.CompilerParams(vmem_limit_bytes=VMEM_LIMIT),
+        compiler_params=pltpu.CompilerParams(vmem_limit_bytes=40 * 1024 * 1024),
         cost_estimate=pl.CostEstimate(
             flops=2 * latitudes * sum(plan.widths) * columns,
             bytes_accessed=2 * latitudes * sum(plan.widths) + 4 * messages * depth * level_cols,
             transcendentals=0,
         ),
         name="grid_bands",
-    )(info, starts, bands, *parts, *tables)
+    )(info, starts, bands, part, *tables)
 
 
 def per_device(control, covariance, legendre, pair_order, band_rows):
@@ -351,16 +383,14 @@
         return lax.all_to_all(rows, axes, split_axis=0, concat_axis=0, tiled=True, axis_index_groups=halves)
 
     mirror = [(d, 2 * group - 1 - d) for d in range(2 * group)]
-    own, other = [], []
-    for _, first, count in plan.chunks:
-        start = jnp.where(is_high == 1, block - first - count, first)
-        block_rows = lax.dynamic_slice_in_dim(covariance, start, count, 0).astype(BF)
-        if other:
-            block_rows, other[-1] = lax.optimization_barrier((block_rows, other[-1]))
-        else:
-            block_rows, control = lax.optimization_barrier((block_rows, control))
-        own.append(block_rows)
-        other.append(lax.ppermute(own[-1], axes, mirror))
+    pieces = 2 if block % 2 == 0 else 1
+    each = block // pieces
+    own = []
+    for fold in range(0, block, each):
+        start = jnp.where(is_high == 1, block - fold - each, fold)
+        own.append(lax.dynamic_slice_in_dim(covariance, start, each, 0).astype(BF))
+    *own, control = lax.optimization_barrier((*own, control))
+    other = [lax.ppermute(piece, axes, mirror) for piece in own]
 
     def slots_of(message, fold, folded, used):
         message = jnp.where(is_high == 1, group - 1 - message, message)
@@ -374,30 +404,18 @@
     sent = jnp.where(upper >= 0, upper, lower)
     received = exchange(pack(plan, control[0], pair_order, sent[:, None]))
 
-    slot_index = jnp.arange(slots, dtype=jnp.int32)[:, None]
-    tables = [
-        jnp.einsum(
-            "sl,sr->lr", legendre[0], (index[None, :] == slot_index).astype(BF), preferred_element_type=F32
-        ).astype(BF)
-        for index in (
-            index[:width] for index, width in zip(slots_of(*plan.transform_rows()), plan.widths)
-        )
-    ]
+    tables = make_tables(plan, legendre[0], slots_of(*plan.transform_rows()))
 
     info = jnp.stack([is_high, mine * block])
     received, tables = lax.optimization_barrier((received, tables))
-    parts, before = [], None
-    for at in range(len(plan.chunks)):
-        result, *rest = filter_rows(plan, at, info, received, own[at], other[at], before)
-        before = rest[0] if rest else None
-        parts.append(exchange(result))
+    filtered = exchange(filter_rows(plan, info, received, own, other))
 
     extra_block = lowest // block
     extra_message = jnp.where(is_high == 1, group - 1 - extra_block, extra_block)
     extra_row = plan.extra_row(extra_message, lowest - extra_block * block)
     where = jnp.stack([extra_message, extra_row])
     starts = jnp.cumsum(band_rows) - band_rows
-    outgoing = to_bands(plan, where, starts, band_rows, parts, tables, depth, level_cols)
+    outgoing = to_bands(plan, where, starts, band_rows, filtered, tables, depth, level_cols)
     outgoing = outgoing.reshape(-1, depth, level_cols)
     return lax.all_to_all(outgoing, axes, split_axis=0, concat_axis=0, tiled=True)
 

time: 309 us -> 279 us (0.903)
  blocking collectives: 179 us -> 149 us
  matrix products: 27.7 us -> 0 us
  starting transfers between devices: 18.5 us -> 34.3 us
  local copies, waits for them, and re-layouts: 5.74 us -> 14.6 us
  Pallas kernels: 31.9 us -> 40.7 us
  waiting for transfers between devices: 41.5 us -> 38.2 us
    all_to_all x1 -> x0, blocking collectives: 30.5 us -> none  [exchange(): lax.all_to_all(rows, axes, split_axis=0, concat_axis=0, tiled=True, axis_...]
    dot_general x2 -> x0, matrix products: 27.7 us -> none  [per_device(): jnp.einsum('sl,sr->lr', legendre[0], (index[None, :] == slot_index).astyp...]
    all_to_all x2, starting transfers between devices: 10.9 us -> 28.7 us  [exchange(): lax.all_to_all(rows, axes, split_axis=0, concat_axis=0, tiled=True, axis_...]
    pallas_call x2, Pallas kernels: 8.18 us -> 24.3 us  [the longest x1 19.7 us: make_tables(): pl.pallas_call(functools.partial(table_kernel, plan), grid=(latitudes //...]
    unnamed x11 -> x15, local copies, waits for them, and re-layouts: 3.51 us -> 12.4 us
    ppermute x2, waiting for transfers between devices: 26.9 us -> 18.4 us  [per_device(): other = [lax.ppermute(piece, axes, mirror) for piece in own]]
    pallas_call x1, Pallas kernels: 18.1 us -> 12.3 us  [to_bands(): pl.pallas_call(functools.partial(grid_kernel, plan, levels, latitudes, de...]
    all_to_all x2, waiting for transfers between devices: 14.5 us -> 19.8 us  [exchange(): lax.all_to_all(rows, axes, split_axis=0, concat_axis=0, tiled=True, axis_...]
  transfers between devices with their start and end apart: 4 -> 4, of which waited for: 2 -> 3; matrix products, arithmetic and copies ran while one was open for 10% -> 0% of each run, Pallas kernels for 2% -> 7%
where the time goes in v4:
time: 279 us
  blocking collectives  149 us (53%)
  Pallas kernels  40.7 us (15%)
  waiting for transfers between devices  38.2 us (14%)
  starting transfers between devices  34.3 us (12%)
  local copies, waits for them, and re-layouts  14.6 us (5%)
    all_to_all x1, blocking collectives, per_device(): lax.all_to_all(outgoing, axes, split_axis=0, concat_axis=0, tiled=True)  149 us
    all_to_all x2, starting transfers between devices, exchange(): lax.all_to_all(rows, axes, split_axis=0, concat_axis=0, tiled=True, axis_...  28.7 us
    all_to_all x2, waiting for transfers between devices, exchange(): lax.all_to_all(rows, axes, split_axis=0, concat_axis=0, tiled=True, axis_...  19.8 us
    pallas_call x1, Pallas kernels, make_tables(): pl.pallas_call(functools.partial(table_kernel, plan), grid=(latitudes //...  19.7 us
    ppermute x2, waiting for transfers between devices, per_device(): other = [lax.ppermute(piece, axes, mirror) for piece in own]  18.4 us
    unnamed x15, local copies, waits for them, and re-layouts  12.4 us
    pallas_call x1, Pallas kernels, to_bands(): pl.pallas_call(functools.partial(grid_kernel, plan, levels, latitudes, de...  12.3 us
    ppermute x2, starting transfers between devices, per_device(): other = [lax.ppermute(piece, axes, mirror) for piece in own]  5.58 us
  transfers between devices with their start and end apart: 4, of which 3 were waited for; matrix products, arithmetic and copies ran while one was open for 0% of the time, Pallas kernels for 7%

profile of v4, /device:TPU:0, one launch (start us, length us, event | category | flops | bytes accessed | tf_op | source)
XLA Modules:
  0.0 278.7 jit_solution(11717926751515089083)
XLA Ops:
  0.8 0.8 multiply_add_fusion
  1.6 0.2 broadcast_in_dim.20.slot_ref
  1.8 1.9 dynamic-slice_convert_fusion
  3.7 0.0 copy-start.6
  3.8 4.0 %pack_rows.1 = bf16[16,336,128]{2,1,0:T(8,128)(2,1)} custom-call(s32[1]{0:T(128)} %copy.20.info_ref, s32[1280,1]{1,0:T(8,128)S(1)} %broadcast_in_dim.20.slot_ref, bf16[1281,512]{1,0:T(8,128)(2,1)S(1)} %bitcast.19), custom_call_target="tpu_custom_call" | custom-call | flops 1 | bytes 1 | tf_op jit(solution)/shard_map/pack_rows/pallas_call | solution.py:119
  7.8 6.3 %all-to-all-start = ((bf16[16,336,128]{2,1,0:T(8,128)(2,1)}), bf16[16,336,128]{2,1,0:T(8,128)(2,1)S(1)}, u32[]{:S(2)}, u32[]{:S(2)}) async-start(bf16[16,336,128]{2,1,0:T(8,128)(2,1)} %pack_rows.1), calls=%async_computation | async-start | bytes 2752512 | tf_op jit(solution)/shard_map/all_to_all | solution.py:383
  14.1 5.5 %collective-permute-start = (bf16[20,128,128]{2,1,0:T(8,128)(2,1)S(1)}, bf16[20,128,128]{2,1,0:T(8,128)(2,1)S(1)}, u32[]{:S(2)}, u32[]{:S(2)}) collective-permute-start(bf16[20,128,128]{2,1,0:T(8,128)(2,1)S(1)} %get-tuple-element.17.refs_0_), channel_id=1, source_target_pairs={{0,31},{1,30},{2,29},{3,28},{4,27},{5,26},{6,25},{7,24},{8,23},{9,... | collective-permute-start | bytes 1966088 | tf_op jit(solution)/shard_map/ppermute | solution.py:393
  19.6 0.1 collective-permute-start.1
  19.7 2.9 %copy-done = bf16[1,1281,2560]{2,1,0:T(8,128)(2,1)S(1)} copy-done((bf16[1,1281,2560]{2,1,0:T(8,128)(2,1)S(1)}, bf16[1,1281,2560]{2,1,0:T(8,128)(2,1)}, u32[]{:S(2)}) %copy-start) | copy-done | bytes 6558744
  22.6 19.7 %make_tables.1 = (bf16[2560,1280]{1,0:T(8,128)(2,1)S(1)}, bf16[2560,768]{1,0:T(8,128)(2,1)S(1)}) custom-call(s32[1,1280]{1,0:T(1,128)S(1)} %broadcast_in_dim.18.upper_ref, s32[1,768]{1,0:T(1,128)S(1)} %broadcast_in_dim.19.lower_ref, bf16[1281,2560]{1,0:T(8,128)(2,1)S(1)} %bitcast.17), custom_call_target="tpu_custom_call" | custom-call | flops 1 | bytes 1 | tf_op jit(solution)/shard_map/make_tables/pallas_call | solution.py:161
  42.3 2.8 copy-done.2
  45.1 1.9 copy-done.3
  46.9 0.1 pad_add_fusion.1.info_ref
  47.0 4.3 %collective-permute-done.refs_2_ = bf16[20,128,128]{2,1,0:T(8,128)(2,1)S(1)} collective-permute-done((bf16[20,128,128]{2,1,0:T(8,128)(2,1)S(1)}, bf16[20,128,128]{2,1,0:T(8,128)(2,1)S(1)}, u32[]{:S(2)}, u32[]{:S(2)}) %collective-permute-start) | collective-permute-done | bytes 655392 | tf_op jit(solution)/shard_map/ppermute | solution.py:393
  51.3 14.1 %collective-permute-done.1.refs_3_ = bf16[20,128,128]{2,1,0:T(8,128)(2,1)} collective-permute-done((bf16[20,128,128]{2,1,0:T(8,128)(2,1)S(1)}, bf16[20,128,128]{2,1,0:T(8,128)(2,1)}, u32[]{:S(2)}, u32[]{:S(2)}) %collective-permute-start.1) | collective-permute-done | bytes 655392 | tf_op jit(solution)/shard_map/ppermute | solution.py:393
  65.4 4.6 %filter_rows.1 = bf16[16,336,128]{2,1,0:T(8,128)(2,1)} custom-call(s32[2]{0:T(128)S(1)} %pad_add_fusion.1.info_ref, bf16[16,336,128]{2,1,0:T(8,128)(2,1)S(1)} %all-to-all-done.rows_ref, bf16[20,128,128]{2,1,0:T(8,128)(2,1)S(1)} %get-tuple-element.17.refs_0_, bf16[20,128,128]{2,1,0:T(8,128)(2,1)S(1)} %get-tuple-element.18.refs_1_, ...), custom_call_target="tpu_custom_call" | custom-call | flops 1342177280 | bytes 5373952 | tf_op jit(solution)/shard_map/filter_rows/pallas_call | solution.py:250
  70.1 22.4 %all-to-all-start.1 = ((bf16[16,336,128]{2,1,0:T(8,128)(2,1)}), bf16[16,336,128]{2,1,0:T(8,128)(2,1)S(1)}, u32[]{:S(2)}, u32[]{:S(2)}) async-start(bf16[16,336,128]{2,1,0:T(8,128)(2,1)} %filter_rows.1), calls=%async_computation.1 | async-start | bytes 2752512 | tf_op jit(solution)/shard_map/all_to_all | solution.py:383
  92.6 0.2 reduce-window.9
  92.8 0.1 pad_add_fusion.info_ref
  92.8 19.8 %all-to-all-done.1.part_ref = bf16[16,336,128]{2,1,0:T(8,128)(2,1)S(1)} async-done(((bf16[16,336,128]{2,1,0:T(8,128)(2,1)}), bf16[16,336,128]{2,1,0:T(8,128)(2,1)S(1)}, u32[]{:S(2)}, u32[]{:S(2)}) %all-to-all-start.1) | async-done | bytes 1376288 | tf_op jit(solution)/shard_map/all_to_all | solution.py:383
  112.6 2.1 copy-done.4
  114.8 12.3 %grid_bands.1 = bf16[32,2,400,128]{3,2,1,0:T(8,128)(2,1)S(1)} custom-call(s32[2]{0:T(128)S(1)} %pad_add_fusion.info_ref, s32[8]{0:T(128)S(1)} %bitcast_subtract_fusion.starts_ref, s32[8]{0:T(128)S(1)} %copy-done.5, bf16[16,336,128]{2,1,0:T(8,128)(2,1)S(1)} %all-to-all-done.1.part_ref, bf16[2560,1280]{1,0:T(8,128)(2,1)} %copy-done.2, ...), custom_call_target="tpu_custom_call" | custom-call | flops 5368709120 | bytes 17039360 | tf_op jit(solution)/shard_map/grid_bands/pallas_call | solution.py:340
  127.1 148.8 %all_to_all.15 = bf16[64,400,128]{2,1,0:T(8,128)(2,1)S(1)} all-to-all(bf16[64,400,128]{2,1,0:T(8,128)(2,1)S(1)} %bitcast.18), channel_id=1, replica_groups=mesh['wave'=8,'lev'=4] {'wave','lev'}, dimensions={0} | all-to-all | bytes 13107200 | tf_op jit(solution)/shard_map/all_to_all | solution.py:420
  275.9 2.8 %copy.21 = bf16[64,400,128]{2,1,0:T(8,128)(2,1)} copy(bf16[64,400,128]{2,1,0:T(8,128)(2,1)S(1)} %all_to_all.15) | data formatting | bytes 13107200
  (14 shorter events, 0.0 us)
Async XLA Ops:
  0.0 3.7 %copy-start.1 = (bf16[1,1281,512]{2,1,0:T(8,128)(2,1)S(1)}, bf16[1,1281,512]{2,1,0:T(8,128)(2,1)}, u32[]{:S(2)}) copy-start(bf16[1,1281,512]{2,1,0:T(8,128)(2,1)} %param.17) | copy-start | bytes 3935236
  3.7 15.9 %copy-start.6 = (pred[1280]{0:T(1024)(128)(4,1)S(1)}, pred[1280]{0:T(1024)(128)(4,1)}, u32[]{:S(2)}) copy-start(pred[1280]{0:T(1024)(128)(4,1)} %constant.75.clone) | copy-start | bytes 3844
  7.8 39.2 %all-to-all-start = ((bf16[16,336,128]{2,1,0:T(8,128)(2,1)}), bf16[16,336,128]{2,1,0:T(8,128)(2,1)S(1)}, u32[]{:S(2)}, u32[]{:S(2)}) async-start(bf16[16,336,128]{2,1,0:T(8,128)(2,1)} %pack_rows.1), calls=%async_computation | async-start | bytes 2752512 | tf_op jit(solution)/shard_map/all_to_all | solution.py:383
  14.1 37.2 %collective-permute-start = (bf16[20,128,128]{2,1,0:T(8,128)(2,1)S(1)}, bf16[20,128,128]{2,1,0:T(8,128)(2,1)S(1)}, u32[]{:S(2)}, u32[]{:S(2)}) collective-permute-start(bf16[20,128,128]{2,1,0:T(8,128)(2,1)S(1)} %get-tuple-element.17.refs_0_), channel_id=1, source_target_pairs={{0,31},{1,30},{2,29},{3,28},{4,27},{5,26},{6,25},{7,24},{8,23},{9,... | collective-permute-start | bytes 1966088 | tf_op jit(solution)/shard_map/ppermute | solution.py:393
  19.6 45.9 %collective-permute-start.1 = (bf16[20,128,128]{2,1,0:T(8,128)(2,1)S(1)}, bf16[20,128,128]{2,1,0:T(8,128)(2,1)}, u32[]{:S(2)}, u32[]{:S(2)}) collective-permute-start(bf16[20,128,128]{2,1,0:T(8,128)(2,1)S(1)} %get-tuple-element.18.refs_1_), channel_id=1, source_target_pairs={{0,31},{1,30},{2,29},{3,28},{4,27},{5,26},{6,25},{7,24},{8,23},{9,... | collective-permute-start | bytes 1966088 | tf_op jit(solution)/shard_map/ppermute | solution.py:393
  19.7 2.9 %copy-start = (bf16[1,1281,2560]{2,1,0:T(8,128)(2,1)S(1)}, bf16[1,1281,2560]{2,1,0:T(8,128)(2,1)}, u32[]{:S(2)}) copy-start(bf16[1,1281,2560]{2,1,0:T(8,128)(2,1)} %param.19) | copy-start | bytes 19676164
  42.3 2.8 %copy-start.2 = (bf16[2560,1280]{1,0:T(8,128)(2,1)}, bf16[2560,1280]{1,0:T(8,128)(2,1)S(1)}, u32[]{:S(2)}) copy-start(bf16[2560,1280]{1,0:T(8,128)(2,1)S(1)} %get-tuple-element.19.refs_0_) | copy-start | bytes 19660804
  45.1 1.9 copy-start.3
  70.1 22.5 %copy-start.5 = (s32[8]{0:T(128)S(1)}, s32[8]{0:T(128)}, u32[]{:S(2)}) copy-start(s32[8]{0:T(128)} %bands_ref.1) | copy-start | bytes 100
  70.1 42.6 %all-to-all-start.1 = ((bf16[16,336,128]{2,1,0:T(8,128)(2,1)}), bf16[16,336,128]{2,1,0:T(8,128)(2,1)S(1)}, u32[]{:S(2)}, u32[]{:S(2)}) async-start(bf16[16,336,128]{2,1,0:T(8,128)(2,1)} %filter_rows.1), calls=%async_computation.1 | async-start | bytes 2752512 | tf_op jit(solution)/shard_map/all_to_all | solution.py:383
  112.6 2.1 copy-start.4

commit v5 on v4

--- a/solution.py
+++ b/solution.py
@@ -178,19 +178,15 @@
     return jnp.where((i // SUB == j % SUB) & (i % SUB == j // SUB), 1.0, 0.0).astype(BF)
 
 
-def filter_kernel(plan, levels, pieces, info_ref, rows_ref, *refs):
-    own_refs, other_refs, (out_ref, x_ref, y_ref) = refs[:pieces], refs[pieces:2 * pieces], refs[2 * pieces:]
-    each = plan.block // pieces
-    is_high = info_ref[0] == 1
-    first_fold = info_ref[1].astype(F32)
+def filter_kernel(plan, levels, info_ref, rows_ref, both_ref, out_ref, x_ref, y_ref):
+    first_fold = info_ref[0].astype(F32)
     swap = swap_matrix()
 
     def low_matrix(fold):
-        return jnp.where(is_high, other_refs[fold // each][fold % each], own_refs[fold // each][fold % each])
+        return both_ref[0, fold]
 
     def high_matrix(fold):
-        at, place = fold // each, each - 1 - fold % each
-        return jnp.where(is_high, own_refs[at][place], other_refs[at][place])
+        return both_ref[1, plan.block - 1 - fold]
 
     def times(rows, matrix):
         return lax.dot_general(rows, matrix, (((1,), (1,)), ((), ())), preferred_element_type=F32)
@@ -243,14 +239,13 @@
         out_ref[sources, 4 * plan.rows:4 * plan.rows + SUB, :] = turn(filled).astype(BF).reshape(SUB, SUB, levels)
 
 
-def filter_rows(plan, info, received, own, other):
+def filter_rows(plan, info, received, both):
     levels = received.shape[2]
-    operands = [info, received, *own, *other]
     vmem = pl.BlockSpec(memory_space=pltpu.VMEM)
     return pl.pallas_call(
-        functools.partial(filter_kernel, plan, levels, len(own)),
+        functools.partial(filter_kernel, plan, levels),
         out_shape=jax.ShapeDtypeStruct(received.shape, BF),
-        in_specs=[pl.BlockSpec(memory_space=pltpu.SMEM)] + [vmem] * (len(operands) - 1),
+        in_specs=[pl.BlockSpec(memory_space=pltpu.SMEM), vmem, vmem],
         out_specs=vmem,
         scratch_shapes=[
             pltpu.VMEM((plan.rows * SUB, 4 * levels), BF),
@@ -263,7 +258,7 @@
             transcendentals=0,
         ),
         name="filter_rows",
-    )(*operands)
+    )(info, received, both)
 
 
 def grid_kernel(plan, levels, latitudes, depth, level_cols, info_ref, starts_ref, bands_ref, part_ref, *refs):
@@ -382,15 +377,8 @@
     def exchange(rows):
         return lax.all_to_all(rows, axes, split_axis=0, concat_axis=0, tiled=True, axis_index_groups=halves)
 
-    mirror = [(d, 2 * group - 1 - d) for d in range(2 * group)]
-    pieces = 2 if block % 2 == 0 else 1
-    each = block // pieces
-    own = []
-    for fold in range(0, block, each):
-        start = jnp.where(is_high == 1, block - fold - each, fold)
-        own.append(lax.dynamic_slice_in_dim(covariance, start, each, 0).astype(BF))
-    *own, control = lax.optimization_barrier((*own, control))
-    other = [lax.ppermute(piece, axes, mirror) for piece in own]
+    pairs = [[d, 2 * group - 1 - d] for d in range(group)]
+    both = lax.all_gather(covariance.astype(BF), axes, axis_index_groups=pairs)
 
     def slots_of(message, fold, folded, used):
         message = jnp.where(is_high == 1, group - 1 - message, message)
@@ -406,9 +394,9 @@
 
     tables = make_tables(plan, legendre[0], slots_of(*plan.transform_rows()))
 
-    info = jnp.stack([is_high, mine * block])
+    info = (mine * block)[None]
     received, tables = lax.optimization_barrier((received, tables))
-    filtered = exchange(filter_rows(plan, info, received, own, other))
+    filtered = exchange(filter_rows(plan, info, received, both))
 
     extra_block = lowest // block
     extra_message = jnp.where(is_high == 1, group - 1 - extra_block, extra_block)

time: 279 us -> 284 us (1.018)
  between operations: 0.92 us -> 14.3 us
  starting transfers between devices: 34.3 us -> 21 us
    ppermute x2 -> x0, waiting for transfers between devices: 18.4 us -> none  [per_device(): other = [lax.ppermute(piece, axes, mirror) for piece in own]]
    all_gather x0 -> x1, waiting for transfers between devices: none -> 14 us  [per_device(): both = lax.all_gather(covariance.astype(BF), axes, axis_index_groups=pairs)]
    all_to_all x2, starting transfers between devices: 28.7 us -> 21 us  [exchange(): lax.all_to_all(rows, axes, split_axis=0, concat_axis=0, tiled=True, axis_...]
    all_to_all x2, waiting for transfers between devices: 19.8 us -> 26.9 us  [exchange(): lax.all_to_all(rows, axes, split_axis=0, concat_axis=0, tiled=True, axis_...]
    ppermute x2 -> x0, starting transfers between devices: 5.58 us -> none  [per_device(): other = [lax.ppermute(piece, axes, mirror) for piece in own]]
    convert_element_type x0 -> x1, other arithmetic: none -> 3.21 us  [per_device(): both = lax.all_gather(covariance.astype(BF), axes, axis_index_groups=pairs)]
    unnamed x15 -> x31, local copies, waits for them, and re-layouts: 12.4 us -> 14.6 us
  transfers between devices with their start and end apart: 4 -> 3, of which waited for: 3 -> 3; matrix products, arithmetic and copies ran while one was open for 0% -> 0% of each run, Pallas kernels for 7% -> 8%
where the time goes in v5:
time: 284 us
  blocking collectives  150 us (53%)
  waiting for transfers between devices  40.9 us (14%)
  Pallas kernels  39.5 us (14%)
  starting transfers between devices  21 us (7%)
  local copies, waits for them, and re-layouts  14.8 us (5%)
  between operations  14.3 us (5%)
  other arithmetic  3.5 us (1%)
    all_to_all x1, blocking collectives, per_device(): lax.all_to_all(outgoing, axes, split_axis=0, concat_axis=0, tiled=True)  150 us
    all_to_all x2, waiting for transfers between devices, exchange(): lax.all_to_all(rows, axes, split_axis=0, concat_axis=0, tiled=True, axis_...  26.9 us
    all_to_all x2, starting transfers between devices, exchange(): lax.all_to_all(rows, axes, split_axis=0, concat_axis=0, tiled=True, axis_...  21 us
    pallas_call x1, Pallas kernels, make_tables(): pl.pallas_call(functools.partial(table_kernel, plan), grid=(latitudes //...  19.7 us
    unnamed x31, local copies, waits for them, and re-layouts  14.6 us
    all_gather x1, waiting for transfers between devices, per_device(): both = lax.all_gather(covariance.astype(BF), axes, axis_index_groups=pairs)  14 us
    pallas_call x1, Pallas kernels, to_bands(): pl.pallas_call(functools.partial(grid_kernel, plan, levels, latitudes, de...  12.3 us
  transfers between devices with their start and end apart: 3, of which 3 were waited for; matrix products, arithmetic and copies ran while one was open for 0% of the time, Pallas kernels for 8%

profile of v5, /device:TPU:0, one launch (start us, length us, event | category | flops | bytes accessed | tf_op | source)
XLA Modules:
  0.0 283.9 jit_solution(7547006563147881484)
XLA Ops:
  6.6 0.0 copy-start.12
  6.6 0.0 copy-start.13
  6.6 0.0 all-gather.3.cloned.1.call-start
  6.6 3.2 %convert_element_type.7 = bf16[40,128,128]{2,1,0:T(8,128)(2,1)} convert(f32[40,128,128]{2,1,0:T(8,128)} %param.18) | non-fusion elementwise | flops 655360 | bytes 3932160 | tf_op jit(solution)/shard_map/convert_element_type | solution.py:381
  9.9 0.0 all-gather.3.cloned.1.call-update
  10.6 0.2 broadcast_in_dim.24.slot_ref
  10.9 4.0 %pack_rows.1 = bf16[16,336,128]{2,1,0:T(8,128)(2,1)} custom-call(s32[1]{0:T(128)} %copy.21.info_ref, s32[1280,1]{1,0:T(8,128)S(1)} %broadcast_in_dim.24.slot_ref, bf16[1281,512]{1,0:T(8,128)(2,1)S(1)} %bitcast.20), custom_call_target="tpu_custom_call" | custom-call | flops 1 | bytes 1 | tf_op jit(solution)/shard_map/pack_rows/pallas_call | solution.py:119
  14.9 6.3 %all-to-all-start = ((bf16[16,336,128]{2,1,0:T(8,128)(2,1)}), bf16[16,336,128]{2,1,0:T(8,128)(2,1)S(1)}, u32[]{:S(2)}, u32[]{:S(2)}) async-start(bf16[16,336,128]{2,1,0:T(8,128)(2,1)} %pack_rows.1), calls=%async_computation | async-start | bytes 2752512 | tf_op jit(solution)/shard_map/all_to_all | solution.py:378
  21.2 3.3 %copy-done = bf16[1,1281,2560]{2,1,0:T(8,128)(2,1)S(1)} copy-done((bf16[1,1281,2560]{2,1,0:T(8,128)(2,1)S(1)}, bf16[1,1281,2560]{2,1,0:T(8,128)(2,1)}, u32[]{:S(2)}) %copy-start) | copy-done | bytes 6558744
  24.5 19.7 %make_tables.1 = (bf16[2560,1280]{1,0:T(8,128)(2,1)S(1)}, bf16[2560,768]{1,0:T(8,128)(2,1)S(1)}) custom-call(s32[1,1280]{1,0:T(1,128)S(1)} %broadcast_in_dim.22.upper_ref, s32[1,768]{1,0:T(1,128)S(1)} %broadcast_in_dim.23.lower_ref, bf16[1281,2560]{1,0:T(8,128)(2,1)S(1)} %bitcast.17), custom_call_target="tpu_custom_call" | custom-call | flops 1 | bytes 1 | tf_op jit(solution)/shard_map/make_tables/pallas_call | solution.py:161
  44.2 2.8 copy-done.3
  47.0 1.9 copy-done.4
  48.9 7.1 %all-to-all-done.rows_ref = bf16[16,336,128]{2,1,0:T(8,128)(2,1)S(1)} async-done(((bf16[16,336,128]{2,1,0:T(8,128)(2,1)}), bf16[16,336,128]{2,1,0:T(8,128)(2,1)S(1)}, u32[]{:S(2)}, u32[]{:S(2)}) %all-to-all-start) | async-done | bytes 1376288 | tf_op jit(solution)/shard_map/all_to_all | solution.py:378
  55.9 14.0 %all-gather.3.cloned.1.call-done = bf16[80,128,128]{2,1,0:T(8,128)(2,1)} async-done(((bf16[40,128,128]{2,1,0:T(8,128)(2,1)}), bf16[80,128,128]{2,1,0:T(8,128)(2,1)}) %all-gather.3.cloned.1.call-update) | async-done | bytes 2621456 | tf_op jit(solution)/shard_map/all_gather | solution.py:381
  69.9 1.7 copy-done.1
  71.7 3.5 %filter_rows.1 = bf16[16,336,128]{2,1,0:T(8,128)(2,1)} custom-call(s32[1]{0:T(128)} %bitcast.5.info_ref, bf16[16,336,128]{2,1,0:T(8,128)(2,1)S(1)} %all-to-all-done.rows_ref, bf16[2,40,128,128]{3,2,1,0:T(8,128)(2,1)S(1)} %bitcast.19), custom_call_target="tpu_custom_call" | custom-call | flops 1342177280 | bytes 5373952 | tf_op jit(solution)/shard_map/filter_rows/pallas_call | solution.py:245
  75.2 14.7 %all-to-all-start.1 = ((bf16[16,336,128]{2,1,0:T(8,128)(2,1)}), bf16[16,336,128]{2,1,0:T(8,128)(2,1)S(1)}, u32[]{:S(2)}, u32[]{:S(2)}) async-start(bf16[16,336,128]{2,1,0:T(8,128)(2,1)} %filter_rows.1), calls=%async_computation.1 | async-start | bytes 2752512 | tf_op jit(solution)/shard_map/all_to_all | solution.py:378
  90.0 0.2 reduce-window.9
  90.2 0.1 pad_add_fusion.info_ref
  90.2 19.8 %all-to-all-done.1.part_ref = bf16[16,336,128]{2,1,0:T(8,128)(2,1)S(1)} async-done(((bf16[16,336,128]{2,1,0:T(8,128)(2,1)}), bf16[16,336,128]{2,1,0:T(8,128)(2,1)S(1)}, u32[]{:S(2)}, u32[]{:S(2)}) %all-to-all-start.1) | async-done | bytes 1376288 | tf_op jit(solution)/shard_map/all_to_all | solution.py:378
  110.1 2.1 copy-done.5
  112.2 12.3 %grid_bands.1 = bf16[32,2,400,128]{3,2,1,0:T(8,128)(2,1)S(1)} custom-call(s32[2]{0:T(128)S(1)} %pad_add_fusion.info_ref, s32[8]{0:T(128)S(1)} %bitcast_subtract_fusion.starts_ref, s32[8]{0:T(128)S(1)} %copy-done.6, bf16[16,336,128]{2,1,0:T(8,128)(2,1)S(1)} %all-to-all-done.1.part_ref, bf16[2560,1280]{1,0:T(8,128)(2,1)} %copy-done.3, ...), custom_call_target="tpu_custom_call" | custom-call | flops 5368709120 | bytes 17039360 | tf_op jit(solution)/shard_map/grid_bands/pallas_call | solution.py:335
  124.5 149.7 %all_to_all.15 = bf16[64,400,128]{2,1,0:T(8,128)(2,1)S(1)} all-to-all(bf16[64,400,128]{2,1,0:T(8,128)(2,1)S(1)} %bitcast.18), channel_id=1, replica_groups=mesh['wave'=8,'lev'=4] {'wave','lev'}, dimensions={0} | all-to-all | bytes 13107200 | tf_op jit(solution)/shard_map/all_to_all | solution.py:408
  274.2 2.8 copy.22
  (28 shorter events, 0.1 us)
Async XLA Ops:
  6.5 4.0 %copy-start.7 = (s32[1280]{0:T(1024)S(1)}, s32[1280]{0:T(1024)}, u32[]{:S(2)}) copy-start(s32[1280]{0:T(1024)} %constant.70.clone) | copy-start | bytes 15364
  6.5 4.0 %copy-start.8 = (s32[1280]{0:T(1024)S(1)}, s32[1280]{0:T(1024)}, u32[]{:S(2)}) copy-start(s32[1280]{0:T(1024)} %constant.69.clone) | copy-start | bytes 15364
  6.5 4.0 %copy-start.9 = (s32[1280]{0:T(1024)S(1)}, s32[1280]{0:T(1024)}, u32[]{:S(2)}) copy-start(s32[1280]{0:T(1024)} %constant.68.clone) | copy-start | bytes 15364
  6.5 4.0 %copy-start.10 = (s32[1280]{0:T(1024)S(1)}, s32[1280]{0:T(1024)}, u32[]{:S(2)}) copy-start(s32[1280]{0:T(1024)} %constant.65.clone) | copy-start | bytes 15364
  6.5 4.0 %copy-start.11 = (s32[1280]{0:T(1024)S(1)}, s32[1280]{0:T(1024)}, u32[]{:S(2)}) copy-start(s32[1280]{0:T(1024)} %constant.64.clone) | copy-start | bytes 15364
  6.6 4.0 %copy-start.12 = (s32[1280]{0:T(1024)S(1)}, s32[1280]{0:T(1024)}, u32[]{:S(2)}) copy-start(s32[1280]{0:T(1024)} %constant.63.clone) | copy-start | bytes 15364
  6.6 4.0 %copy-start.13 = (pred[1280]{0:T(1024)(128)(4,1)S(1)}, pred[1280]{0:T(1024)(128)(4,1)}, u32[]{:S(2)}) copy-start(pred[1280]{0:T(1024)(128)(4,1)} %constant.71.clone) | copy-start | bytes 3844
  6.6 4.0 %copy-start.14 = (pred[1280]{0:T(1024)(128)(4,1)S(1)}, pred[1280]{0:T(1024)(128)(4,1)}, u32[]{:S(2)}) copy-start(pred[1280]{0:T(1024)(128)(4,1)} %constant.66.clone) | copy-start | bytes 3844
  6.6 4.3 %copy-start.2 = (bf16[1,1281,512]{2,1,0:T(8,128)(2,1)S(1)}, bf16[1,1281,512]{2,1,0:T(8,128)(2,1)}, u32[]{:S(2)}) copy-start(bf16[1,1281,512]{2,1,0:T(8,128)(2,1)} %param.17) | copy-start | bytes 3935236
  6.6 63.3 %all-gather.3.cloned.1.call-start = ((), (), s32[]{:S(2)}) async-start(), calls=%async_computation.3 | async-start | bytes 3932160 | tf_op jit(solution)/shard_map/all_gather | solution.py:381
  14.9 41.1 %all-to-all-start = ((bf16[16,336,128]{2,1,0:T(8,128)(2,1)}), bf16[16,336,128]{2,1,0:T(8,128)(2,1)S(1)}, u32[]{:S(2)}, u32[]{:S(2)}) async-start(bf16[16,336,128]{2,1,0:T(8,128)(2,1)} %pack_rows.1), calls=%async_computation | async-start | bytes 2752512 | tf_op jit(solution)/shard_map/all_to_all | solution.py:378
  21.2 3.3 %copy-start = (bf16[1,1281,2560]{2,1,0:T(8,128)(2,1)S(1)}, bf16[1,1281,2560]{2,1,0:T(8,128)(2,1)}, u32[]{:S(2)}) copy-start(bf16[1,1281,2560]{2,1,0:T(8,128)(2,1)} %param.19) | copy-start | bytes 19676164
  44.2 2.8 copy-start.3
  47.0 1.9 copy-start.4
  69.9 1.7 copy-start.1
  75.2 14.8 %copy-start.6 = (s32[8]{0:T(128)S(1)}, s32[8]{0:T(128)}, u32[]{:S(2)}) copy-start(s32[8]{0:T(128)} %bands_ref.1) | copy-start | bytes 100
  75.2 34.9 %all-to-all-start.1 = ((bf16[16,336,128]{2,1,0:T(8,128)(2,1)}), bf16[16,336,128]{2,1,0:T(8,128)(2,1)S(1)}, u32[]{:S(2)}, u32[]{:S(2)}) async-start(bf16[16,336,128]{2,1,0:T(8,128)(2,1)} %filter_rows.1), calls=%async_computation.1 | async-start | bytes 2752512 | tf_op jit(solution)/shard_map/all_to_all | solution.py:378
  110.1 2.1 copy-start.5
Sparse Core Ops, SparseCore 0:
  10.0 59.8 all-gather.2

commit v6 on v5

--- a/solution.py
+++ b/solution.py
@@ -166,8 +166,10 @@
         + [pl.BlockSpec((slots, tile), lambda t: (0, t))],
         out_specs=[pl.BlockSpec((tile, width), lambda t: (t, 0)) for width in plan.widths],
         scratch_shapes=[pltpu.VMEM((slots - 1 + SUB, width), BF) for width in plan.widths],
-        compiler_params=pltpu.CompilerParams(vmem_limit_bytes=32 * 1024 * 1024),
-        cost_estimate=pl.CostEstimate(flops=1, bytes_accessed=1, transcendentals=0),
+        compiler_params=pltpu.CompilerParams(vmem_limit_bytes=20 * 1024 * 1024),
+        cost_estimate=pl.CostEstimate(
+            flops=20 * latitudes * slots * sum(plan.widths), bytes_accessed=2 * legendre.size, transcendentals=0
+        ),
         name="make_tables",
     )(*index, legendre)
 
@@ -178,15 +180,17 @@
     return jnp.where((i // SUB == j % SUB) & (i % SUB == j // SUB), 1.0, 0.0).astype(BF)
 
 
-def filter_kernel(plan, levels, info_ref, rows_ref, both_ref, out_ref, x_ref, y_ref):
-    first_fold = info_ref[0].astype(F32)
+def filter_kernel(plan, levels, info_ref, rows_ref, near_ref, far_ref, out_ref, x_ref, y_ref):
+    is_high = info_ref[0] == 1
+    first_fold = info_ref[1].astype(F32)
     swap = swap_matrix()
 
     def low_matrix(fold):
-        return both_ref[0, fold]
+        return jnp.where(is_high, far_ref[fold], near_ref[fold])
 
     def high_matrix(fold):
-        return both_ref[1, plan.block - 1 - fold]
+        at = plan.block - 1 - fold
+        return jnp.where(is_high, near_ref[at], far_ref[at])
 
     def times(rows, matrix):
         return lax.dot_general(rows, matrix, (((1,), (1,)), ((), ())), preferred_element_type=F32)
@@ -239,65 +243,70 @@
         out_ref[sources, 4 * plan.rows:4 * plan.rows + SUB, :] = turn(filled).astype(BF).reshape(SUB, SUB, levels)
 
 
-def filter_rows(plan, info, received, both):
+def filter_rows(plan, info, received, near_block, far_block):
     levels = received.shape[2]
     vmem = pl.BlockSpec(memory_space=pltpu.VMEM)
     return pl.pallas_call(
         functools.partial(filter_kernel, plan, levels),
         out_shape=jax.ShapeDtypeStruct(received.shape, BF),
-        in_specs=[pl.BlockSpec(memory_space=pltpu.SMEM), vmem, vmem],
+        in_specs=[pl.BlockSpec(memory_space=pltpu.SMEM), vmem, vmem, vmem],
         out_specs=vmem,
         scratch_shapes=[
             pltpu.VMEM((plan.rows * SUB, 4 * levels), BF),
             pltpu.VMEM((plan.rows * SUB, 4 * levels), BF),
         ],
-        compiler_params=pltpu.CompilerParams(vmem_limit_bytes=20 * 1024 * 1024),
+        compiler_params=pltpu.CompilerParams(vmem_limit_bytes=12 * 1024 * 1024),
         cost_estimate=pl.CostEstimate(
             flops=2 * plan.group * 16 * plan.block * levels * levels * 4,
             bytes_accessed=2 * 2 * received.size + 4 * plan.block * levels * levels,
             transcendentals=0,
         ),
         name="filter_rows",
-    )(info, received, both)
-
-
-def grid_kernel(plan, levels, latitudes, depth, level_cols, info_ref, starts_ref, bands_ref, part_ref, *refs):
-    tables, (out_ref, rows_ref, grid_ref) = refs[:2], refs[2:]
-    half, step = pl.program_id(0), pl.program_id(1)
-    tile = tables[0].shape[0]
-
-    @pl.when((half == 0) & (step == 0))
-    def _():
-        base = 0
-        for at, first, rows in plan.segments:
-            for k in range(plan.group):
-                for c in range(4):
-                    start = c * plan.rows + plan.chunks[at][0] + first
-                    rows_ref[base + k * rows:base + (k + 1) * rows, c * levels:(c + 1) * levels] = part_ref[
-                        k, start:start + rows, :
-                    ]
-            base += plan.group * rows
-
-    @pl.when((half == 1) & (step == 0))
-    def _():
-        extra = part_ref[info_ref[0], 4 * plan.rows:4 * plan.rows + SUB, :]
-        base = info_ref[1] // SUB * SUB
-        place = pl.ds(pl.multiple_of(base, SUB), SUB)
-        here = lax.broadcasted_iota(jnp.int32, (SUB, levels), 0) == info_ref[1] - base
-        for c in range(4):
-            cols = slice(c * levels, (c + 1) * levels)
-            held = rows_ref[place, cols].astype(F32)
-            rows_ref[place, cols] = jnp.where(here, extra[c:c + 1, :].astype(F32), held).astype(BF)
-
-    for at in range(2):
-        @pl.when(half == at)
-        def _():
-            grid_ref[pl.ds(pl.multiple_of(step * tile, tile), tile), :] = jnp.dot(
-                tables[at][...], rows_ref[:plan.widths[at], :], preferred_element_type=F32
+    )(info, received, near_block, far_block)
+
+
+def grid_kernel(plan, levels, latitudes, depth, level_cols, tile, info_ref, starts_ref, bands_ref, part_ref, *refs):
+    tables, out_ref, held_tables, (upper_ref, lower_ref, *grids, sems) = refs[:2], refs[2], refs[3:5], refs[5:]
+    tiles = [slice(at, at + tile) for at in range(0, latitudes, tile)]
+
+    def copy(half, at):
+        rows = tiles[at]
+        return pltpu.make_async_copy(tables[half].at[rows], held_tables[half].at[rows], sems.at[half, at])
+
+    for half in range(2):
+        for at in range(len(tiles)):
+            copy(half, at).start()
+
+    base = 0
+    for at, first, rows in plan.segments:
+        for k in range(plan.group):
+            for c in range(4):
+                start = c * plan.rows + plan.chunks[at][0] + first
+                cols = slice(c * levels, (c + 1) * levels)
+                value = part_ref[k, start:start + rows, :]
+                upper_ref[base + k * rows:base + (k + 1) * rows, cols] = value
+                if base < plan.widths[1]:
+                    lower_ref[base + k * rows:base + (k + 1) * rows, cols] = value
+        base += plan.group * rows
+
+    extra = part_ref[info_ref[0], 4 * plan.rows:4 * plan.rows + SUB, :]
+    base = info_ref[1] // SUB * SUB
+    place = pl.ds(pl.multiple_of(base, SUB), SUB)
+    here = lax.broadcasted_iota(jnp.int32, (SUB, levels), 0) == info_ref[1] - base
+    for c in range(4):
+        cols = slice(c * levels, (c + 1) * levels)
+        held = upper_ref[place, cols].astype(F32)
+        lower_ref[place, cols] = jnp.where(here, extra[c:c + 1, :].astype(F32), held).astype(BF)
+
+    def transform(half):
+        for at, rows in enumerate(tiles):
+            copy(half, at).wait()
+            grids[half][rows, :] = jnp.dot(
+                held_tables[half][rows, :], (upper_ref, lower_ref)[half][...], preferred_element_type=F32
             )
 
-    @pl.when(step == pl.num_programs(1) - 1)
-    def _():
+    def cut(half):
+        grid_ref = grids[half]
         waves = bands_ref.shape[0]
         groups = 4 * levels // level_cols
         place = lax.broadcasted_iota(jnp.int32, (8, 4 * levels), 0)
@@ -320,8 +329,13 @@
                     rows = jnp.concatenate(done, axis=0).astype(BF)
                     first = r + 8 - rows.shape[0]
                     for g in range(groups):
-                        out_ref[w * groups + g, 0, first:r + 8, :] = rows[:, g * level_cols:(g + 1) * level_cols]
+                        out_ref[w * groups + g, half, first:r + 8, :] = rows[:, g * level_cols:(g + 1) * level_cols]
                     done = []
+
+    transform(0)
+    cut(0)
+    transform(1)
+    cut(1)
 
 
 def to_bands(plan, info, starts, bands, part, tables, depth, level_cols):
@@ -329,25 +343,27 @@
     levels = part.shape[2]
     columns = 4 * levels
     tile = 512
-    steps = latitudes // tile
-    smem = pl.BlockSpec(memory_space=pltpu.SMEM)
+    smem, vmem = pl.BlockSpec(memory_space=pltpu.SMEM), pl.BlockSpec(memory_space=pltpu.VMEM)
     messages = bands.shape[0] * columns // level_cols
+    grid = pltpu.VMEM((ceil_to(latitudes + depth, 8) + 8, columns), F32)
+    held = 2 * (latitudes + columns) * sum(plan.widths) + 8 * (latitudes + depth) * columns
+    held += 4 * messages * depth * ceil_to(level_cols, 128) + 2 * part.size
+    limit = max(52 * 1024 * 1024, held + 4 * 1024 * 1024)
     return pl.pallas_call(
-        functools.partial(grid_kernel, plan, levels, latitudes, depth, level_cols),
-        grid=(2, steps),
+        functools.partial(grid_kernel, plan, levels, latitudes, depth, level_cols, tile),
         out_shape=jax.ShapeDtypeStruct((messages, 2, depth, level_cols), BF),
-        in_specs=[
-            smem, smem, smem,
-            pl.BlockSpec(part.shape, lambda h, t: (0, 0, 0)),
-            pl.BlockSpec((tile, plan.widths[0]), lambda h, t: (jnp.where(h == 0, t, steps - 1), 0)),
-            pl.BlockSpec((tile, plan.widths[1]), lambda h, t: (jnp.where(h == 0, 0, t), 0)),
+        in_specs=[smem, smem, smem, vmem] + [pl.BlockSpec(memory_space=pl.ANY)] * 2,
+        out_specs=vmem,
+        scratch_shapes=[
+            pltpu.VMEM(tables[0].shape, BF),
+            pltpu.VMEM(tables[1].shape, BF),
+            pltpu.VMEM((plan.widths[0], columns), BF),
+            pltpu.VMEM((plan.widths[1], columns), BF),
+            grid,
+            grid,
+            pltpu.SemaphoreType.DMA((2, latitudes // tile)),
         ],
-        out_specs=pl.BlockSpec((messages, 1, depth, level_cols), lambda h, t: (0, h, 0, 0)),
-        scratch_shapes=[
-            pltpu.VMEM((plan.widths[0], columns), BF),
-            pltpu.VMEM((ceil_to(latitudes + depth, 8) + 8, columns), F32),
-        ],
-        compiler_params=pltpu.CompilerParams(vmem_limit_bytes=40 * 1024 * 1024),
+        compiler_params=pltpu.CompilerParams(vmem_limit_bytes=limit),
         cost_estimate=pl.CostEstimate(
             flops=2 * latitudes * sum(plan.widths) * columns,
             bytes_accessed=2 * latitudes * sum(plan.widths) + 4 * messages * depth * level_cols,
@@ -369,20 +385,27 @@
     group, block = plan.group, plan.block
     me = lax.axis_index("wave") * lev_count + lax.axis_index("lev")
     is_high = (me >= group).astype(jnp.int32)
-    rank = me - group * is_high
-    mine = jnp.where(is_high == 1, group - 1 - rank, rank)
     lowest = pair_order[0]
     halves = [list(range(group)), list(range(group, 2 * group))]
 
     def exchange(rows):
         return lax.all_to_all(rows, axes, split_axis=0, concat_axis=0, tiled=True, axis_index_groups=halves)
 
-    pairs = [[d, 2 * group - 1 - d] for d in range(group)]
-    both = lax.all_gather(covariance.astype(BF), axes, axis_index_groups=pairs)
+    plane = group // 2
+    whole = range(2 * group)
+    far = [(d, (3 - d // plane) * plane + d % plane) for d in whole]
+    near = [(d, d // plane * plane + plane - 1 - d % plane) for d in whole]
+    own = covariance.astype(BF)
+    own, control = lax.optimization_barrier((own, control))
+    far_block = lax.ppermute(own, axes, far)
+    near_block = lax.ppermute(own, axes, near)
+
+    def fold_block(rank):
+        rank = jnp.where(is_high == 1, group - 1 - rank, rank)
+        return rank // plane * plane + plane - 1 - rank % plane
 
     def slots_of(message, fold, folded, used):
-        message = jnp.where(is_high == 1, group - 1 - message, message)
-        degree = message * block + fold
+        degree = fold_block(message) * block + fold
         upper = jnp.where(folded, degree - lowest, degrees - 1 - degree - lowest)
         upper = jnp.where(used & (upper >= 0), upper, -1)
         lower = jnp.where(used & folded & (degree <= lowest), degrees - degree, -1)
@@ -394,12 +417,12 @@
 
     tables = make_tables(plan, legendre[0], slots_of(*plan.transform_rows()))
 
-    info = (mine * block)[None]
+    info = jnp.stack([is_high, fold_block(me - group * is_high) * block])
     received, tables = lax.optimization_barrier((received, tables))
-    filtered = exchange(filter_rows(plan, info, received, both))
+    filtered = exchange(filter_rows(plan, info, received, near_block, far_block))
 
     extra_block = lowest // block
-    extra_message = jnp.where(is_high == 1, group - 1 - extra_block, extra_block)
+    extra_message = fold_block(extra_block)
     extra_row = plan.extra_row(extra_message, lowest - extra_block * block)
     where = jnp.stack([extra_message, extra_row])
     starts = jnp.cumsum(band_rows) - band_rows

time: 284 us -> 259 us (0.912)
  between operations: 14.3 us -> 0.93 us
  waiting for transfers between devices: 40.9 us -> 30.2 us
  local copies, waits for them, and re-layouts: 14.8 us -> 10.7 us
    all_gather x1 -> x0, waiting for transfers between devices: 14 us -> none  [per_device(): both = lax.all_gather(covariance.astype(BF), axes, axis_index_groups=pairs)]
    ppermute x0 -> x2, starting transfers between devices: none -> 6.67 us  [the longest x1 5.07 us: per_device(): far_block = lax.ppermute(own, axes, far)]
    all_to_all x2, starting transfers between devices: 21 us -> 15.6 us  [exchange(): lax.all_to_all(rows, axes, split_axis=0, concat_axis=0, tiled=True, axis_...]
    unnamed x31 -> x27, local copies, waits for them, and re-layouts: 14.6 us -> 10.4 us
    all_to_all x2, waiting for transfers between devices: 26.9 us -> 30.2 us  [exchange(): lax.all_to_all(rows, axes, split_axis=0, concat_axis=0, tiled=True, axis_...]
  transfers between devices with their start and end apart: 3 -> 4, of which waited for: 3 -> 2; matrix products, arithmetic and copies ran while one was open for 0% -> 0% of each run, Pallas kernels for 8% -> 9%
where the time goes in v6:
time: 259 us
  blocking collectives  149 us (58%)
  Pallas kernels  42.1 us (16%)
  waiting for transfers between devices  30.2 us (12%)
  starting transfers between devices  22.3 us (9%)
  local copies, waits for them, and re-layouts  10.7 us (4%)
  other arithmetic  3.52 us (1%)
    all_to_all x1, blocking collectives, per_device(): lax.all_to_all(outgoing, axes, split_axis=0, concat_axis=0, tiled=True)  149 us
    all_to_all x2, waiting for transfers between devices, exchange(): lax.all_to_all(rows, axes, split_axis=0, concat_axis=0, tiled=True, axis_...  30.2 us
    pallas_call x1, Pallas kernels, make_tables(): pl.pallas_call(functools.partial(table_kernel, plan), grid=(latitudes //...  19.7 us
    all_to_all x2, starting transfers between devices, exchange(): lax.all_to_all(rows, axes, split_axis=0, concat_axis=0, tiled=True, axis_...  15.6 us
    pallas_call x1, Pallas kernels, to_bands(): pl.pallas_call(functools.partial(grid_kernel, plan, levels, latitudes, de...  13.4 us
    unnamed x27, local copies, waits for them, and re-layouts  10.4 us
  transfers between devices with their start and end apart: 4, of which 2 were waited for; matrix products, arithmetic and copies ran while one was open for 0% of the time, Pallas kernels for 9%

profile of v6, /device:TPU:0, one launch (start us, length us, event | category | flops | bytes accessed | tf_op | source)
XLA Modules:
  0.0 259.1 jit_solution(12276884846695033213)
XLA Ops:
  0.0 3.1 %convert_element_type.7 = bf16[40,128,128]{2,1,0:T(8,128)(2,1)} convert(f32[40,128,128]{2,1,0:T(8,128)} %param.18) | non-fusion elementwise | flops 655360 | bytes 3932160 | tf_op jit(solution)/shard_map/convert_element_type | solution.py:398
  3.1 5.1 %collective-permute-start.1 = (bf16[40,128,128]{2,1,0:T(8,128)(2,1)}, bf16[40,128,128]{2,1,0:T(8,128)(2,1)S(1)}, u32[]{:S(2)}, u32[]{:S(2)}) collective-permute-start(bf16[40,128,128]{2,1,0:T(8,128)(2,1)} %convert_element_type.7), channel_id=1, source_target_pairs={{0,24},{1,25},{2,26},{3,27},{4,28},{5,29},{6,30},{7,31},{8,16},{9,... | collective-permute-start | bytes 3932168 | tf_op jit(solution)/shard_map/ppermute | solution.py:400
  8.2 1.6 collective-permute-start
  10.5 0.2 broadcast_in_dim.17.slot_ref
  10.8 4.0 %pack_rows.1 = bf16[16,336,128]{2,1,0:T(8,128)(2,1)} custom-call(s32[1]{0:T(128)} %copy.20.info_ref, s32[1280,1]{1,0:T(8,128)S(1)} %broadcast_in_dim.17.slot_ref, bf16[1281,512]{1,0:T(8,128)(2,1)S(1)} %bitcast.18), custom_call_target="tpu_custom_call" | custom-call | flops 1 | bytes 1 | tf_op jit(solution)/shard_map/pack_rows/pallas_call | solution.py:119
  14.8 3.8 %all-to-all-start = ((bf16[16,336,128]{2,1,0:T(8,128)(2,1)}), bf16[16,336,128]{2,1,0:T(8,128)(2,1)S(1)}, u32[]{:S(2)}, u32[]{:S(2)}) async-start(bf16[16,336,128]{2,1,0:T(8,128)(2,1)} %pack_rows.1), calls=%async_computation | async-start | bytes 2752512 | tf_op jit(solution)/shard_map/all_to_all | solution.py:392
  18.8 0.0 copy-start.1
  18.8 2.9 %copy-done.1 = bf16[1,1281,2560]{2,1,0:T(8,128)(2,1)S(1)} copy-done((bf16[1,1281,2560]{2,1,0:T(8,128)(2,1)S(1)}, bf16[1,1281,2560]{2,1,0:T(8,128)(2,1)}, u32[]{:S(2)}) %copy-start.1) | copy-done | bytes 6558744
  21.6 19.7 %make_tables.1 = (bf16[2560,1280]{1,0:T(8,128)(2,1)S(1)}, bf16[2560,768]{1,0:T(8,128)(2,1)S(1)}) custom-call(s32[1,1280]{1,0:T(1,128)S(1)} %broadcast_in_dim.15.upper_ref, s32[1,768]{1,0:T(1,128)S(1)} %broadcast_in_dim.16.lower_ref, bf16[1281,2560]{1,0:T(8,128)(2,1)S(1)} %bitcast.19), custom_call_target="tpu_custom_call" | custom-call | flops 134322585600 | bytes 6558720 | tf_op jit(solution)/shard_map/make_tables/pallas_call | solution.py:161
  41.4 0.0 copy-start.3
  41.4 2.8 %copy-done.3 = bf16[2560,1280]{1,0:T(8,128)(2,1)} copy-done((bf16[2560,1280]{1,0:T(8,128)(2,1)}, bf16[2560,1280]{1,0:T(8,128)(2,1)S(1)}, u32[]{:S(2)}) %copy-start.3) | copy-done | bytes 6553624
  44.1 2.0 copy-done.4
  46.1 0.1 pad_add_fusion.1.info_ref
  46.2 10.4 %all-to-all-done.rows_ref = bf16[16,336,128]{2,1,0:T(8,128)(2,1)S(1)} async-done(((bf16[16,336,128]{2,1,0:T(8,128)(2,1)}), bf16[16,336,128]{2,1,0:T(8,128)(2,1)S(1)}, u32[]{:S(2)}, u32[]{:S(2)}) %all-to-all-start) | async-done | bytes 1376288 | tf_op jit(solution)/shard_map/all_to_all | solution.py:392
  56.6 0.0 collective-permute-done.1.far_ref
  56.6 0.0 collective-permute-done.near_ref
  56.6 4.9 %filter_rows.1 = bf16[16,336,128]{2,1,0:T(8,128)(2,1)} custom-call(s32[2]{0:T(128)S(1)} %pad_add_fusion.1.info_ref, bf16[16,336,128]{2,1,0:T(8,128)(2,1)S(1)} %all-to-all-done.rows_ref, bf16[40,128,128]{2,1,0:T(8,128)(2,1)} %collective-permute-done.near_ref, bf16[40,128,128]{2,1,0:T(8,128)(2,1)S(1)} %collective-permute-done.1.far_ref), custom_call_target="tpu_custom_call" | custom-call | flops 1342177280 | bytes 5373952 | tf_op jit(solution)/shard_map/filter_rows/pallas_call | solution.py:249
  61.5 11.8 %all-to-all-start.1 = ((bf16[16,336,128]{2,1,0:T(8,128)(2,1)}), bf16[16,336,128]{2,1,0:T(8,128)(2,1)S(1)}, u32[]{:S(2)}, u32[]{:S(2)}) async-start(bf16[16,336,128]{2,1,0:T(8,128)(2,1)} %filter_rows.1), calls=%async_computation.1 | async-start | bytes 2752512 | tf_op jit(solution)/shard_map/all_to_all | solution.py:392
  73.4 0.2 reduce-window.9
  73.6 0.1 pad_add_fusion.info_ref
  73.7 19.8 %all-to-all-done.1.part_ref = bf16[16,336,128]{2,1,0:T(8,128)(2,1)S(1)} async-done(((bf16[16,336,128]{2,1,0:T(8,128)(2,1)}), bf16[16,336,128]{2,1,0:T(8,128)(2,1)S(1)}, u32[]{:S(2)}, u32[]{:S(2)}) %all-to-all-start.1) | async-done | bytes 1376288 | tf_op jit(solution)/shard_map/all_to_all | solution.py:392
  93.5 13.4 %grid_bands.1 = bf16[32,2,400,128]{3,2,1,0:T(8,128)(2,1)} custom-call(s32[2]{0:T(128)S(1)} %pad_add_fusion.info_ref, s32[8]{0:T(128)S(1)} %bitcast_subtract_fusion.starts_ref, s32[8]{0:T(128)S(1)} %copy-done.2, bf16[16,336,128]{2,1,0:T(8,128)(2,1)S(1)} %all-to-all-done.1.part_ref, bf16[2560,1280]{1,0:T(8,128)(2,1)} %copy-done.3, bf16[2560,768]{1,0:T(8,128)(2,1)} %copy-done.4), custom_call_target="tpu_custom_call" | custom-call | flops 5368709120 | bytes 17039360 | tf_op jit(solution)/shard_map/grid_bands/pallas_call | solution.py:352
  106.9 149.4 %all_to_all.15 = bf16[64,400,128]{2,1,0:T(8,128)(2,1)S(1)} all-to-all(bf16[64,400,128]{2,1,0:T(8,128)(2,1)} %bitcast.21), channel_id=1, replica_groups=mesh['wave'=8,'lev'=4] {'wave','lev'}, dimensions={0} | all-to-all | bytes 13107200 | tf_op jit(solution)/shard_map/all_to_all | solution.py:431
  256.3 2.8 %copy.21 = bf16[64,400,128]{2,1,0:T(8,128)(2,1)} copy(bf16[64,400,128]{2,1,0:T(8,128)(2,1)S(1)} %all_to_all.15) | data formatting | bytes 13107200
  (27 shorter events, 0.1 us)
Async XLA Ops:
  0.0 10.5 %copy-start.8 = (s32[1280]{0:T(1024)S(1)}, s32[1280]{0:T(1024)}, u32[]{:S(2)}) copy-start(s32[1280]{0:T(1024)} %constant.136.clone) | copy-start | bytes 15364
  0.0 10.5 %copy-start.9 = (s32[1280]{0:T(1024)S(1)}, s32[1280]{0:T(1024)}, u32[]{:S(2)}) copy-start(s32[1280]{0:T(1024)} %constant.135.clone) | copy-start | bytes 15364
  0.0 10.5 %copy-start.10 = (s32[1280]{0:T(1024)S(1)}, s32[1280]{0:T(1024)}, u32[]{:S(2)}) copy-start(s32[1280]{0:T(1024)} %constant.134.clone) | copy-start | bytes 15364
  0.0 10.5 %copy-start.12 = (pred[1280]{0:T(1024)(128)(4,1)S(1)}, pred[1280]{0:T(1024)(128)(4,1)}, u32[]{:S(2)}) copy-start(pred[1280]{0:T(1024)(128)(4,1)} %constant.137.clone) | copy-start | bytes 3844
  0.0 10.8 %copy-start = (bf16[1,1281,512]{2,1,0:T(8,128)(2,1)S(1)}, bf16[1,1281,512]{2,1,0:T(8,128)(2,1)}, u32[]{:S(2)}) copy-start(bf16[1,1281,512]{2,1,0:T(8,128)(2,1)} %param.17) | copy-start | bytes 3935236
  3.1 53.5 %collective-permute-start.1 = (bf16[40,128,128]{2,1,0:T(8,128)(2,1)}, bf16[40,128,128]{2,1,0:T(8,128)(2,1)S(1)}, u32[]{:S(2)}, u32[]{:S(2)}) collective-permute-start(bf16[40,128,128]{2,1,0:T(8,128)(2,1)} %convert_element_type.7), channel_id=1, source_target_pairs={{0,24},{1,25},{2,26},{3,27},{4,28},{5,29},{6,30},{7,31},{8,16},{9,... | collective-permute-start | bytes 3932168 | tf_op jit(solution)/shard_map/ppermute | solution.py:400
  8.2 48.4 %collective-permute-start = (bf16[40,128,128]{2,1,0:T(8,128)(2,1)}, bf16[40,128,128]{2,1,0:T(8,128)(2,1)}, u32[]{:S(2)}, u32[]{:S(2)}) collective-permute-start(bf16[40,128,128]{2,1,0:T(8,128)(2,1)} %convert_element_type.7), channel_id=1, source_target_pairs={{0,7},{1,6},{2,5},{3,4},{4,3},{5,2},{6,1},{7,0},{8,15},{9,14},{10,... | collective-permute-start | bytes 3932168 | tf_op jit(solution)/shard_map/ppermute | solution.py:401
  14.8 3.9 %copy-start.5 = (s32[1280]{0:T(1024)S(1)}, s32[1280]{0:T(1024)}, u32[]{:S(2)}) copy-start(s32[1280]{0:T(1024)} %constant.141.clone) | copy-start | bytes 15364
  14.8 3.9 %copy-start.6 = (s32[1280]{0:T(1024)S(1)}, s32[1280]{0:T(1024)}, u32[]{:S(2)}) copy-start(s32[1280]{0:T(1024)} %constant.140.clone) | copy-start | bytes 15364
  14.8 3.9 %copy-start.7 = (s32[1280]{0:T(1024)S(1)}, s32[1280]{0:T(1024)}, u32[]{:S(2)}) copy-start(s32[1280]{0:T(1024)} %constant.139.clone) | copy-start | bytes 15364
  14.8 3.9 %copy-start.11 = (pred[1280]{0:T(1024)(128)(4,1)S(1)}, pred[1280]{0:T(1024)(128)(4,1)}, u32[]{:S(2)}) copy-start(pred[1280]{0:T(1024)(128)(4,1)} %constant.142.clone) | copy-start | bytes 3844
  14.8 41.8 %all-to-all-start = ((bf16[16,336,128]{2,1,0:T(8,128)(2,1)}), bf16[16,336,128]{2,1,0:T(8,128)(2,1)S(1)}, u32[]{:S(2)}, u32[]{:S(2)}) async-start(bf16[16,336,128]{2,1,0:T(8,128)(2,1)} %pack_rows.1), calls=%async_computation | async-start | bytes 2752512 | tf_op jit(solution)/shard_map/all_to_all | solution.py:392
  18.8 2.9 %copy-start.1 = (bf16[1,1281,2560]{2,1,0:T(8,128)(2,1)S(1)}, bf16[1,1281,2560]{2,1,0:T(8,128)(2,1)}, u32[]{:S(2)}) copy-start(bf16[1,1281,2560]{2,1,0:T(8,128)(2,1)} %param.19) | copy-start | bytes 19676164
  41.4 2.8 %copy-start.3 = (bf16[2560,1280]{1,0:T(8,128)(2,1)}, bf16[2560,1280]{1,0:T(8,128)(2,1)S(1)}, u32[]{:S(2)}) copy-start(bf16[2560,1280]{1,0:T(8,128)(2,1)S(1)} %get-tuple-element.17.refs_0_) | copy-start | bytes 19660804
  44.1 2.0 copy-start.4
  61.5 11.8 %copy-start.2 = (s32[8]{0:T(128)S(1)}, s32[8]{0:T(128)}, u32[]{:S(2)}) copy-start(s32[8]{0:T(128)} %bands_ref.1) | copy-start | bytes 100
  61.5 31.9 %all-to-all-start.1 = ((bf16[16,336,128]{2,1,0:T(8,128)(2,1)}), bf16[16,336,128]{2,1,0:T(8,128)(2,1)S(1)}, u32[]{:S(2)}, u32[]{:S(2)}) async-start(bf16[16,336,128]{2,1,0:T(8,128)(2,1)} %filter_rows.1), calls=%async_computation.1 | async-start | bytes 2752512 | tf_op jit(solution)/shard_map/all_to_all | solution.py:392

commit v7 on v6

--- a/solution.py
+++ b/solution.py
@@ -180,17 +180,28 @@
     return jnp.where((i // SUB == j % SUB) & (i % SUB == j // SUB), 1.0, 0.0).astype(BF)
 
 
-def filter_kernel(plan, levels, info_ref, rows_ref, near_ref, far_ref, out_ref, x_ref, y_ref):
+def filter_kernel(plan, levels, info_ref, rows_ref, *refs):
+    pieces = len(refs) // 2 - 3
+    blocks, out_ref = refs[:pieces], refs[pieces]
+    held_blocks, (x_ref, y_ref, z_ref, in_sems, out_sems) = refs[pieces + 1:2 * pieces + 1], refs[2 * pieces + 1:]
+    each = blocks[0].shape[0]
     is_high = info_ref[0] == 1
     first_fold = info_ref[1].astype(F32)
     swap = swap_matrix()
+    arrivals = [pltpu.make_async_copy(blocks[at], held_blocks[at], in_sems.at[at]) for at in range(pieces)]
+    for arrival in arrivals:
+        arrival.start()
+    near_refs, far_refs = held_blocks[:pieces // 2], held_blocks[pieces // 2:]
+
+    def matrix(refs, fold):
+        return refs[fold // each][fold % each]
 
     def low_matrix(fold):
-        return jnp.where(is_high, far_ref[fold], near_ref[fold])
+        return jnp.where(is_high, matrix(far_refs, fold), matrix(near_refs, fold))
 
     def high_matrix(fold):
         at = plan.block - 1 - fold
-        return jnp.where(is_high, near_ref[at], far_ref[at])
+        return jnp.where(is_high, matrix(near_refs, at), matrix(far_refs, at))
 
     def times(rows, matrix):
         return lax.dot_general(rows, matrix, (((1,), (1,)), ((), ())), preferred_element_type=F32)
@@ -198,24 +209,44 @@
     def turn(rows):
         return jnp.dot(swap, rows, preferred_element_type=F32)
 
-    for g in range(plan.group // SUB):
+    groups = plan.group // SUB
+    held = plan.rows * SUB
+    for g in range(groups):
         sources = slice(g * SUB, (g + 1) * SUB)
         for r in range(0, plan.rows, SUB):
             parts = []
             for c in range(4):
                 start = c * plan.rows + r
                 parts.append(rows_ref[sources, start:start + SUB, :].reshape(SUB * SUB, levels))
-            x_ref[r * SUB:(r + SUB) * SUB, :] = turn(jnp.concatenate(parts, axis=1)).astype(BF)
+            x_ref[g * held + r * SUB:g * held + (r + SUB) * SUB, :] = turn(jnp.concatenate(parts, axis=1)).astype(BF)
+
+    for arrival in arrivals:
+        arrival.wait()
+
+    departures = []
+
+    def send(rows):
+        at = len(departures)
+        departures.append(pltpu.make_async_copy(z_ref.at[:, rows, :], out_ref.at[:, rows, :], out_sems.at[at]))
+        departures[at].start()
+
+    tails = []
+    for g in range(groups):
+        sources = slice(g * SUB, (g + 1) * SUB)
         tail = turn(rows_ref[sources, 4 * plan.rows:4 * plan.rows + SUB, :].reshape(SUB * SUB, levels))
-        extra = tail[:4 * SUB].astype(BF)
         low = tail[4 * SUB:5 * SUB] * DIGIT + tail[5 * SUB:6 * SUB]
-        low = jnp.concatenate([low] * 4, axis=0)
-        kept = jnp.zeros((4 * SUB, levels), F32)
-        for row0, fold0, count in plan.chunks:
+        tails.append([tail[:4 * SUB].astype(BF), jnp.concatenate([low] * 4, axis=0), jnp.zeros((4 * SUB, levels), F32)])
+
+    for row0, fold0, count in plan.chunks:
+        height = ceil_to(2 * count, SUB)
+        for g in range(groups):
+            sources = slice(g * SUB, (g + 1) * SUB)
+            extra, low, kept = tails[g]
             for i in range(count):
                 def stack(row):
+                    at = g * held + row * SUB
                     return jnp.concatenate(
-                        [x_ref[row * SUB:(row + 1) * SUB, c * levels:(c + 1) * levels] for c in range(4)], axis=0
+                        [x_ref[at:at + SUB, c * levels:(c + 1) * levels] for c in range(4)], axis=0
                     )
 
                 folded, high = stack(row0 + i), stack(row0 + count + i)
@@ -228,45 +259,62 @@
                     value = value.astype(BF)
                     for c in range(4):
                         y_ref[row * SUB:(row + 1) * SUB, c * levels:(c + 1) * levels] = value[c * SUB:(c + 1) * SUB]
-            unused = ceil_to(2 * count, SUB) - 2 * count
-            if unused:
-                start = (row0 + 2 * count) * SUB
-                y_ref[start:start + unused * SUB, :] = jnp.zeros((unused * SUB, 4 * levels), BF)
-        for r in range(0, plan.rows, SUB):
-            back = turn(y_ref[r * SUB:(r + SUB) * SUB, :]).astype(BF)
-            for c in range(4):
-                start = c * plan.rows + r
-                out_ref[sources, start:start + SUB, :] = back[:, c * levels:(c + 1) * levels].reshape(
-                    SUB, SUB, levels
+            tails[g][2] = kept
+            if height > 2 * count:
+                y_ref[(row0 + 2 * count) * SUB:(row0 + height) * SUB, :] = jnp.zeros(
+                    ((height - 2 * count) * SUB, 4 * levels), BF
                 )
-        filled = jnp.concatenate([kept, jnp.zeros((12 * SUB, levels), F32)], axis=0).astype(BF)
-        out_ref[sources, 4 * plan.rows:4 * plan.rows + SUB, :] = turn(filled).astype(BF).reshape(SUB, SUB, levels)
-
-
-def filter_rows(plan, info, received, near_block, far_block):
+            for r in range(row0, row0 + height, SUB):
+                back = turn(y_ref[r * SUB:(r + SUB) * SUB, :]).astype(BF)
+                for c in range(4):
+                    start = c * plan.rows + r
+                    z_ref[sources, start:start + SUB, :] = back[:, c * levels:(c + 1) * levels].reshape(
+                        SUB, SUB, levels
+                    )
+        for c in range(4):
+            send(pl.ds(c * plan.rows + row0, height))
+    for g in range(groups):
+        sources = slice(g * SUB, (g + 1) * SUB)
+        filled = jnp.concatenate([tails[g][2], jnp.zeros((12 * SUB, levels), F32)], axis=0).astype(BF)
+        z_ref[sources, 4 * plan.rows:4 * plan.rows + SUB, :] = turn(filled).astype(BF).reshape(SUB, SUB, levels)
+    send(pl.ds(4 * plan.rows, SUB))
+    for departure in departures:
+        departure.wait()
+
+
+def filter_rows(plan, info, received, near_blocks, far_blocks):
     levels = received.shape[2]
-    vmem = pl.BlockSpec(memory_space=pltpu.VMEM)
+    blocks = [*near_blocks, *far_blocks]
+    smem, vmem = pl.BlockSpec(memory_space=pltpu.SMEM), pl.BlockSpec(memory_space=pltpu.VMEM)
+    anywhere = pl.BlockSpec(memory_space=pl.ANY)
     return pl.pallas_call(
         functools.partial(filter_kernel, plan, levels),
         out_shape=jax.ShapeDtypeStruct(received.shape, BF),
-        in_specs=[pl.BlockSpec(memory_space=pltpu.SMEM), vmem, vmem, vmem],
-        out_specs=vmem,
-        scratch_shapes=[
+        in_specs=[smem, vmem] + [anywhere] * len(blocks),
+        out_specs=anywhere,
+        scratch_shapes=[pltpu.VMEM(part.shape, BF) for part in blocks]
+        + [
+            pltpu.VMEM((plan.group * plan.rows, 4 * levels), BF),
             pltpu.VMEM((plan.rows * SUB, 4 * levels), BF),
-            pltpu.VMEM((plan.rows * SUB, 4 * levels), BF),
+            pltpu.VMEM(received.shape, BF),
+            pltpu.SemaphoreType.DMA((len(blocks),)),
+            pltpu.SemaphoreType.DMA((4 * len(plan.chunks) + 1,)),
         ],
-        compiler_params=pltpu.CompilerParams(vmem_limit_bytes=12 * 1024 * 1024),
+        compiler_params=pltpu.CompilerParams(vmem_limit_bytes=20 * 1024 * 1024),
         cost_estimate=pl.CostEstimate(
             flops=2 * plan.group * 16 * plan.block * levels * levels * 4,
             bytes_accessed=2 * 2 * received.size + 4 * plan.block * levels * levels,
             transcendentals=0,
         ),
         name="filter_rows",
-    )(info, received, near_block, far_block)
+    )(info, received, *blocks)
 
 
 def grid_kernel(plan, levels, latitudes, depth, level_cols, tile, info_ref, starts_ref, bands_ref, part_ref, *refs):
-    tables, out_ref, held_tables, (upper_ref, lower_ref, *grids, sems) = refs[:2], refs[2], refs[3:5], refs[5:]
+    tables, out_ref, held_tables = refs[:2], refs[2], refs[3:5]
+    upper_ref, lower_ref, *grids, cut_ref, sems, out_sems = refs[5:]
+    waves = bands_ref.shape[0]
+    groups = 4 * levels // level_cols
     tiles = [slice(at, at + tile) for at in range(0, latitudes, tile)]
 
     def copy(half, at):
@@ -298,44 +346,52 @@
         held = upper_ref[place, cols].astype(F32)
         lower_ref[place, cols] = jnp.where(here, extra[c:c + 1, :].astype(F32), held).astype(BF)
 
-    def transform(half):
-        for at, rows in enumerate(tiles):
-            copy(half, at).wait()
-            grids[half][rows, :] = jnp.dot(
-                held_tables[half][rows, :], (upper_ref, lower_ref)[half][...], preferred_element_type=F32
-            )
-
-    def cut(half):
-        grid_ref = grids[half]
-        waves = bands_ref.shape[0]
-        groups = 4 * levels // level_cols
+    def transform(half, at):
+        copy(half, at).wait()
+        rows = tiles[at]
+        grids[half][rows, :] = jnp.dot(
+            held_tables[half][rows, :], (upper_ref, lower_ref)[half][...], preferred_element_type=F32
+        )
+
+    def departure(half, w):
+        messages = pl.ds(w * groups, groups)
+        return pltpu.make_async_copy(cut_ref.at[messages, half], out_ref.at[messages, half], out_sems.at[half, w])
+
+    def cut(half, w):
         place = lax.broadcasted_iota(jnp.int32, (8, 4 * levels), 0)
+        start = starts_ref[w]
+        base = start // 8 * 8
+        offset = start - base
+
+        def slab(at):
+            held = grids[half][pl.ds(pl.multiple_of(base + at, 8), 8), :]
+            return pltpu.roll(held, (8 - offset) % 8, axis=0)
+
+        after = slab(0)
+        done = []
+        for r in range(0, depth, 8):
+            now, after = after, slab(r + 8)
+            got = jnp.where(place < 8 - offset, now, after)
+            done.append(jnp.where(place < bands_ref[w] - r, got, 0.0))
+            if len(done) == 2 or r + 8 == depth:
+                rows = jnp.concatenate(done, axis=0).astype(BF)
+                first = r + 8 - rows.shape[0]
+                for g in range(groups):
+                    cut_ref[w * groups + g, half, first:r + 8, :] = rows[:, g * level_cols:(g + 1) * level_cols]
+                done = []
+        departure(half, w).start()
+
+    for at in range(len(tiles)):
+        transform(0, at)
+    for at in range(len(tiles)):
+        transform(1, at)
+        for w in range(at * waves // len(tiles), (at + 1) * waves // len(tiles)):
+            cut(0, w)
+    for w in range(waves):
+        cut(1, w)
+    for half in range(2):
         for w in range(waves):
-            start = starts_ref[w]
-            base = start // 8 * 8
-            offset = start - base
-
-            def slab(at):
-                held = grid_ref[pl.ds(pl.multiple_of(base + at, 8), 8), :]
-                return pltpu.roll(held, (8 - offset) % 8, axis=0)
-
-            after = slab(0)
-            done = []
-            for r in range(0, depth, 8):
-                now, after = after, slab(r + 8)
-                got = jnp.where(place < 8 - offset, now, after)
-                done.append(jnp.where(place < bands_ref[w] - r, got, 0.0))
-                if len(done) == 2 or r + 8 == depth:
-                    rows = jnp.concatenate(done, axis=0).astype(BF)
-                    first = r + 8 - rows.shape[0]
-                    for g in range(groups):
-                        out_ref[w * groups + g, half, first:r + 8, :] = rows[:, g * level_cols:(g + 1) * level_cols]
-                    done = []
-
-    transform(0)
-    cut(0)
-    transform(1)
-    cut(1)
+            departure(half, w).wait()
 
 
 def to_bands(plan, info, starts, bands, part, tables, depth, level_cols):
@@ -353,7 +409,7 @@
         functools.partial(grid_kernel, plan, levels, latitudes, depth, level_cols, tile),
         out_shape=jax.ShapeDtypeStruct((messages, 2, depth, level_cols), BF),
         in_specs=[smem, smem, smem, vmem] + [pl.BlockSpec(memory_space=pl.ANY)] * 2,
-        out_specs=vmem,
+        out_specs=pl.BlockSpec(memory_space=pl.ANY),
         scratch_shapes=[
             pltpu.VMEM(tables[0].shape, BF),
             pltpu.VMEM(tables[1].shape, BF),
@@ -361,7 +417,9 @@
             pltpu.VMEM((plan.widths[1], columns), BF),
             grid,
             grid,
+            pltpu.VMEM((messages, 2, depth, level_cols), BF),
             pltpu.SemaphoreType.DMA((2, latitudes // tile)),
+            pltpu.SemaphoreType.DMA((2, bands.shape[0])),
         ],
         compiler_params=pltpu.CompilerParams(vmem_limit_bytes=limit),
         cost_estimate=pl.CostEstimate(
@@ -395,10 +453,11 @@
     whole = range(2 * group)
     far = [(d, (3 - d // plane) * plane + d % plane) for d in whole]
     near = [(d, d // plane * plane + plane - 1 - d % plane) for d in whole]
-    own = covariance.astype(BF)
-    own, control = lax.optimization_barrier((own, control))
-    far_block = lax.ppermute(own, axes, far)
-    near_block = lax.ppermute(own, axes, near)
+    pieces = 2 if block % 2 == 0 else 1
+    own = [part.astype(BF) for part in jnp.split(covariance, pieces)]
+    *own, control = lax.optimization_barrier((*own, control))
+    far_blocks = [lax.ppermute(part, axes, far) for part in own]
+    near_blocks = [lax.ppermute(part, axes, near) for part in own]
 
     def fold_block(rank):
         rank = jnp.where(is_high == 1, group - 1 - rank, rank)
@@ -419,7 +478,7 @@
 
     info = jnp.stack([is_high, fold_block(me - group * is_high) * block])
     received, tables = lax.optimization_barrier((received, tables))
-    filtered = exchange(filter_rows(plan, info, received, near_block, far_block))
+    filtered = exchange(filter_rows(plan, info, received, near_blocks, far_blocks))
 
     extra_block = lowest // block
     extra_message = fold_block(extra_block)

time: 259 us -> 258 us (level)
    convert_element_type x1 -> x0, other arithmetic: 3.12 us -> none  [per_device(): own = covariance.astype(BF)]
    ppermute x2 -> x4, starting transfers between devices: 6.67 us -> 7.7 us  [the longest x2 5.33 us: per_device(): far_blocks = [lax.ppermute(part, axes, far) for part in own]]
  transfers between devices with their start and end apart: 4 -> 6, of which waited for: 2 -> 2; matrix products, arithmetic and copies ran while one was open for 0% -> 0% of each run, Pallas kernels for 9% -> 9%
where the time goes in v7:
time: 258 us; the launch traced here: 257 us
  blocking collectives  149 us (58%)
  Pallas kernels  40.4 us (16%)
  waiting for transfers between devices  29.2 us (11%)
  starting transfers between devices  23.1 us (9%)
  local copies, waits for them, and re-layouts  11.9 us (5%)
    all_to_all x1, blocking collectives, per_device(): lax.all_to_all(outgoing, axes, split_axis=0, concat_axis=0, tiled=True)  149 us
    all_to_all x2, waiting for transfers between devices, exchange(): lax.all_to_all(rows, axes, split_axis=0, concat_axis=0, tiled=True, axis_...  29.2 us
    pallas_call x1, Pallas kernels, make_tables(): pl.pallas_call(functools.partial(table_kernel, plan), grid=(latitudes //...  19.7 us
    all_to_all x2, starting transfers between devices, exchange(): lax.all_to_all(rows, axes, split_axis=0, concat_axis=0, tiled=True, axis_...  15.4 us
    pallas_call x1, Pallas kernels, to_bands(): pl.pallas_call(functools.partial(grid_kernel, plan, levels, latitudes, de...  11.7 us
    unnamed x27, local copies, waits for them, and re-layouts  10.5 us
    ppermute x2, starting transfers between devices, per_device(): far_blocks = [lax.ppermute(part, axes, far) for part in own]  5.33 us
  transfers between devices with their start and end apart: 6, of which 2 were waited for; matrix products, arithmetic and copies ran while one was open for 0% of the time, Pallas kernels for 9%

profile of v7, /device:TPU:0, one launch (start us, length us, event | category | flops | bytes accessed | tf_op | source)
XLA Modules:
  0.0 257.3 jit_solution(16411070605210156017)
XLA Ops:
  0.0 2.0 convert.4
  2.0 1.2 fusion.19
  3.2 5.0 %collective-permute-start.2 = (bf16[20,128,128]{2,1,0:T(8,128)(2,1)}, bf16[20,128,128]{2,1,0:T(8,128)(2,1)S(1)}, u32[]{:S(2)}, u32[]{:S(2)}) collective-permute-start(bf16[20,128,128]{2,1,0:T(8,128)(2,1)} %get-tuple-element.17), channel_id=1, source_target_pairs={{0,24},{1,25},{2,26},{3,27},{4,28},{5,29},{6,30},{7,31},{8,16},{9,... | collective-permute-start | bytes 1966088 | tf_op jit(solution)/shard_map/ppermute | solution.py:459
  8.2 1.6 collective-permute-start
  9.8 0.3 collective-permute-start.3
  10.1 0.8 collective-permute-start.1
  11.6 0.2 broadcast_in_dim.17.slot_ref
  11.9 0.0 copy-start.6
  11.9 4.0 %pack_rows.1 = bf16[16,336,128]{2,1,0:T(8,128)(2,1)} custom-call(s32[1]{0:T(128)} %copy.20.info_ref, s32[1280,1]{1,0:T(8,128)S(1)} %broadcast_in_dim.17.slot_ref, bf16[1281,512]{1,0:T(8,128)(2,1)S(1)} %bitcast.18), custom_call_target="tpu_custom_call" | custom-call | flops 1 | bytes 1 | tf_op jit(solution)/shard_map/pack_rows/pallas_call | solution.py:119
  15.9 3.8 %all-to-all-start = ((bf16[16,336,128]{2,1,0:T(8,128)(2,1)}), bf16[16,336,128]{2,1,0:T(8,128)(2,1)S(1)}, u32[]{:S(2)}, u32[]{:S(2)}) async-start(bf16[16,336,128]{2,1,0:T(8,128)(2,1)} %pack_rows.1), calls=%async_computation | async-start | bytes 2752512 | tf_op jit(solution)/shard_map/all_to_all | solution.py:450
  19.9 2.9 %copy-done.1 = bf16[1,1281,2560]{2,1,0:T(8,128)(2,1)S(1)} copy-done((bf16[1,1281,2560]{2,1,0:T(8,128)(2,1)S(1)}, bf16[1,1281,2560]{2,1,0:T(8,128)(2,1)}, u32[]{:S(2)}) %copy-start.1) | copy-done | bytes 6558744
  22.7 19.7 %make_tables.1 = (bf16[2560,1280]{1,0:T(8,128)(2,1)S(1)}, bf16[2560,768]{1,0:T(8,128)(2,1)S(1)}) custom-call(s32[1,1280]{1,0:T(1,128)S(1)} %broadcast_in_dim.15.upper_ref, s32[1,768]{1,0:T(1,128)S(1)} %broadcast_in_dim.16.lower_ref, bf16[1281,2560]{1,0:T(8,128)(2,1)S(1)} %bitcast.19), custom_call_target="tpu_custom_call" | custom-call | flops 134322585600 | bytes 6558720 | tf_op jit(solution)/shard_map/make_tables/pallas_call | solution.py:161
  42.5 2.8 %copy-done.3 = bf16[2560,1280]{1,0:T(8,128)(2,1)} copy-done((bf16[2560,1280]{1,0:T(8,128)(2,1)}, bf16[2560,1280]{1,0:T(8,128)(2,1)S(1)}, u32[]{:S(2)}) %copy-start.3) | copy-done | bytes 6553624
  45.2 2.0 copy-done.4
  47.2 0.1 pad_add_fusion.1.info_ref
  47.3 9.4 %all-to-all-done.rows_ref = bf16[16,336,128]{2,1,0:T(8,128)(2,1)S(1)} async-done(((bf16[16,336,128]{2,1,0:T(8,128)(2,1)}), bf16[16,336,128]{2,1,0:T(8,128)(2,1)S(1)}, u32[]{:S(2)}, u32[]{:S(2)}) %all-to-all-start) | async-done | bytes 1376288 | tf_op jit(solution)/shard_map/all_to_all | solution.py:450
  56.7 5.0 %filter_rows.1 = bf16[16,336,128]{2,1,0:T(8,128)(2,1)} custom-call(s32[2]{0:T(128)S(1)} %pad_add_fusion.1.info_ref, bf16[16,336,128]{2,1,0:T(8,128)(2,1)S(1)} %all-to-all-done.rows_ref, bf16[20,128,128]{2,1,0:T(8,128)(2,1)S(1)} %collective-permute-done.refs_0_, bf16[20,128,128]{2,1,0:T(8,128)(2,1)} %collective-permute-done.1.refs_1_, ...), custom_call_target="tpu_custom_call" | custom-call | flops 1342177280 | bytes 5373952 | tf_op jit(solution)/shard_map/filter_rows/pallas_call | solution.py:290
  61.7 11.6 %all-to-all-start.1 = ((bf16[16,336,128]{2,1,0:T(8,128)(2,1)}), bf16[16,336,128]{2,1,0:T(8,128)(2,1)S(1)}, u32[]{:S(2)}, u32[]{:S(2)}) async-start(bf16[16,336,128]{2,1,0:T(8,128)(2,1)} %filter_rows.1), calls=%async_computation.1 | async-start | bytes 2752512 | tf_op jit(solution)/shard_map/all_to_all | solution.py:450
  73.5 0.2 reduce-window.9
  73.6 0.1 pad_add_fusion.info_ref
  73.7 19.8 %all-to-all-done.1.part_ref = bf16[16,336,128]{2,1,0:T(8,128)(2,1)S(1)} async-done(((bf16[16,336,128]{2,1,0:T(8,128)(2,1)}), bf16[16,336,128]{2,1,0:T(8,128)(2,1)S(1)}, u32[]{:S(2)}, u32[]{:S(2)}) %all-to-all-start.1) | async-done | bytes 1376288 | tf_op jit(solution)/shard_map/all_to_all | solution.py:450
  93.5 11.7 %grid_bands.1 = bf16[32,2,400,128]{3,2,1,0:T(8,128)(2,1)} custom-call(s32[2]{0:T(128)S(1)} %pad_add_fusion.info_ref, s32[8]{0:T(128)S(1)} %bitcast_subtract_fusion.starts_ref, s32[8]{0:T(128)S(1)} %copy-done.2, bf16[16,336,128]{2,1,0:T(8,128)(2,1)S(1)} %all-to-all-done.1.part_ref, bf16[2560,1280]{1,0:T(8,128)(2,1)} %copy-done.3, bf16[2560,768]{1,0:T(8,128)(2,1)} %copy-done.4), custom_call_target="tpu_custom_call" | custom-call | flops 5368709120 | bytes 17039360 | tf_op jit(solution)/shard_map/grid_bands/pallas_call | solution.py:408
  105.2 149.4 %all_to_all.15 = bf16[64,400,128]{2,1,0:T(8,128)(2,1)S(1)} all-to-all(bf16[64,400,128]{2,1,0:T(8,128)(2,1)} %bitcast.21), channel_id=1, replica_groups=mesh['wave'=8,'lev'=4] {'wave','lev'}, dimensions={0} | all-to-all | bytes 13107200 | tf_op jit(solution)/shard_map/all_to_all | solution.py:490
  254.5 2.8 %copy.21 = bf16[64,400,128]{2,1,0:T(8,128)(2,1)} copy(bf16[64,400,128]{2,1,0:T(8,128)(2,1)S(1)} %all_to_all.15) | data formatting | bytes 13107200
  (32 shorter events, 0.1 us)
Async XLA Ops:
  0.0 11.5 %copy-start.8 = (s32[1280]{0:T(1024)S(1)}, s32[1280]{0:T(1024)}, u32[]{:S(2)}) copy-start(s32[1280]{0:T(1024)} %constant.136.clone) | copy-start | bytes 15364
  0.0 11.5 %copy-start.9 = (s32[1280]{0:T(1024)S(1)}, s32[1280]{0:T(1024)}, u32[]{:S(2)}) copy-start(s32[1280]{0:T(1024)} %constant.135.clone) | copy-start | bytes 15364
  0.0 11.6 %copy-start.10 = (s32[1280]{0:T(1024)S(1)}, s32[1280]{0:T(1024)}, u32[]{:S(2)}) copy-start(s32[1280]{0:T(1024)} %constant.134.clone) | copy-start | bytes 15364
  0.0 11.6 %copy-start.12 = (pred[1280]{0:T(1024)(128)(4,1)S(1)}, pred[1280]{0:T(1024)(128)(4,1)}, u32[]{:S(2)}) copy-start(pred[1280]{0:T(1024)(128)(4,1)} %constant.137.clone) | copy-start | bytes 3844
  2.0 9.8 %copy-start = (bf16[1,1281,512]{2,1,0:T(8,128)(2,1)S(1)}, bf16[1,1281,512]{2,1,0:T(8,128)(2,1)}, u32[]{:S(2)}) copy-start(bf16[1,1281,512]{2,1,0:T(8,128)(2,1)} %param.17) | copy-start | bytes 3935236
  3.2 53.5 %collective-permute-start.2 = (bf16[20,128,128]{2,1,0:T(8,128)(2,1)}, bf16[20,128,128]{2,1,0:T(8,128)(2,1)S(1)}, u32[]{:S(2)}, u32[]{:S(2)}) collective-permute-start(bf16[20,128,128]{2,1,0:T(8,128)(2,1)} %get-tuple-element.17), channel_id=1, source_target_pairs={{0,24},{1,25},{2,26},{3,27},{4,28},{5,29},{6,30},{7,31},{8,16},{9,... | collective-permute-start | bytes 1966088 | tf_op jit(solution)/shard_map/ppermute | solution.py:459
  8.2 48.4 %collective-permute-start = (bf16[20,128,128]{2,1,0:T(8,128)(2,1)}, bf16[20,128,128]{2,1,0:T(8,128)(2,1)S(1)}, u32[]{:S(2)}, u32[]{:S(2)}) collective-permute-start(bf16[20,128,128]{2,1,0:T(8,128)(2,1)} %get-tuple-element.17), channel_id=1, source_target_pairs={{0,7},{1,6},{2,5},{3,4},{4,3},{5,2},{6,1},{7,0},{8,15},{9,14},{10,... | collective-permute-start | bytes 1966088 | tf_op jit(solution)/shard_map/ppermute | solution.py:460
  9.8 46.8 %collective-permute-start.3 = (bf16[20,128,128]{2,1,0:T(8,128)(2,1)}, bf16[20,128,128]{2,1,0:T(8,128)(2,1)S(1)}, u32[]{:S(2)}, u32[]{:S(2)}) collective-permute-start(bf16[20,128,128]{2,1,0:T(8,128)(2,1)} %get-tuple-element.18), channel_id=1, source_target_pairs={{0,24},{1,25},{2,26},{3,27},{4,28},{5,29},{6,30},{7,31},{8,16},{9,... | collective-permute-start | bytes 1966088 | tf_op jit(solution)/shard_map/ppermute | solution.py:459
  10.1 46.6 %collective-permute-start.1 = (bf16[20,128,128]{2,1,0:T(8,128)(2,1)}, bf16[20,128,128]{2,1,0:T(8,128)(2,1)}, u32[]{:S(2)}, u32[]{:S(2)}) collective-permute-start(bf16[20,128,128]{2,1,0:T(8,128)(2,1)} %get-tuple-element.18), channel_id=1, source_target_pairs={{0,7},{1,6},{2,5},{3,4},{4,3},{5,2},{6,1},{7,0},{8,15},{9,14},{10,... | collective-permute-start | bytes 1966088 | tf_op jit(solution)/shard_map/ppermute | solution.py:460
  11.8 7.9 %copy-start.5 = (s32[1280]{0:T(1024)S(1)}, s32[1280]{0:T(1024)}, u32[]{:S(2)}) copy-start(s32[1280]{0:T(1024)} %constant.141.clone) | copy-start | bytes 15364
  11.9 7.9 %copy-start.6 = (s32[1280]{0:T(1024)S(1)}, s32[1280]{0:T(1024)}, u32[]{:S(2)}) copy-start(s32[1280]{0:T(1024)} %constant.140.clone) | copy-start | bytes 15364
  11.9 7.9 %copy-start.7 = (s32[1280]{0:T(1024)S(1)}, s32[1280]{0:T(1024)}, u32[]{:S(2)}) copy-start(s32[1280]{0:T(1024)} %constant.139.clone) | copy-start | bytes 15364
  11.9 7.9 %copy-start.11 = (pred[1280]{0:T(1024)(128)(4,1)S(1)}, pred[1280]{0:T(1024)(128)(4,1)}, u32[]{:S(2)}) copy-start(pred[1280]{0:T(1024)(128)(4,1)} %constant.142.clone) | copy-start | bytes 3844
  15.9 40.8 %all-to-all-start = ((bf16[16,336,128]{2,1,0:T(8,128)(2,1)}), bf16[16,336,128]{2,1,0:T(8,128)(2,1)S(1)}, u32[]{:S(2)}, u32[]{:S(2)}) async-start(bf16[16,336,128]{2,1,0:T(8,128)(2,1)} %pack_rows.1), calls=%async_computation | async-start | bytes 2752512 | tf_op jit(solution)/shard_map/all_to_all | solution.py:450
  19.8 2.9 %copy-start.1 = (bf16[1,1281,2560]{2,1,0:T(8,128)(2,1)S(1)}, bf16[1,1281,2560]{2,1,0:T(8,128)(2,1)}, u32[]{:S(2)}) copy-start(bf16[1,1281,2560]{2,1,0:T(8,128)(2,1)} %param.19) | copy-start | bytes 19676164
  42.4 2.8 %copy-start.3 = (bf16[2560,1280]{1,0:T(8,128)(2,1)}, bf16[2560,1280]{1,0:T(8,128)(2,1)S(1)}, u32[]{:S(2)}) copy-start(bf16[2560,1280]{1,0:T(8,128)(2,1)S(1)} %get-tuple-element.19.refs_0_) | copy-start | bytes 19660804
  45.2 2.0 copy-start.4
  61.7 11.7 %copy-start.2 = (s32[8]{0:T(128)S(1)}, s32[8]{0:T(128)}, u32[]{:S(2)}) copy-start(s32[8]{0:T(128)} %bands_ref.1) | copy-start | bytes 100
  61.7 31.8 %all-to-all-start.1 = ((bf16[16,336,128]{2,1,0:T(8,128)(2,1)}), bf16[16,336,128]{2,1,0:T(8,128)(2,1)S(1)}, u32[]{:S(2)}, u32[]{:S(2)}) async-start(bf16[16,336,128]{2,1,0:T(8,128)(2,1)} %filter_rows.1), calls=%async_computation.1 | async-start | bytes 2752512 | tf_op jit(solution)/shard_map/all_to_all | solution.py:450
